TPU v7x, 32 devices: a whole 2x2x4 slice. The times are simulated.
32 devices in a mesh: dp: 8 (over y, x, core), mp: 4 (over z).
Axes of the slice: x: 2, y: 2, z: 4, core: 2. Of those that a mesh axis runs over, the one named last changes fastest.
Arguments:
- token_ids: int32 [24576], P(('dp', 'mp')), may hold values from 0 to 26
- timesteps: int32 [24], P('dp'), may hold values from 1 to 1000
- importance: float32 [24], P('dp'), may hold values from 0.5 to 2
- cotangent: bfloat16 [24576, 512], P(('dp', 'mp')), may hold values from -6 to 6
- qkv_weight: float32 [2, 512, 3, 512], P(None, 'dp', None, 'mp'), may hold values from -0.25 to 0.25
- out_weight: float32 [2, 512, 512], P(None, 'mp', 'dp'), may hold values from -0.25 to 0.25
- up_weight: float32 [2, 512, 2048], P(None, 'dp', 'mp'), may hold values from -0.25 to 0.25
- down_weight: float32 [2, 2048, 512], P(None, 'mp', 'dp'), may hold values from -0.25 to 0.25
- norm_params: float32 [2, 4, 512], replicated, may hold values from -0.5 to 1.3, as said below
- embed_table: float32 [27, 512], replicated, may hold values from -6 to 6
- qkv_first: float32 [2, 512, 3, 512], P(None, 'dp', None, 'mp'), as said below
- qkv_second: float32 [2, 512, 3, 512], P(None, 'dp', None, 'mp'), as said below
- out_first: float32 [2, 512, 512], P(None, 'mp', 'dp'), as said below
- out_second: float32 [2, 512, 512], P(None, 'mp', 'dp'), as said below
- up_first: float32 [2, 512, 2048], P(None, 'dp', 'mp'), as said below
- up_second: float32 [2, 512, 2048], P(None, 'dp', 'mp'), as said below
- down_first: float32 [2, 2048, 512], P(None, 'mp', 'dp'), as said below
- down_second: float32 [2, 2048, 512], P(None, 'mp', 'dp'), as said below
- norm_first: float32 [2, 4, 512], replicated, as said below
- norm_second: float32 [2, 4, 512], replicated, as said below
- embed_first: float32 [27, 512], replicated, as said below
- embed_second: float32 [27, 512], replicated, as said below
Outputs:
- activations: float32 [24576, 512], P(('dp', 'mp'))
- input_grad: float32 [24576, 512], P(('dp', 'mp'))
- qkv_master: float32 [2, 512, 3, 512], P(None, 'dp', None, 'mp')
- qkv_mean: float32 [2, 512, 3, 512], P(None, 'dp', None, 'mp')
- qkv_square: float32 [2, 512, 3, 512], P(None, 'dp', None, 'mp')
- qkv_copy: bfloat16 [2, 512, 3, 512], P(None, 'dp', None, 'mp')
- out_master: float32 [2, 512, 512], P(None, 'mp', 'dp')
- out_mean: float32 [2, 512, 512], P(None, 'mp', 'dp')
- out_square: float32 [2, 512, 512], P(None, 'mp', 'dp')
- out_copy: bfloat16 [2, 512, 512], P(None, 'mp', 'dp')
- up_master: float32 [2, 512, 2048], P(None, 'dp', 'mp')
- up_mean: float32 [2, 512, 2048], P(None, 'dp', 'mp')
- up_square: float32 [2, 512, 2048], P(None, 'dp', 'mp')
- up_copy: bfloat16 [2, 512, 2048], P(None, 'dp', 'mp')
- down_master: float32 [2, 2048, 512], P(None, 'mp', 'dp')
- down_mean: float32 [2, 2048, 512], P(None, 'mp', 'dp')
- down_square: float32 [2, 2048, 512], P(None, 'mp', 'dp')
- down_copy: bfloat16 [2, 2048, 512], P(None, 'mp', 'dp')
- norm_master: float32 [2, 4, 512], replicated
- norm_mean: float32 [2, 4, 512], replicated
- norm_square: float32 [2, 4, 512], replicated
- embed_master: float32 [27, 512], replicated
- embed_mean: float32 [27, 512], replicated
- embed_square: float32 [27, 512], replicated
Inputs may be any that keep to these rules, and one draw needn't show every extreme that they name: `norm_params`: rows 0 and 2 of each layer are gains, rows 1 and 3 shifts. `qkv_first`: entries of either sign, none zero. `qkv_second`: positive entries. `out_first`: entries of either sign, none zero. `out_second`: positive entries. `up_first`: entries of either sign, none zero. `up_second`: positive entries. `down_first`: entries of either sign, none zero. `down_second`: positive entries. `norm_first`: entries of either sign, none zero. `norm_second`: positive entries. `embed_first`: entries of either sign, none zero. `embed_second`: positive entries.
All inputs are finite; a program needn't handle non-finite values.
Results may differ from a plain program's by a relative error of at most 0.028.
Values may be sent and summed in bfloat16 or wider, within the bound.
No kernel may reach another device: no remote copies, remote signals or barrier semaphores. Data moves between devices by JAX's collectives and lax.ppermute only.
A program may use at most 192 MiB of HBM per device.

v0:
```python
import math

import jax
import jax.numpy as jnp
from jax import lax
from jax.sharding import PartitionSpec as P

HEAD_DIM = 64
FF = 2048
VOCAB = 27
LAYERS = 2
LEN = 1024
STEP = 10
D = 512


highest = lax.Precision.HIGHEST
eps_norm = 1e-05
beta_one = 0.5
beta_two = 0.5
adam_eps = 1e-08
decay_matrix = 0.01
vector_rate = 0.6
embed_rate = 1.0


def layer_norm(values, gain_vec, shift_vec):
    row_mean = jnp.mean(values, axis=-1, keepdims=True)
    centered = values - row_mean
    variance = jnp.mean(centered * centered, axis=-1, keepdims=True)
    return centered * lax.rsqrt(variance + eps_norm) * gain_vec + shift_vec


def gelu_exact(hidden):
    return jax.nn.gelu(hidden, approximate=False)


def time_features(step_values):
    half_width = D // 2
    frequency = jnp.exp(-math.log(10000.0) * jnp.arange(half_width, dtype=jnp.float32) / half_width)
    angles = step_values.astype(jnp.float32)[:, None] * frequency[None, :]
    return jnp.concatenate([jnp.sin(angles), jnp.cos(angles)], axis=1)


def adamw(weight, mean_old, square_old, gradient, step_rate, decay_weight):
    mean_new = beta_one * mean_old + (1.0 - beta_one) * gradient
    square_new = beta_two * square_old + (1.0 - beta_two) * gradient * gradient
    fix_one = 1.0 - beta_one**STEP
    fix_two = 1.0 - beta_two**STEP
    direction = mean_new / fix_one / (jnp.sqrt(square_new / fix_two) + adam_eps)
    return (weight - step_rate * (direction + decay_weight * weight), mean_new, square_new)


def contract_first(left_side, right_side):
    return lax.dot_general(
        left_side, right_side, (((0,), (0,)), ((), ())), preferred_element_type=jnp.float32
    )


def contract_last(left_side, right_side):
    return lax.dot_general(
        left_side, right_side, (((1,), (1,)), ((), ())), preferred_element_type=jnp.float32
    )


def gather_weights(qkv_weight, out_weight, up_weight, down_weight, layer_index):
    return (
        lax.all_gather(qkv_weight[layer_index].astype(jnp.bfloat16), "dp", axis=0, tiled=True),
        lax.all_gather(out_weight[layer_index].astype(jnp.bfloat16), "dp", axis=1, tiled=True),
        lax.all_gather(up_weight[layer_index].astype(jnp.bfloat16), "dp", axis=0, tiled=True),
        lax.all_gather(down_weight[layer_index].astype(jnp.bfloat16), "dp", axis=1, tiled=True),
    )


def gather_rows(values):
    return lax.all_gather(values.astype(jnp.bfloat16), "mp", axis=0, tiled=True)


def gather_grads(values):
    return lax.all_gather(values.astype(jnp.bfloat16), "mp", axis=0, tiled=True)


def scatter_rows(left_side, right_side, row_count):

    def partial_rows(begin_row, row_span):
        return jnp.dot(left_side, right_side, preferred_element_type=jnp.float32)

    return lax.psum_scatter(
        partial_rows(jnp.int32(0), row_count * lax.axis_size("mp")),
        "mp",
        scatter_dimension=0,
        tiled=True,
    )


def scatter_grads(left_side, right_side, row_count):

    def partial_rows(begin_row, row_span):
        return contract_last(left_side, right_side)

    return lax.psum_scatter(
        partial_rows(jnp.int32(0), row_count * lax.axis_size("mp")),
        "mp",
        scatter_dimension=0,
        tiled=True,
    )


def split_heads(flat_qkv, seq_here):
    heads_here = flat_qkv.shape[1] // (3 * HEAD_DIM)
    shaped = flat_qkv.reshape(seq_here, LEN, 3, heads_here, HEAD_DIM)
    return (shaped[:, :, 0], shaped[:, :, 1], shaped[:, :, 2])


def query_blocks(values):
    block_rows = min(512, LEN)
    shaped = values.reshape((values.shape[0], LEN // block_rows, block_rows) + values.shape[2:])
    return jnp.swapaxes(shaped, 0, 1)


def from_blocks(values):
    return jnp.swapaxes(values, 0, 1).reshape(values.shape[1] * LEN, -1)


def attend_forward(flat_qkv, seq_here):
    query, keys, values = split_heads(flat_qkv, seq_here)
    score_scale = HEAD_DIM ** (-0.5)

    def block_step(query_part):
        scores = (
            jnp.einsum("sqhd,skhd->shqk", query_part, keys, preferred_element_type=jnp.float32)
            * score_scale
        )
        row_max = jnp.max(scores, axis=-1, keepdims=True)
        exponent = jnp.exp(scores - row_max)
        denominator = jnp.sum(exponent, axis=-1, keepdims=True)
        probability = (exponent / denominator).astype(jnp.bfloat16)
        attended = jnp.einsum(
            "shqk,skhd->sqhd", probability, values, preferred_element_type=jnp.float32
        )
        return (attended.astype(jnp.bfloat16), (row_max + jnp.log(denominator))[..., 0])

    attended, logsum = lax.map(block_step, query_blocks(query))
    return (from_blocks(attended), logsum)


def attend_backward(flat_qkv, logsum, grad_attended, seq_here):
    query, keys, values = split_heads(flat_qkv, seq_here)
    heads_here = query.shape[2]
    grad_heads = grad_attended.reshape(seq_here, LEN, heads_here, HEAD_DIM)
    score_scale = HEAD_DIM ** (-0.5)

    def block_step(running, block_inputs):
        key_sum, value_sum = running
        query_part, logsum_part, grad_part = block_inputs
        scores = (
            jnp.einsum("sqhd,skhd->shqk", query_part, keys, preferred_element_type=jnp.float32)
            * score_scale
        )
        probability = jnp.exp(scores - logsum_part[..., None])
        prob_low = probability.astype(jnp.bfloat16)
        attended = jnp.einsum(
            "shqk,skhd->sqhd", prob_low, values, preferred_element_type=jnp.float32
        ).astype(jnp.bfloat16)
        grad_prob = jnp.einsum(
            "sqhd,skhd->shqk", grad_part, values, preferred_element_type=jnp.float32
        )
        grad_scores = (
            probability * (grad_prob - jnp.sum(grad_prob * probability, axis=-1, keepdims=True))
        ).astype(jnp.bfloat16)
        grad_query = (
            jnp.einsum("shqk,skhd->sqhd", grad_scores, keys, preferred_element_type=jnp.float32)
            * score_scale
        )
        key_sum = (
            key_sum
            + jnp.einsum(
                "shqk,sqhd->skhd", grad_scores, query_part, preferred_element_type=jnp.float32
            )
            * score_scale
        )
        value_sum = value_sum + jnp.einsum(
            "shqk,sqhd->skhd", prob_low, grad_part, preferred_element_type=jnp.float32
        )
        return ((key_sum, value_sum), (attended, grad_query))

    zero_block = jnp.zeros((seq_here, LEN, heads_here, HEAD_DIM), jnp.float32)
    (key_sum, value_sum), (attended, grad_query) = lax.scan(
        block_step,
        (zero_block, zero_block),
        (query_blocks(query), logsum, query_blocks(grad_heads)),
    )
    grad_query = jnp.swapaxes(grad_query, 0, 1).reshape(seq_here, LEN, heads_here, HEAD_DIM)
    grad_qkv = jnp.stack([grad_query, key_sum, value_sum], axis=2).astype(jnp.bfloat16)
    return (from_blocks(attended), grad_qkv.reshape(seq_here * LEN, 3 * heads_here * HEAD_DIM))


def shards(
    token_ids,
    timesteps,
    importance,
    cotangent,
    qkv_weight,
    out_weight,
    up_weight,
    down_weight,
    norm_params,
    embed_table,
    qkv_first,
    qkv_second,
    out_first,
    out_second,
    up_first,
    up_second,
    down_first,
    down_second,
    norm_first,
    norm_second,
    embed_first,
    embed_second,
):
    row_count = token_ids.shape[0]
    seq_here = timesteps.shape[0]
    row_start = lax.axis_index("mp") * row_count
    position = row_start + jnp.arange(row_count, dtype=jnp.int32)
    member = (position[:, None] // LEN == jnp.arange(seq_here, dtype=jnp.int32)[None, :]).astype(
        jnp.float32
    )
    letters = (token_ids[:, None] == jnp.arange(VOCAB, dtype=jnp.int32)[None, :]).astype(
        jnp.float32
    )
    residual = jnp.dot(letters, embed_table, precision=highest) + jnp.dot(
        member, time_features(timesteps), precision=highest
    )
    kept_values = []
    for layer_index in range(LAYERS):
        gathered = gather_weights(qkv_weight, out_weight, up_weight, down_weight, layer_index)
        qkv_w, out_w, up_w, down_w = gathered
        normed = gather_rows(
            layer_norm(residual, norm_params[layer_index, 0], norm_params[layer_index, 1])
        )
        projected = jnp.dot(
            normed, qkv_w.reshape(D, -1), preferred_element_type=jnp.float32
        ).astype(jnp.bfloat16)
        attended, logsum = attend_forward(projected, seq_here)
        middle = residual + scatter_rows(attended, out_w, row_count)
        normed_two = gather_rows(
            layer_norm(middle, norm_params[layer_index, 2], norm_params[layer_index, 3])
        )
        hidden = jnp.dot(normed_two, up_w, preferred_element_type=jnp.float32)
        activated = gelu_exact(hidden).astype(jnp.bfloat16)
        after = middle + scatter_rows(activated, down_w, row_count)
        kept_values.append((residual, middle, logsum, gathered, normed, normed_two))
        residual = after
    residual_grad = (
        cotangent.astype(jnp.float32) * jnp.dot(member, importance, precision=highest)[:, None]
    )
    norm_grads = [None] * LAYERS
    layer_grads = [None] * LAYERS
    for layer_index in reversed(range(LAYERS)):
        layer_input, middle, logsum, kept_weights, kept_normed, kept_two = kept_values[layer_index]
        qkv_w, out_w, up_w, down_w = gather_weights(
            qkv_weight, out_weight, up_weight, down_weight, layer_index
        )
        normed_two = gather_rows(
            layer_norm(middle, norm_params[layer_index, 2], norm_params[layer_index, 3])
        )
        normed = gather_rows(
            layer_norm(layer_input, norm_params[layer_index, 0], norm_params[layer_index, 1])
        )
        grad_branch = gather_grads(residual_grad)
        hidden = jnp.dot(normed_two, up_w, preferred_element_type=jnp.float32)
        activated, gelu_back = jax.vjp(gelu_exact, hidden)
        down_grad = contract_first(activated.astype(jnp.bfloat16), grad_branch)
        grad_hidden = gelu_back(contract_last(grad_branch, down_w))[0].astype(jnp.bfloat16)
        up_grad = contract_first(normed_two, grad_hidden)
        grad_normed = scatter_grads(grad_hidden, up_w, row_count)
        unused_two, norm_back = jax.vjp(
            layer_norm, middle, norm_params[layer_index, 2], norm_params[layer_index, 3]
        )
        grad_middle, gain_two, shift_two = norm_back(grad_normed)
        residual_grad = residual_grad + grad_middle
        grad_attn = gather_grads(residual_grad)
        qkv_flat = qkv_w.reshape(D, -1)
        projected = jnp.dot(normed, qkv_flat, preferred_element_type=jnp.float32).astype(
            jnp.bfloat16
        )
        grad_attended = contract_last(grad_attn, out_w).astype(jnp.bfloat16)
        attended, grad_qkv = attend_backward(projected, logsum, grad_attended, seq_here)
        out_grad = contract_first(attended, grad_attn)
        qkv_grad = contract_first(normed, grad_qkv).reshape(qkv_w.shape)
        grad_entry = scatter_grads(grad_qkv, qkv_flat, row_count)
        unused_one, norm_back = jax.vjp(
            layer_norm, layer_input, norm_params[layer_index, 0], norm_params[layer_index, 1]
        )
        grad_input, gain_one, shift_one = norm_back(grad_entry)
        residual_grad = residual_grad + grad_input
        norm_grads[layer_index] = jnp.stack([gain_one, shift_one, gain_two, shift_two])
        layer_grads[layer_index] = (
            lax.psum_scatter(qkv_grad, "dp", scatter_dimension=0, tiled=True),
            lax.psum_scatter(out_grad, "dp", scatter_dimension=1, tiled=True),
            lax.psum_scatter(up_grad, "dp", scatter_dimension=0, tiled=True),
            lax.psum_scatter(down_grad, "dp", scatter_dimension=1, tiled=True),
        )
    embed_local = lax.dot_general(
        letters,
        residual_grad,
        (((0,), (0,)), ((), ())),
        precision=highest,
        preferred_element_type=jnp.float32,
    )
    norm_grad, embed_grad = lax.psum((jnp.stack(norm_grads), embed_local), ("dp", "mp"))
    qkv_grad = jnp.stack([entry_grads[0] for entry_grads in layer_grads])
    out_grad = jnp.stack([entry_grads[1] for entry_grads in layer_grads])
    up_grad = jnp.stack([entry_grads[2] for entry_grads in layer_grads])
    down_grad = jnp.stack([entry_grads[3] for entry_grads in layer_grads])
    qkv_master, qkv_mean, qkv_square = adamw(
        qkv_weight, qkv_first, qkv_second, qkv_grad, 2.0 / math.sqrt(D), decay_matrix
    )
    out_master, out_mean, out_square = adamw(
        out_weight, out_first, out_second, out_grad, 2.0 / math.sqrt(D), decay_matrix
    )
    up_master, up_mean, up_square = adamw(
        up_weight, up_first, up_second, up_grad, 2.0 / math.sqrt(D), decay_matrix
    )
    down_master, down_mean, down_square = adamw(
        down_weight, down_first, down_second, down_grad, 2.0 / math.sqrt(FF), decay_matrix
    )
    norm_master, norm_mean, norm_square = adamw(
        norm_params, norm_first, norm_second, norm_grad, vector_rate, 0.0
    )
    embed_master, embed_mean, embed_square = adamw(
        embed_table, embed_first, embed_second, embed_grad, embed_rate, 0.0
    )
    return (
        residual,
        residual_grad,
        qkv_master,
        qkv_mean,
        qkv_square,
        qkv_master.astype(jnp.bfloat16),
        out_master,
        out_mean,
        out_square,
        out_master.astype(jnp.bfloat16),
        up_master,
        up_mean,
        up_square,
        up_master.astype(jnp.bfloat16),
        down_master,
        down_mean,
        down_square,
        down_master.astype(jnp.bfloat16),
        norm_master,
        norm_mean,
        norm_square,
        embed_master,
        embed_mean,
        embed_square,
    )


def solution(mesh):
    placed = (
        P(("dp", "mp")),
        P("dp"),
        P("dp"),
        P(("dp", "mp"), None),
        P(None, "dp", None, "mp"),
        P(None, "mp", "dp"),
        P(None, "dp", "mp"),
        P(None, "mp", "dp"),
        P(),
        P(),
        P(None, "dp", None, "mp"),
        P(None, "dp", None, "mp"),
        P(None, "mp", "dp"),
        P(None, "mp", "dp"),
        P(None, "dp", "mp"),
        P(None, "dp", "mp"),
        P(None, "mp", "dp"),
        P(None, "mp", "dp"),
        P(),
        P(),
        P(),
        P(),
    )
    return jax.shard_map(
        shards,
        mesh=mesh,
        in_specs=placed,
        out_specs=(
            P(("dp", "mp"), None),
            P(("dp", "mp"), None),
            P(None, "dp", None, "mp"),
            P(None, "dp", None, "mp"),
            P(None, "dp", None, "mp"),
            P(None, "dp", None, "mp"),
            P(None, "mp", "dp"),
            P(None, "mp", "dp"),
            P(None, "mp", "dp"),
            P(None, "mp", "dp"),
            P(None, "dp", "mp"),
            P(None, "dp", "mp"),
            P(None, "dp", "mp"),
            P(None, "dp", "mp"),
            P(None, "mp", "dp"),
            P(None, "mp", "dp"),
            P(None, "mp", "dp"),
            P(None, "mp", "dp"),
            P(),
            P(),
            P(),
            P(),
            P(),
            P(),
        ),
        check_vma=False,
    )
```

profile of v0, /device:TPU:0, one launch (start us, length us, event | category | flops | bytes accessed | tf_op | source)
XLA Modules:
  0.0 2139.6 jit_solution(10763487934154703272)
XLA Ops:
  14.7 11.0 all-gather
  35.7 44.5 %all-gather.17.cloned.1.call-done = bf16[3072,512]{0,1:T(8,128)(2,1)} async-done(((bf16[768,512]{0,1:T(8,128)(2,1)}), bf16[3072,512]{0,1:T(8,128)(2,1)}) %all-gather.17.cloned.1.call-update) | async-done | bytes 3145744 | tf_op jit(solution)/shard_map/all_gather | solution.py:76
  108.8 20.6 while.58
  140.8 109.5 %reduce-scatter.17.cloned.1.call-done = f32[768,512]{0,1:T(8,128)} async-done(((f32[3072,512]{0,1:T(8,128)}), f32[768,512]{0,1:T(8,128)}) %reduce-scatter.17.cloned.1.call-update) | async-done | bytes 1572880 | tf_op jit(solution)/shard_map/reduce_scatter | solution.py:88
  255.5 10.2 all-gather.3
  276.2 42.7 %all-gather.19.cloned.1.call-done = bf16[3072,512]{0,1:T(8,128)(2,1)} async-done(((bf16[768,512]{0,1:T(8,128)(2,1)}), bf16[3072,512]{0,1:T(8,128)(2,1)}) %all-gather.19.cloned.1.call-update) | async-done | bytes 3145744 | tf_op jit(solution)/shard_map/all_gather | solution.py:76
  318.9 17.7 multiply_convert_fusion.3
  342.7 109.5 %reduce-scatter.19.cloned.1.call-done = f32[768,512]{0,1:T(8,128)} async-done(((f32[3072,512]{0,1:T(8,128)}), f32[768,512]{0,1:T(8,128)}) %reduce-scatter.19.cloned.1.call-update) | async-done | bytes 1572880 | tf_op jit(solution)/shard_map/reduce_scatter | solution.py:88
  475.3 45.1 %all-gather.21.cloned.1.call-done = bf16[3072,512]{0,1:T(8,128)(2,1)} async-done(((bf16[768,512]{0,1:T(8,128)(2,1)}), bf16[3072,512]{0,1:T(8,128)(2,1)}) %all-gather.21.cloned.1.call-update) | async-done | bytes 3145744 | tf_op jit(solution)/shard_map/all_gather | solution.py:76
  540.4 18.6 while.59
  569.8 109.5 %reduce-scatter.21.cloned.1.call-done = f32[768,512]{0,1:T(8,128)} async-done(((f32[3072,512]{0,1:T(8,128)}), f32[768,512]{0,1:T(8,128)}) %reduce-scatter.21.cloned.1.call-update) | async-done | bytes 1572880 | tf_op jit(solution)/shard_map/reduce_scatter | solution.py:88
  688.9 10.0 all-gather.7
  698.9 10.8 all-gather.6
  709.7 38.3 %all-gather.23.cloned.1.call-done = bf16[3072,512]{0,1:T(8,128)(2,1)} async-done(((bf16[768,512]{0,1:T(8,128)(2,1)}), bf16[3072,512]{0,1:T(8,128)(2,1)}) %all-gather.23.cloned.1.call-update) | async-done | bytes 3145744 | tf_op jit(solution)/shard_map/all_gather | solution.py:76
  748.0 18.0 multiply_convert_fusion.2
  766.0 45.7 %all-gather.25.cloned.1.call-done = bf16[3072,512]{0,1:T(8,128)(2,1)} async-done(((bf16[768,512]{0,1:T(8,128)(2,1)}), bf16[3072,512]{0,1:T(8,128)(2,1)}) %all-gather.25.cloned.1.call-update) | async-done | bytes 3145744 | tf_op jit(solution)/shard_map/all_gather | solution.py:80
  832.9 102.5 %reduce-scatter.25.cloned.1.call-done = f32[768,512]{0,1:T(8,128)} async-done(((f32[3072,512]{0,1:T(8,128)}), f32[768,512]{0,1:T(8,128)}) %reduce-scatter.25.cloned.1.call-update) | async-done | bytes 1572880 | tf_op jit(solution)/shard_map/reduce_scatter | solution.py:101
  938.4 110.4 %reduce-scatter.23.cloned.1.call-done = f32[768,512]{0,1:T(8,128)} async-done(((f32[3072,512]{0,1:T(8,128)}), f32[768,512]{0,1:T(8,128)}) %reduce-scatter.23.cloned.1.call-update) | async-done | bytes 1572880 | tf_op jit(solution)/shard_map/reduce_scatter | solution.py:88
  1055.4 64.1 %all-gather.27.cloned.1.call-done = bf16[3072,512]{0,1:T(8,128)(2,1)} async-done(((bf16[768,512]{0,1:T(8,128)(2,1)}), bf16[3072,512]{0,1:T(8,128)(2,1)}) %all-gather.27.cloned.1.call-update) | async-done | bytes 3145744 | tf_op jit(solution)/shard_map/all_gather | solution.py:80
  1133.4 59.8 %while.60 = (s32[]{:T(128)}, f32[3,1024,2,64]{1,3,2,0:T(8,128)}, f32[3,1024,2,64]{1,3,2,0:T(8,128)}, bf16[2,3,512,2,64]{2,4,3,1,0:T(8,128)(2,1)}, bf16[2,3,512,2...) while((s32[]{:T(128)}, f32[3,1024,2,64]{1,3,2,0:T(8,128)}, ...), condition=%wide.region_25.26_spmd.clone, body=%wide.region_23.25_spmd.clone.sunk | while | flops 2465461248 | bytes 147554672 | solution.py:188
  1210.3 109.5 %reduce-scatter.27.cloned.1.call-done = f32[768,512]{0,1:T(8,128)} async-done(((f32[3072,512]{0,1:T(8,128)}), f32[768,512]{0,1:T(8,128)}) %reduce-scatter.27.cloned.1.call-update) | async-done | bytes 1572880 | tf_op jit(solution)/shard_map/reduce_scatter | solution.py:101
  1325.7 63.7 %all-gather.29.cloned.1.call-done = bf16[3072,512]{0,1:T(8,128)(2,1)} async-done(((bf16[768,512]{0,1:T(8,128)(2,1)}), bf16[3072,512]{0,1:T(8,128)(2,1)}) %all-gather.29.cloned.1.call-update) | async-done | bytes 3145744 | tf_op jit(solution)/shard_map/all_gather | solution.py:80
  1405.1 109.5 %reduce-scatter.29.cloned.1.call-done = f32[768,512]{0,1:T(8,128)} async-done(((f32[3072,512]{0,1:T(8,128)}), f32[768,512]{0,1:T(8,128)}) %reduce-scatter.29.cloned.1.call-update) | async-done | bytes 1572880 | tf_op jit(solution)/shard_map/reduce_scatter | solution.py:101
  1550.8 33.5 %all-gather.31.cloned.1.call-done = bf16[3072,512]{0,1:T(8,128)(2,1)} async-done(((bf16[768,512]{0,1:T(8,128)(2,1)}), bf16[3072,512]{0,1:T(8,128)(2,1)}) %all-gather.31.cloned.1.call-update) | async-done | bytes 3145744 | tf_op jit(solution)/shard_map/all_gather | solution.py:80
  1594.1 58.3 %while.61 = (s32[]{:T(128)}, f32[3,1024,2,64]{1,3,2,0:T(8,128)}, f32[3,1024,2,64]{1,3,2,0:T(8,128)}, bf16[2,3,512,2,64]{2,4,3,1,0:T(8,128)(2,1)}, bf16[2,3,512,2...) while((s32[]{:T(128)}, f32[3,1024,2,64]{1,3,2,0:T(8,128)}, ...), condition=%wide.region_34.35_spmd.clone, body=%wide.region_32.34_spmd.clone.sunk | while | flops 2465461248 | bytes 144408912 | solution.py:188
  1700.4 39.2 %reduce-scatter.41.cloned.1.call-done = f32[64,512]{1,0:T(8,128)} async-done(((f32[512,512]{1,0:T(8,128)}), f32[64,512]{1,0:T(8,128)}) %reduce-scatter.41.cloned.1.call-update) | async-done | bytes 131088 | tf_op jit(solution)/shard_map/reduce_scatter | solution.py:302
  1747.2 28.9 %reduce-scatter.39.cloned.1.call-done = f32[128,64]{0,1:T(8,128)} async-done(((f32[128,512]{0,1:T(8,128)}), f32[128,64]{0,1:T(8,128)}) %reduce-scatter.39.cloned.1.call-update) | async-done | bytes 32784 | tf_op jit(solution)/shard_map/reduce_scatter | solution.py:301
  1776.1 36.9 %reduce-scatter.37.cloned.1.call-done = f32[128,64]{0,1:T(8,128)} async-done(((f32[128,512]{0,1:T(8,128)}), f32[128,64]{0,1:T(8,128)}) %reduce-scatter.37.cloned.1.call-update) | async-done | bytes 32784 | tf_op jit(solution)/shard_map/reduce_scatter | solution.py:301
  1814.5 111.6 %reduce-scatter.31.cloned.1.call-done = f32[768,512]{0,1:T(8,128)} async-done(((f32[3072,512]{0,1:T(8,128)}), f32[768,512]{0,1:T(8,128)}) %reduce-scatter.31.cloned.1.call-update) | async-done | bytes 1572880 | tf_op jit(solution)/shard_map/reduce_scatter | solution.py:101
  1934.4 31.0 %reduce-scatter.35.cloned.1.call-done = f32[64,3,128]{2,0,1:T(8,128)} async-done(((f32[512,3,128]{2,0,1:T(8,128)}), f32[64,3,128]{2,0,1:T(8,128)}) %reduce-scatter.35.cloned.1.call-update) | async-done | bytes 98320 | tf_op jit(solution)/shard_map/reduce_scatter | solution.py:300
  1965.4 38.0 %reduce-scatter.33.cloned.1.call-done = f32[64,3,128]{2,0,1:T(8,128)} async-done(((f32[512,3,128]{2,0,1:T(8,128)}), f32[64,3,128]{2,0,1:T(8,128)}) %reduce-scatter.33.cloned.1.call-update) | async-done | bytes 98320 | tf_op jit(solution)/shard_map/reduce_scatter | solution.py:300
  2008.4 121.3 %all-reduce.3.cloned.1.call-done = (f32[2,4,512]{2,1,0:T(4,128)}, f32[27,512]{1,0:T(8,128)}) async-done(((f32[2,4,512]{2,1,0:T(4,128)}, f32[27,512]{1,0:T(8,128)}), (f32[2,4,512]{2,1,0:T(4,128)}, f32[27,512]{1,0:T(8,128)})) %all-reduce.3.cloned.1.call-update) | async-done | bytes 71696 | tf_op jit(solution)/shard_map/psum | solution.py:312
  (554 shorter events, 500.1 us)
Async XLA Ops:
  7.2 679.0 %copy-start = (f32[3]{0:T(128)S(1)}, f32[3]{0:T(128)}, u32[]{:S(2)}) copy-start(f32[3]{0:T(128)} %param.32) | copy-start | bytes 40
  7.2 73.0 %all-gather.17.cloned.1.call-start = ((), (), s32[]{:S(2)}) async-start(), calls=%async_computation.16 | async-start | bytes 3932160 | tf_op jit(solution)/shard_map/all_gather | solution.py:76
  9.4 243.5 %copy-start.120 = (f32[1,1,512]{2,1,0:T(1,128)}, f32[1,1,512]{2,1,0:T(1,128)S(1)}, u32[]{:S(2)}) copy-start(f32[1,1,512]{2,1,0:T(1,128)S(1)} %get-tuple-element.557) | copy-start | bytes 6148
  12.4 237.9 %copy-start.8 = (f32[768,512]{0,1:T(8,128)}, f32[768,512]{0,1:T(8,128)S(1)}, u32[]{:S(2)}) copy-start(f32[768,512]{0,1:T(8,128)S(1)} %get-tuple-element.564) | copy-start | bytes 4718596
  13.9 236.5 %reduce-scatter.17.cloned.1.call-start = ((), (), s32[]{:S(2)}) async-start(), calls=%async_computation.17 | async-start | bytes 7864320 | tf_op jit(solution)/shard_map/reduce_scatter | solution.py:88
  140.8 178.1 %all-gather.19.cloned.1.call-start = ((), (), s32[]{:S(2)}) async-start(), calls=%async_computation.18 | async-start | bytes 3932160 | tf_op jit(solution)/shard_map/all_gather | solution.py:76
  252.1 200.1 %copy-start.21 = (f32[768,512]{0,1:T(8,128)}, f32[768,512]{0,1:T(8,128)S(1)}, u32[]{:S(2)}) copy-start(f32[768,512]{0,1:T(8,128)S(1)} %get-tuple-element.529) | copy-start | bytes 4718596
  254.7 197.5 %reduce-scatter.19.cloned.1.call-start = ((), (), s32[]{:S(2)}) async-start(), calls=%async_computation.19 | async-start | bytes 7864320 | tf_op jit(solution)/shard_map/reduce_scatter | solution.py:88
  342.6 177.8 %all-gather.21.cloned.1.call-start = ((), (), s32[]{:S(2)}) async-start(), calls=%async_computation.20 | async-start | bytes 3932160 | tf_op jit(solution)/shard_map/all_gather | solution.py:76
  456.3 223.0 %reduce-scatter.21.cloned.1.call-start = ((), (), s32[]{:S(2)}) async-start(), calls=%async_computation.21 | async-start | bytes 7864320 | tf_op jit(solution)/shard_map/reduce_scatter | solution.py:88
  569.8 178.2 %all-gather.23.cloned.1.call-start = ((), (), s32[]{:S(2)}) async-start(), calls=%async_computation.22 | async-start | bytes 3932160 | tf_op jit(solution)/shard_map/all_gather | solution.py:76
  683.8 127.9 %all-gather.25.cloned.1.call-start = ((), (), s32[]{:S(2)}) async-start(), calls=%async_computation.24 | async-start | bytes 3932160 | tf_op jit(solution)/shard_map/all_gather | solution.py:80
  686.6 366.3 %copy-start.108 = (f32[768]{0:T(1024)}, f32[768]{0:T(1024)S(1)}, u32[]{:S(2)}) copy-start(f32[768]{0:T(1024)S(1)} %convolution_reduce_fusion) | copy-start | bytes 9220
  688.8 246.6 %reduce-scatter.25.cloned.1.call-start = ((), (), s32[]{:S(2)}) async-start(), calls=%async_computation.25 | async-start | bytes 7864320 | tf_op jit(solution)/shard_map/reduce_scatter | solution.py:101
  825.8 223.0 %reduce-scatter.23.cloned.1.call-start = ((), (), s32[]{:S(2)}) async-start(), calls=%async_computation.23 | async-start | bytes 7864320 | tf_op jit(solution)/shard_map/reduce_scatter | solution.py:88
  832.8 286.6 %all-gather.27.cloned.1.call-start = ((), (), s32[]{:S(2)}) async-start(), calls=%async_computation.26 | async-start | bytes 3932160 | tf_op jit(solution)/shard_map/all_gather | solution.py:80
  1055.3 264.5 %reduce-scatter.27.cloned.1.call-start = ((), (), s32[]{:S(2)}) async-start(), calls=%async_computation.27 | async-start | bytes 7864320 | tf_op jit(solution)/shard_map/reduce_scatter | solution.py:101
  1210.3 179.1 %all-gather.29.cloned.1.call-start = ((), (), s32[]{:S(2)}) async-start(), calls=%async_computation.28 | async-start | bytes 3932160 | tf_op jit(solution)/shard_map/all_gather | solution.py:80
  1325.3 189.4 %reduce-scatter.29.cloned.1.call-start = ((), (), s32[]{:S(2)}) async-start(), calls=%async_computation.29 | async-start | bytes 7864320 | tf_op jit(solution)/shard_map/reduce_scatter | solution.py:101
  1405.1 179.2 %all-gather.31.cloned.1.call-start = ((), (), s32[]{:S(2)}) async-start(), calls=%async_computation.30 | async-start | bytes 3932160 | tf_op jit(solution)/shard_map/all_gather | solution.py:80
  1520.1 168.6 %reduce-scatter.47.cloned.1.call-start = ((), (), s32[]{:S(2)}) async-start(), calls=%async_computation.39 | async-start | bytes 1179648 | tf_op jit(solution)/shard_map/reduce_scatter | solution.py:303
  1526.0 162.8 %reduce-scatter.45.cloned.1.call-start = ((), (), s32[]{:S(2)}) async-start(), calls=%async_computation.38 | async-start | bytes 1179648 | tf_op jit(solution)/shard_map/reduce_scatter | solution.py:303
  1531.0 169.4 %reduce-scatter.43.cloned.1.call-start = ((), (), s32[]{:S(2)}) async-start(), calls=%async_computation.37 | async-start | bytes 1179648 | tf_op jit(solution)/shard_map/reduce_scatter | solution.py:302
  1536.8 202.9 %reduce-scatter.41.cloned.1.call-start = ((), (), s32[]{:S(2)}) async-start(), calls=%async_computation.36 | async-start | bytes 1179648 | tf_op jit(solution)/shard_map/reduce_scatter | solution.py:302
  1541.5 234.6 %reduce-scatter.39.cloned.1.call-start = ((), (), s32[]{:S(2)}) async-start(), calls=%async_computation.35 | async-start | bytes 294912 | tf_op jit(solution)/shard_map/reduce_scatter | solution.py:301
  1550.8 262.3 %reduce-scatter.37.cloned.1.call-start = ((), (), s32[]{:S(2)}) async-start(), calls=%async_computation.34 | async-start | bytes 294912 | tf_op jit(solution)/shard_map/reduce_scatter | solution.py:301
  1672.9 253.2 %reduce-scatter.31.cloned.1.call-start = ((), (), s32[]{:S(2)}) async-start(), calls=%async_computation.31 | async-start | bytes 7864320 | tf_op jit(solution)/shard_map/reduce_scatter | solution.py:101
  1679.1 286.3 %reduce-scatter.35.cloned.1.call-start = ((), (), s32[]{:S(2)}) async-start(), calls=%async_computation.33 | async-start | bytes 884736 | tf_op jit(solution)/shard_map/reduce_scatter | solution.py:300
  1685.5 317.9 %reduce-scatter.33.cloned.1.call-start = ((), (), s32[]{:S(2)}) async-start(), calls=%async_computation.32 | async-start | bytes 884736 | tf_op jit(solution)/shard_map/reduce_scatter | solution.py:300
  1747.2 382.6 %all-reduce.3.cloned.1.call-start = ((), (), s32[]{:S(2)}) async-start(), calls=%async_computation.40 | async-start | bytes 163840 | tf_op jit(solution)/shard_map/psum | solution.py:312
  1930.9 201.7 %copy-start.1 = (f32[3]{0:T(128)S(1)}, f32[3]{0:T(128)}, u32[]{:S(2)}) copy-start(f32[3]{0:T(128)} %param.32) | copy-start | bytes 40
  1932.7 198.4 %copy-start.79 = (f32[27,512]{1,0:T(8,128)S(1)}, f32[27,512]{1,0:T(8,128)}, u32[]{:S(2)}) copy-start(f32[27,512]{1,0:T(8,128)} %param.39) | copy-start | bytes 165892
  (146 other events, 5559.3 us)
Sparse Core Ops, SparseCore 0:
  14.0 66.1 all-gather.16
  140.9 109.4 reduce-scatter.16
  254.8 63.9 all-gather.18
  342.7 109.4 reduce-scatter.18
  456.4 63.9 all-gather.20
  569.9 109.4 reduce-scatter.20
  683.9 63.9 all-gather.22
  749.5 62.1 all-gather.24
  825.9 109.4 reduce-scatter.24
  937.5 111.2 reduce-scatter.22
  1055.4 63.9 all-gather.26
  1210.4 109.4 reduce-scatter.26
  1325.4 63.9 all-gather.28
  1405.2 109.4 reduce-scatter.28
  1520.2 63.9 all-gather.30
  1587.3 34.7 reduce-scatter.46
  1625.2 36.0 reduce-scatter.44
  1664.3 36.0 reduce-scatter.42
  1703.5 36.0 reduce-scatter.40
  1742.5 33.5 reduce-scatter.38
  1779.4 33.5 reduce-scatter.36
  1815.3 110.7 reduce-scatter.30
  1929.8 35.5 reduce-scatter.34
  1968.4 34.9 reduce-scatter.32
  2009.7 120.0 all-reduce.2
where the time goes:
time: 2150 us; the launch traced here: 2140 us
  waiting for transfers between devices  1560 us (73%)
  matrix products  260 us (12%)
  local copies, waits for them, and re-layouts  138 us (6%)
  other arithmetic  88.3 us (4%)
  blocking collectives  79.8 us (4%)
    reduce_scatter x4, waiting for transfers between devices, scatter_rows(): lax.psum_scatter(partial_rows(jnp.int32(0), row_count * lax.axis_size('mp...  439 us
    reduce_scatter x4, waiting for transfers between devices, scatter_grads(): lax.psum_scatter(partial_rows(jnp.int32(0), row_count * lax.axis_size('mp...  433 us
    all_gather x4, waiting for transfers between devices, gather_grads(): return lax.all_gather(values.astype(jnp.bfloat16), 'mp', axis=0, tiled=True)  207 us
    all_gather x4, waiting for transfers between devices, gather_rows(): return lax.all_gather(values.astype(jnp.bfloat16), 'mp', axis=0, tiled=True)  171 us
    psum x1, waiting for transfers between devices, shards(): lax.psum((jnp.stack(norm_grads), embed_local), ('dp', 'mp'))  121 us
    reduce_scatter x2, waiting for transfers between devices, shards(): lax.psum_scatter(qkv_grad, 'dp', scatter_dimension=0, tiled=True)  69 us
    reduce_scatter x2, waiting for transfers between devices, shards(): lax.psum_scatter(out_grad, 'dp', scatter_dimension=1, tiled=True)  65.8 us
    reduce_scatter x2, waiting for transfers between devices, shards(): lax.psum_scatter(up_grad, 'dp', scatter_dimension=0, tiled=True)  48.8 us
  transfers between devices with their start and end apart: 25, of which 23 were waited for; matrix products, arithmetic and copies ran while one was open for 9% of the time, Pallas kernels for 0%

commit v1 on v0

v1 whole, which is shorter than its diff:
```python
import functools
import math

import jax
import jax.numpy as jnp
from jax import lax
from jax.experimental import pallas as pl
from jax.experimental.pallas import tpu as pltpu
from jax.sharding import PartitionSpec as P

HEAD_DIM = 64
FF = 2048
VOCAB = 27
LAYERS = 2
LEN = 1024
STEP = 10
D = 512
PAIR = 2 * HEAD_DIM
CH = 256
SLOT = LEN // CH

bf16 = jnp.bfloat16
f32 = jnp.float32
highest = lax.Precision.HIGHEST
eps_norm = 1e-05
beta_one = 0.5
beta_two = 0.5
adam_eps = 1e-08
decay_matrix = 0.01
vector_rate = 0.6
embed_rate = 1.0
LOG2E = math.log2(math.e)
LN2 = math.log(2.0)
ALL = ("dp", "mp")

NN = (((1,), (0,)), ((), ()))
NT = (((1,), (1,)), ((), ()))


def mm(left, right, dims=NN):
    return lax.dot_general(left, right, dims, preferred_element_type=f32)


def vmem():
    return pl.BlockSpec(memory_space=pltpu.VMEM)


def smem():
    return pl.BlockSpec(memory_space=pltpu.SMEM)


def hbm():
    return pl.BlockSpec(memory_space=pl.ANY)


def after_operands(kernel, prefetched, count):
    def call(*refs):
        return kernel(*refs[:prefetched], *refs[prefetched + count :])

    return call


def params(mib):
    return pltpu.CompilerParams(
        dimension_semantics=("arbitrary",), vmem_limit_bytes=mib * 1024 * 1024
    )


def norm_parts(values):
    row_mean = jnp.mean(values, axis=-1, keepdims=True)
    centered = values - row_mean
    variance = jnp.mean(centered * centered, axis=-1, keepdims=True)
    inverse = lax.rsqrt(variance + eps_norm)
    return centered * inverse, inverse


def layer_norm(values, gain_vec, shift_vec):
    scaled, _ = norm_parts(values)
    return scaled * gain_vec + shift_vec


def norm_backward(grad_out, values, gain_vec):
    scaled, inverse = norm_parts(values)
    weighted = grad_out * gain_vec
    mean_plain = jnp.mean(weighted, axis=-1, keepdims=True)
    mean_scaled = jnp.mean(weighted * scaled, axis=-1, keepdims=True)
    grad_in = (weighted - mean_plain - scaled * mean_scaled) * inverse
    gain_grad = jnp.sum(grad_out * scaled, axis=0, keepdims=True)
    shift_grad = jnp.sum(grad_out, axis=0, keepdims=True)
    return grad_in, gain_grad, shift_grad


def gelu_pair(hidden):
    square = hidden * hidden
    bell = jnp.exp2(square * (-0.5 * LOG2E))
    ratio = 1.0 / (1.0 + (0.3275911 / math.sqrt(2.0)) * jnp.abs(hidden))
    poly = ratio * (
        0.5 * 0.254829592
        + ratio
        * (
            0.5 * -0.284496736
            + ratio * (0.5 * 1.421413741 + ratio * (0.5 * -1.453152027 + ratio * (0.5 * 1.061405429)))
        )
    )
    tail = poly * bell
    phi = jnp.where(hidden < 0.0, tail, 1.0 - tail)
    return hidden * phi, phi + hidden * bell * (1.0 / math.sqrt(2.0 * math.pi))


def time_features(step_values):
    half_width = D // 2
    frequency = jnp.exp(-math.log(10000.0) * jnp.arange(half_width, dtype=f32) / half_width)
    angles = step_values.astype(f32)[:, None] * frequency[None, :]
    return jnp.concatenate([jnp.sin(angles), jnp.cos(angles)], axis=1)


def adamw(weight, mean_old, square_old, gradient, step_rate, decay_weight):
    mean_new = beta_one * mean_old + (1.0 - beta_one) * gradient
    square_new = beta_two * square_old + (1.0 - beta_two) * gradient * gradient
    fix_one = 1.0 - beta_one**STEP
    fix_two = 1.0 - beta_two**STEP
    direction = mean_new / fix_one / (jnp.sqrt(square_new / fix_two) + adam_eps)
    return (weight - step_rate * (direction + decay_weight * weight), mean_new, square_new)


def permute_all(values, target):
    count = lax.axis_size("dp") * lax.axis_size("mp")
    return lax.ppermute(values, ALL, [(i, target(i)) for i in range(count)])


def block_places(my_dp):
    index = jnp.arange(32, dtype=jnp.int32)
    apart = (index >> 2) ^ my_dp
    place = ((apart & 1) << 4) | ((apart >> 1) << 2) | (index & 3)
    owner = my_dp ^ ((((index >> 2) & 3) << 1) | (index >> 4))
    return place, owner


def tie(values, after):
    return lax.optimization_barrier((values, after))


def flip(values, bits):
    return permute_all(values, lambda i: i ^ bits)


def gather_z(values):
    return jnp.stack([values] + [flip(values, bits) for bits in (1, 2, 3)])


def scatter_core(blocks):
    half = blocks.shape[0] // 2
    arrived = flip(blocks[half:], 4)
    return (blocks[:half].astype(f32) + arrived.astype(f32)).astype(bf16)


def scatter_four(blocks, unit):
    size = blocks.shape[0] // 4
    found = [flip(blocks[i * size : (i + 1) * size], i * unit) for i in (1, 2, 3)]
    return blocks[:size], found


def add_four(own, found, last):
    one, two, three = [part.astype(f32) for part in found]
    total = (own.astype(f32) + one) + (two + three)
    return total[0] if last else total.astype(bf16)


def gather_dp(held):
    return lax.all_gather(held, "dp", axis=0, tiled=False)


def scatter_dp(blocks, dp):
    places, rows, columns = blocks.shape
    flat = blocks.reshape(places * rows, columns)
    return lax.psum_scatter(flat, "dp", scatter_dimension=0, tiled=True).reshape(
        places // dp, rows, columns
    )


def plain_gather(values):
    dp, mp = lax.axis_size("dp"), lax.axis_size("mp")
    rows, columns = values.shape
    found = lax.all_gather(values, ALL, axis=0, tiled=True).reshape(dp, mp, rows, columns)
    if rows % 16 == 0:
        return found
    return jnp.swapaxes(found, 0, 1).reshape(1, mp, dp * rows, columns)


def plain_scatter(blocks, dp):
    places, rows, columns = blocks.shape
    mp = lax.axis_size("mp")
    if places != dp * mp:
        blocks = jnp.swapaxes(blocks.reshape(mp, dp, D // dp, columns), 0, 1)
    flat = blocks.reshape(dp * mp * (D // dp), columns)
    return lax.psum_scatter(flat, ALL, scatter_dimension=0, tiled=True).astype(f32)


def shift_right(values):
    count = lax.axis_size("mp")
    return lax.ppermute(values, "mp", [(i, i + 1) for i in range(count - 1)])


def shift_left(values):
    count = lax.axis_size("mp")
    return lax.ppermute(values, "mp", [(i + 1, i) for i in range(count - 1)])


def sum_four(values, unit):
    one, two, three = [flip(values, i * unit) for i in (1, 2, 3)]
    return (values + one) + (two + three)


def fetch_blocks(table, near, far, targets, sems):
    copies = []
    for place in range(32):
        owner = table[place]
        source = near.at[place] if place < 16 else far.at[place - 16]
        for index, (target, begin, width) in enumerate(targets):
            copies.append(
                pltpu.make_async_copy(
                    source.at[:, pl.ds(begin, width)],
                    target.at[owner, place % 4],
                    sems.at[place, index],
                )
            )
    for copy in copies:
        copy.start()
    return copies


def attn_forward_kernel(gathered, groups, meta, table, *refs):
    if gathered:
        near, far, left, own, right, resid, norm = refs[:7]
        middle, normed, q_o, k_o, v_o, o_o, lse_o, w_o = refs[7:15]
        ext, total, sems = refs[15:]
    else:
        w_in, left, own, right, resid, norm = refs[:6]
        middle, normed, q_o, k_o, v_o, o_o, lse_o = refs[6:13]
        ext, total = refs[13:]
    step = pl.program_id(0)

    @pl.when(step == 0)
    def _():
        if gathered:
            copies = fetch_blocks(table, near, far, [(w_o, 0, D)], sems)
        for index, part in enumerate((left, own, right)):
            ext[pl.ds(3 * index, 3)] = part[...].reshape(3, CH, D)
        total[...] = jnp.zeros_like(total)
        if gathered:
            for copy in copies:
                copy.wait()

    def weight(begin, end):
        found = w_o[:, step, :, begin:end] if gathered else w_in[:, 0, :, begin:end]
        return found.reshape(D, end - begin)

    for j in range(3):
        q_o[0, j] = (mm(ext[3 + j], weight(0, PAIR)) * (LOG2E / math.sqrt(HEAD_DIM))).astype(bf16)

    def project(slot, carry):
        begin = meta[slot]
        kv_w = weight(PAIR, 3 * PAIR)
        for i in range(SLOT):
            both = mm(ext[begin + i], kv_w).astype(bf16)
            k_o[0, slot * SLOT + i] = both[:, :PAIR]
            v_o[0, slot * SLOT + i] = both[:, PAIR:]
        return carry

    lax.fori_loop(0, meta[2], project, 0)
    lane = lax.broadcasted_iota(jnp.int32, (CH, PAIR), 1)

    for j in range(3):
        slot = meta[3 + j]
        query = q_o[0, j]
        keys = k_o[0, pl.ds(slot * SLOT, SLOT)].reshape(LEN, PAIR)
        values = v_o[0, pl.ds(slot * SLOT, SLOT)].reshape(LEN, PAIR)
        parts = []
        for h in range(2):
            q_h = jnp.where((lane // HEAD_DIM) == h, query, jnp.zeros_like(query))
            scores = mm(q_h, keys, NT)
            top = jnp.max(scores, axis=1, keepdims=True)
            weights = jnp.exp2(scores - top)
            denominator = jnp.sum(weights, axis=1, keepdims=True)
            mixed = mm(weights.astype(bf16), values)
            parts.append(mixed * (1.0 / denominator))
            spread = jnp.broadcast_to(top + jnp.log2(denominator), (CH, PAIR))
            lse_o[0, j, h : h + 1] = spread.T[0:1]
        out = jnp.where((lane // HEAD_DIM) == 0, parts[0], parts[1]).astype(bf16)
        o_o[0, j] = out
        total[j] += mm(out, weight(3 * PAIR, D), NT)

    @pl.when(step == groups - 1)
    def _():
        for j in range(3):
            rows = pl.ds(j * CH, CH)
            values = resid[rows] + total[j]
            middle[rows] = values
            normed[rows] = layer_norm(values, norm[2:3], norm[3:4]).astype(bf16)


def attn_forward(weights, meta, table, left, own, right, resid, norm, groups):
    rows = own.shape[0]
    gathered = isinstance(weights, tuple)
    const = lambda s, *_: (0, 0)
    pair = lambda s, *_: (s, 0, 0, 0)
    full = pl.BlockSpec((rows, D), const)
    out_shape = [
        jax.ShapeDtypeStruct((rows, D), f32),
        jax.ShapeDtypeStruct((rows, D), bf16),
        jax.ShapeDtypeStruct((groups, 3, CH, PAIR), bf16),
        jax.ShapeDtypeStruct((groups, 2 * SLOT, CH, PAIR), bf16),
        jax.ShapeDtypeStruct((groups, 2 * SLOT, CH, PAIR), bf16),
        jax.ShapeDtypeStruct((groups, 3, CH, PAIR), bf16),
        jax.ShapeDtypeStruct((groups, 3, 8, CH), f32),
    ]
    out_specs = [
        full,
        full,
        pl.BlockSpec((1, 3, CH, PAIR), pair),
        pl.BlockSpec((1, 2 * SLOT, CH, PAIR), pair),
        pl.BlockSpec((1, 2 * SLOT, CH, PAIR), pair),
        pl.BlockSpec((1, 3, CH, PAIR), pair),
        pl.BlockSpec((1, 3, 8, CH), pair),
    ]
    scratch = [
        pltpu.VMEM((9, CH, D), bf16),
        pltpu.VMEM((3, CH, D), f32),
    ]
    if gathered:
        w_args = list(weights)
        w_specs = [hbm(), hbm()]
        out_shape.append(jax.ShapeDtypeStruct((8, 4, 64, D), bf16))
        out_specs.append(pl.BlockSpec((8, 4, 64, D), pair_zero))
        scratch.append(pltpu.SemaphoreType.DMA((32, 1)))
    else:
        w_args = [weights]
        split, _, high, _ = weights.shape
        w_specs = [pl.BlockSpec((split, 1, high, D), lambda s, *_: (0, s, 0, 0))]
    outs = pl.pallas_call(
        functools.partial(attn_forward_kernel, gathered, groups),
        grid_spec=pltpu.PrefetchScalarGridSpec(
            num_scalar_prefetch=2,
            grid=(groups,),
            in_specs=w_specs
            + [full, full, full, full, pl.BlockSpec((4, D), const)],
            out_specs=out_specs,
            scratch_shapes=scratch,
        ),
        out_shape=out_shape,
        compiler_params=params(56),
        cost_estimate=pl.CostEstimate(
            flops=29_000_000_000, bytes_accessed=14_000_000, transcendentals=0
        ),
        name="attn_forward",
    )(meta, table, *w_args, left, own, right, resid, norm)
    if gathered:
        return outs[:7], outs[7]
    return outs, weights


def pair_zero(s, *_):
    return (0, 0, 0, 0)


def mlp_forward_kernel(gathered, last, groups, table, *refs):
    if gathered:
        near, far, normed, middle, norm = refs[:5]
        refs = refs[5:]
    else:
        up_in, down_in, normed, middle, norm = refs[:5]
        refs = refs[5:]
    after, act_o, slope_o = refs[:3]
    refs = refs[3:]
    if not last:
        next_o = refs[0]
        refs = refs[1:]
    if gathered:
        up_o, down_o, total, sems = refs
    else:
        (total,) = refs
    step = pl.program_id(0)

    @pl.when(step == 0)
    def _():
        if gathered:
            copies = fetch_blocks(table, near, far, [(up_o, 0, D), (down_o, D, D)], sems)
        total[...] = jnp.zeros_like(total)
        if gathered:
            for copy in copies:
                copy.wait()

    if gathered:
        up_w = up_o[:, step].reshape(D, D)
        down_w = down_o[:, step].reshape(D, D)
    else:
        up_w = up_in[:, 0].reshape(D, D)
        down_w = down_in[:, 0].reshape(D, D)
    for j in range(3):
        rows = pl.ds(j * CH, CH)
        hidden = mm(normed[rows], up_w)
        act, slope = gelu_pair(hidden)
        act = act.astype(bf16)
        act_o[0, rows] = act
        slope_o[0, rows] = slope.astype(bf16)
        total[j] += mm(act, down_w, NT)

    @pl.when(step == groups - 1)
    def _():
        for j in range(3):
            rows = pl.ds(j * CH, CH)
            values = middle[rows] + total[j]
            after[rows] = values
            if not last:
                next_o[rows] = layer_norm(values, norm[0:1], norm[1:2]).astype(bf16)


def mlp_forward(weights, table, normed, middle, norm, groups, last):
    rows = normed.shape[0]
    gathered = not isinstance(weights[0], tuple)
    const = lambda s, *_: (0, 0)
    full = pl.BlockSpec((rows, D), const)
    part = pl.BlockSpec((1, rows, D), lambda s, *_: (s, 0, 0))
    out_shape = [
        jax.ShapeDtypeStruct((rows, D), f32),
        jax.ShapeDtypeStruct((groups, rows, D), bf16),
        jax.ShapeDtypeStruct((groups, rows, D), bf16),
    ]
    out_specs = [full, part, part]
    if not last:
        out_shape.append(jax.ShapeDtypeStruct((rows, D), bf16))
        out_specs.append(full)
    scratch = [pltpu.VMEM((3, CH, D), f32)]
    if gathered:
        w_args = list(weights)
        w_specs = [hbm(), hbm()]
        for _ in range(2):
            out_shape.append(jax.ShapeDtypeStruct((8, 4, 64, D), bf16))
            out_specs.append(pl.BlockSpec((8, 4, 64, D), pair_zero))
        scratch.append(pltpu.SemaphoreType.DMA((32, 2)))
    else:
        (up_w, up_at), (down_w, down_at) = weights
        w_args = [up_w, down_w]
        w_specs = [weight_spec(up_w, up_at), weight_spec(down_w, down_at)]
    outs = pl.pallas_call(
        functools.partial(mlp_forward_kernel, gathered, last, groups),
        grid_spec=pltpu.PrefetchScalarGridSpec(
            num_scalar_prefetch=1,
            grid=(groups,),
            in_specs=w_specs + [full, full, pl.BlockSpec((4, D), const)],
            out_specs=out_specs,
            scratch_shapes=scratch,
        ),
        out_shape=out_shape,
        compiler_params=params(56),
        cost_estimate=pl.CostEstimate(
            flops=15_000_000_000, bytes_accessed=18_000_000, transcendentals=0
        ),
        name="mlp_forward",
    )(table, *w_args, normed, middle, norm)
    if gathered:
        return outs[:-2], ((outs[-2], 0), (outs[-1], 0))
    return outs, weights


def weight_spec(weight, at):
    split, _, high, _ = weight.shape
    return pl.BlockSpec((split, 1, high, D), lambda s, *_: (0, s, 0, at))


def put_blocks(out, table, step, groups, split, begin, values):
    high = D // split
    width = values.shape[1]
    for d in range(split):
        place = table[d * groups + step]
        out[place, :, begin : begin + width] = values[d * high : (d + 1) * high]


def mlp_backward_kernel(first, groups, split, meta, place, *refs):
    if first:
        scale, cot = refs[:2]
        refs = refs[2:]
    else:
        grad_in, d_own, d_left, d_right, source, norm_up = refs[:6]
        refs = refs[6:]
    up_in, down_in, act, slope, normed, middle, norm = refs[:7]
    refs = refs[7:]
    w_grad, grad_out, n_grad = refs[:3]
    refs = refs[3:]
    grad, low, low_t, norm_t, total = refs
    step = pl.program_id(0)

    @pl.when(step == 0)
    def _():
        n_grad[...] = jnp.zeros_like(n_grad)
        for j in range(3):
            rows = pl.ds(j * CH, CH)
            if first:
                values = cot[rows].astype(f32) * scale[meta[6 + j]]
            else:
                arrived = d_own[rows] + d_left[rows].astype(f32) + d_right[rows].astype(f32)
                back, gain_grad, shift_grad = norm_backward(arrived, source[rows], norm_up[0:1])
                values = grad_in[rows] + back
                n_grad[0:1] += gain_grad
                n_grad[1:2] += shift_grad
            grad[j] = values
            rounded = values.astype(bf16)
            low[rows] = rounded
            low_t[:, j * CH : (j + 1) * CH] = rounded.T
            norm_t[:, j * CH : (j + 1) * CH] = normed[rows].T
        total[...] = jnp.zeros_like(total)

    up_w = up_in[:, 0].reshape(D, D)
    down_w = down_in[:, 0].reshape(D, D)
    down_grad = mm(low_t[...], act[0]).astype(bf16)
    put_blocks(w_grad, place, step, groups, split, D, down_grad)
    pieces = []
    for j in range(3):
        rows = pl.ds(j * CH, CH)
        piece = (mm(low[rows], down_w) * slope[0, rows].astype(f32)).astype(bf16)
        pieces.append(piece)
        total[j] += mm(piece, up_w, NT)
    up_grad = mm(norm_t[...], jnp.concatenate(pieces, axis=0)).astype(bf16)
    put_blocks(w_grad, place, step, groups, split, 0, up_grad)

    @pl.when(step == groups - 1)
    def _():
        for j in range(3):
            rows = pl.ds(j * CH, CH)
            back, gain_grad, shift_grad = norm_backward(total[j], middle[rows], norm[2:3])
            grad_out[rows] = grad[j] + back
            n_grad[2:3] += gain_grad
            n_grad[3:4] += shift_grad


def mlp_backward(
    weights, meta, place, begin, act, slope, normed, middle, norm, groups, split, after=()
):
    rows = normed.shape[0]
    first = len(begin) == 2
    const = lambda s, *_: (0, 0)
    full = pl.BlockSpec((rows, D), const)
    part = pl.BlockSpec((1, rows, D), lambda s, *_: (s, 0, 0))
    vec = pl.BlockSpec((4, D), const)
    (up_w, up_at), (down_w, down_at) = weights
    begin_specs = [smem(), full] if first else [full] * 5 + [vec]
    places = split * groups
    return pl.pallas_call(
        after_operands(
            functools.partial(mlp_backward_kernel, first, groups, split), 2, len(after)
        ),
        grid_spec=pltpu.PrefetchScalarGridSpec(
            num_scalar_prefetch=2,
            grid=(groups,),
            in_specs=[hbm()] * len(after)
            + begin_specs
            + [weight_spec(up_w, up_at), weight_spec(down_w, down_at)]
            + [part, part, full, full, vec],
            out_specs=[
                pl.BlockSpec((places, D // split, 2 * D), lambda s, *_: (0, 0, 0)),
                full,
                pl.BlockSpec((8, D), const),
            ],
            scratch_shapes=[
                pltpu.VMEM((3, CH, D), f32),
                pltpu.VMEM((rows, D), bf16),
                pltpu.VMEM((D, rows), bf16),
                pltpu.VMEM((D, rows), bf16),
                pltpu.VMEM((3, CH, D), f32),
            ],
        ),
        out_shape=[
            jax.ShapeDtypeStruct((places, D // split, 2 * D), bf16),
            jax.ShapeDtypeStruct((rows, D), f32),
            jax.ShapeDtypeStruct((8, D), f32),
        ],
        compiler_params=params(56),
        cost_estimate=pl.CostEstimate(
            flops=20_000_000_000, bytes_accessed=20_000_000, transcendentals=0
        ),
        name="mlp_backward",
    )(meta, place, *after, *begin, up_w, down_w, act, slope, normed, middle, norm)


def attn_backward_kernel(groups, split, meta, place, *refs):
    w_in, left, own, right, grad_in, small, q_i, k_i, v_i, o_i, lse_i = refs[:11]
    w_grad, d_left, d_own, d_right, small_o = refs[11:16]
    ext, ext_t, low, low_t, k_t, dk, dv, d_ext, dq_all = refs[16:]
    step = pl.program_id(0)

    @pl.when(step == 0)
    def _():
        for index, part in enumerate((left, own, right)):
            for j in range(3):
                values = part[pl.ds(j * CH, CH)]
                ext[3 * index + j] = values
                ext_t[3 * index + j] = values.T
        for j in range(3):
            rounded = grad_in[pl.ds(j * CH, CH)].astype(bf16)
            low[j] = rounded
            low_t[:, j * CH : (j + 1) * CH] = rounded.T
        d_ext[...] = jnp.zeros_like(d_ext)
        small_o[...] = small[...]

    def weight(begin, end):
        return w_in[:, 0, :, begin:end].reshape(D, end - begin)

    slots = meta[2]

    def prepare(slot, carry):
        for i in range(SLOT):
            k_t[slot, :, i * CH : (i + 1) * CH] = k_i[0, slot * SLOT + i].T
        dk[slot] = jnp.zeros((LEN, PAIR), f32)
        dv[slot] = jnp.zeros((LEN, PAIR), f32)
        return carry

    lax.fori_loop(0, slots, prepare, 0)
    lane = lax.broadcasted_iota(jnp.int32, (CH, PAIR), 1)

    def chunk(j, carry):
        slot = meta[3 + j]
        query = q_i[0, j]
        out = o_i[0, j]
        keys = k_i[0, pl.ds(slot * SLOT, SLOT)].reshape(LEN, PAIR)
        values = v_i[0, pl.ds(slot * SLOT, SLOT)].reshape(LEN, PAIR)
        grad_out = mm(low[j], weight(3 * PAIR, D))
        grad_low = grad_out.astype(bf16)
        product = (grad_low.astype(f32) * out.astype(f32)).T
        delta = jnp.sum(product.reshape(2, HEAD_DIM, CH), axis=1)
        p_all = []
        ds_all = []
        q_all = []
        g_all = []
        dq_t = []
        for h in range(2):
            q_h = jnp.where((lane // HEAD_DIM) == h, query, jnp.zeros_like(query))
            g_h = jnp.where((lane // HEAD_DIM) == h, grad_low, jnp.zeros_like(grad_low))
            probability = jnp.exp2(mm(keys, q_h, NT) - lse_i[0, j, h : h + 1])
            grad_p = mm(values, g_h, NT)
            grad_s = (probability * (grad_p - delta[h : h + 1])).astype(bf16)
            dq_t.append(mm(k_t[slot, h * HEAD_DIM : (h + 1) * HEAD_DIM, :], grad_s))
            dv[slot] += mm(probability.astype(bf16), g_h)
            dk[slot] += mm(grad_s, q_h)
        dq = jnp.concatenate(dq_t, axis=0).T * (1.0 / math.sqrt(HEAD_DIM))
        dq_low = dq.astype(bf16)
        dq_all[pl.ds(j * CH, CH)] = dq_low
        d_ext[3 + j] += mm(dq_low, weight(0, PAIR), NT)
        return carry

    lax.fori_loop(0, 3, chunk, 0)
    out_grad = mm(low_t[...], o_i[0].reshape(3 * CH, PAIR)).astype(bf16)
    put_blocks(w_grad, place, step, groups, split, 3 * PAIR, out_grad)
    own_t = jnp.concatenate([ext_t[3], ext_t[4], ext_t[5]], axis=1)
    q_grad = mm(own_t, dq_all[...]).astype(bf16)
    put_blocks(w_grad, place, step, groups, split, 0, q_grad)

    def collect(slot, running):
        begin = meta[slot]
        kv_w = weight(PAIR, 3 * PAIR)
        for i in range(SLOT):
            rows = pl.ds(i * CH, CH)
            both = jnp.concatenate(
                [(dk[slot, rows] * LN2).astype(bf16), dv[slot, rows].astype(bf16)], axis=1
            )
            d_ext[begin + i] += mm(both, kv_w, NT)
            running = running + mm(ext_t[begin + i], both)
        return running

    kv_grad = lax.fori_loop(0, slots, collect, jnp.zeros((D, 2 * PAIR), f32))
    put_blocks(w_grad, place, step, groups, split, PAIR, kv_grad.astype(bf16))

    @pl.when(step == groups - 1)
    def _():
        for j in range(3):
            rows = pl.ds(j * CH, CH)
            d_left[rows] = d_ext[j].astype(bf16)
            d_own[rows] = d_ext[3 + j]
            d_right[rows] = d_ext[6 + j].astype(bf16)


def attn_backward(
    weight, meta, place, left, own, right, grad_in, kept, groups, split, small, after=()
):
    rows = own.shape[0]
    q_i, k_i, v_i, o_i, lse_i = kept
    const = lambda s, *_: (0, 0)
    pair = lambda s, *_: (s, 0, 0, 0)
    full = pl.BlockSpec((rows, D), const)
    places = split * groups
    return pl.pallas_call(
        after_operands(
            functools.partial(attn_backward_kernel, groups, split), 2, len(after)
        ),
        grid_spec=pltpu.PrefetchScalarGridSpec(
            num_scalar_prefetch=2,
            grid=(groups,),
            in_specs=[hbm()] * len(after)
            + [
                weight_spec(*weight),
                full,
                full,
                full,
                full,
                pl.BlockSpec((8, D), const),
                pl.BlockSpec((1, 3, CH, PAIR), pair),
                pl.BlockSpec((1, 2 * SLOT, CH, PAIR), pair),
                pl.BlockSpec((1, 2 * SLOT, CH, PAIR), pair),
                pl.BlockSpec((1, 3, CH, PAIR), pair),
                pl.BlockSpec((1, 3, 8, CH), pair),
            ],
            out_specs=[
                pl.BlockSpec((places, D // split, D), lambda s, *_: (0, 0, 0)),
                full,
                full,
                full,
                pl.BlockSpec((8, D), const),
            ],
            scratch_shapes=[
                pltpu.VMEM((9, CH, D), bf16),
                pltpu.VMEM((9, D, CH), bf16),
                pltpu.VMEM((3, CH, D), bf16),
                pltpu.VMEM((D, rows), bf16),
                pltpu.VMEM((2, PAIR, LEN), bf16),
                pltpu.VMEM((2, LEN, PAIR), f32),
                pltpu.VMEM((2, LEN, PAIR), f32),
                pltpu.VMEM((9, CH, D), f32),
                pltpu.VMEM((rows, PAIR), bf16),
            ],
        ),
        out_shape=[
            jax.ShapeDtypeStruct((places, D // split, D), bf16),
            jax.ShapeDtypeStruct((rows, D), bf16),
            jax.ShapeDtypeStruct((rows, D), f32),
            jax.ShapeDtypeStruct((rows, D), bf16),
            jax.ShapeDtypeStruct((8, D), f32),
        ],
        compiler_params=params(58),
        cost_estimate=pl.CostEstimate(
            flops=45_000_000_000, bytes_accessed=24_000_000, transcendentals=0
        ),
        name="attn_backward",
    )(meta, place, *after, weight[0], left, own, right, grad_in, small, q_i, k_i, v_i, o_i, lse_i)


def entry_backward_kernel(grad_in, d_own, d_left, d_right, source, norm, ids, grad_out, small):
    small[...] = jnp.zeros_like(small)
    for j in range(3):
        rows = pl.ds(j * CH, CH)
        arrived = d_own[rows] + d_left[rows].astype(f32) + d_right[rows].astype(f32)
        back, gain_grad, shift_grad = norm_backward(arrived, source[rows], norm[0:1])
        values = grad_in[rows] + back
        grad_out[rows] = values
        small[0:1] += gain_grad
        small[1:2] += shift_grad
        letter = lax.broadcasted_iota(jnp.int32, (32, CH), 0)
        chosen = (letter == ids[:, j * CH : (j + 1) * CH]).astype(bf16)
        high = values.astype(bf16)
        rest = values - high.astype(f32)
        middle = rest.astype(bf16)
        low = (rest - middle.astype(f32)).astype(bf16)
        small[8:40] += mm(chosen, high) + mm(chosen, middle) + mm(chosen, low)


def entry_backward(grad_in, d_own, d_left, d_right, source, norm, ids, after=()):
    rows = grad_in.shape[0]
    return pl.pallas_call(
        after_operands(entry_backward_kernel, 0, len(after)),
        in_specs=[hbm()] * len(after) + [vmem()] * 7,
        out_specs=[vmem()] * 2,
        out_shape=[
            jax.ShapeDtypeStruct((rows, D), f32),
            jax.ShapeDtypeStruct((40, D), f32),
        ],
        compiler_params=pltpu.CompilerParams(vmem_limit_bytes=40 * 1024 * 1024),
        cost_estimate=pl.CostEstimate(
            flops=100_000_000, bytes_accessed=9_000_000, transcendentals=0
        ),
        name="entry_backward",
    )(*after, grad_in, d_own, d_left, d_right, source, norm, ids)


def shards(
    token_ids,
    timesteps,
    importance,
    cotangent,
    qkv_weight,
    out_weight,
    up_weight,
    down_weight,
    norm_params,
    embed_table,
    qkv_first,
    qkv_second,
    out_first,
    out_second,
    up_first,
    up_second,
    down_first,
    down_second,
    norm_first,
    norm_second,
    embed_first,
    embed_second,
):
    dp, mp = lax.axis_size("dp"), lax.axis_size("mp")
    small = dp == 8 and mp == 4
    groups = mp
    split = dp if small else 1
    row_count = token_ids.shape[0]
    seq_here = timesteps.shape[0]
    high = D // dp
    my_mp = lax.axis_index("mp")
    my_dp = lax.axis_index("dp")
    row_start = my_mp * row_count

    first_seq = row_start // LEN
    last_seq = (row_start + row_count - 1) // LEN
    chunk_seq = [(row_start + CH * j) // LEN for j in range(3)]
    meta = jnp.stack(
        [
            3 + (first_seq * LEN - row_start) // CH,
            3 + (last_seq * LEN - row_start) // CH,
            last_seq - first_seq + 1,
        ]
        + [seq - first_seq for seq in chunk_seq]
        + chunk_seq
    ).astype(jnp.int32)
    in_order = jnp.arange(split * groups, dtype=jnp.int32)
    if small:
        place, owner = block_places(my_dp)
    else:
        place = owner = in_order

    attn_mine = []
    mlp_mine = []
    for layer in range(LAYERS):
        attn_mine.append(
            jnp.concatenate(
                [qkv_weight[layer].reshape(high, -1), out_weight[layer].T], axis=1
            ).astype(bf16)
        )
        mlp_mine.append(
            jnp.concatenate([up_weight[layer], down_weight[layer].T], axis=1).astype(bf16)
        )
    both_mine = jnp.concatenate([attn_mine[1], mlp_mine[1]], axis=1)
    ids_left, ids_right = shift_right(token_ids), shift_left(token_ids)
    if small:
        attn_sent = [flip(attn_mine[0], bits) for bits in (1, 2, 3)]
        attn_sent, (ids_left, ids_right) = tie(attn_sent, (ids_left, ids_right))
        attn_z = jnp.stack([attn_mine[0]] + list(attn_sent))
    ids_ext = jnp.concatenate([ids_left, token_ids, ids_right])
    seq_ext = (row_start - row_count + jnp.arange(3 * row_count, dtype=jnp.int32)) // LEN
    letters = (ids_ext[:, None] == jnp.arange(VOCAB, dtype=jnp.int32)[None, :]).astype(f32)
    member = (seq_ext[:, None] == jnp.arange(seq_here, dtype=jnp.int32)[None, :]).astype(f32)
    entry_ext = jnp.dot(letters, embed_table, precision=highest) + jnp.dot(
        member, time_features(timesteps), precision=highest
    )
    normed_ext = layer_norm(entry_ext, norm_params[0, 0], norm_params[0, 1]).astype(bf16)
    resid = entry_ext[row_count : 2 * row_count]
    ext = (
        normed_ext[:row_count],
        normed_ext[row_count : 2 * row_count],
        normed_ext[2 * row_count :],
    )

    if small:
        mlp_first, attn_z = tie(mlp_mine[0], attn_z)
        attn_sent = [flip(attn_z, bits) for bits in (8, 16, 24)]
        attn_sent, (ext, resid) = tie(attn_sent, (ext, resid))
        attn_xy = jnp.concatenate([attn_z] + list(attn_sent), axis=0)
        mlp_z = gather_z(mlp_first)
        mlp_z, attn_xy = tie(mlp_z, attn_xy)
        attn_w = [(attn_xy, flip(attn_xy, 4))]
        mlp_found = gather_dp(mlp_z)
        both_mine, mlp_z = tie(both_mine, mlp_z)
        both_sent = [flip(both_mine, bits) for bits in (1, 2, 3)]
    else:
        attn_w = [plain_gather(attn_mine[0])]
        mlp_found = plain_gather(mlp_mine[0])
        attn_w.append(plain_gather(both_mine))
        mlp_w = [((mlp_found, 0), (mlp_found, 1)), ((attn_w[1], 1), (attn_w[1], 2))]

    kept = []
    for layer in range(LAYERS):
        last = layer == LAYERS - 1
        outs, w_attn = attn_forward(
            attn_w[layer], meta, owner, *ext, resid, norm_params[layer], groups
        )
        middle, normed = outs[:2]
        if small and layer == 0:
            both_sent, normed = tie(both_sent, normed)
            both_found = gather_dp(jnp.stack([both_mine] + list(both_sent)))
            attn_w.append(both_found)
            mlp_w = [((mlp_found, 0), (mlp_found, 1)), ((both_found, 1), (both_found, 2))]
        next_norm = norm_params[min(layer + 1, LAYERS - 1)]
        mlp_outs, w_mlp = mlp_forward(
            mlp_w[layer], owner, normed, middle, next_norm, groups, last
        )
        kept.append((ext, resid, middle, normed, outs[2:], mlp_outs[1:3], (w_attn, 0), w_mlp))
        resid = mlp_outs[0]
        if not last:
            following = mlp_outs[3]
            ext = (shift_right(following), following, shift_left(following))
    activations = resid

    norm_grads = [[None] * 4 for _ in range(LAYERS)]
    attn_grads = [None] * LAYERS
    mlp_grads = [None] * LAYERS
    begin = (importance, cotangent)
    after = ()
    for layer in reversed(range(LAYERS)):
        ext, source, middle, normed, attn_kept, (act, slope), w_attn, w_mlp = kept[layer]
        mlp_grad, grad_mid, n_grad = mlp_backward(
            w_mlp,
            meta,
            in_order,
            begin,
            act,
            slope,
            normed,
            middle,
            norm_params[layer],
            groups,
            split,
            after,
        )
        after = ()
        if small:
            if layer + 1 < LAYERS:
                attn_found, (mlp_grad, grad_mid) = tie(attn_found, (mlp_grad, grad_mid))
            mlp_rows = scatter_dp(mlp_grad, dp)
            if layer + 1 < LAYERS:
                attn_rows = add_four(attn_mine_rows, attn_found, False)
                above = jnp.concatenate([attn_rows, above], axis=2)
                above_mine, above_found = scatter_four(above, 1)
                after = (above,)
        attn_grad, d_left, d_own, d_right, n_grad = attn_backward(
            w_attn, meta, place, *ext, grad_mid, attn_kept, groups, split, n_grad, after
        )
        if small and layer + 1 < LAYERS:
            above_found, (attn_grad, d_left, d_right) = tie(
                above_found, (attn_grad, d_left, d_right)
            )
        from_right = shift_left(d_left)
        from_left = shift_right(d_right)
        if small:
            attn_held = scatter_core(attn_grad)
            attn_mine_rows, attn_found = scatter_four(attn_held, 8)
            if layer + 1 < LAYERS:
                above_total = add_four(above_mine, above_found, True)
                attn_grads[1] = above_total[:, :D]
                mlp_grads[1] = above_total[:, D:]
            else:
                above = mlp_rows
            after = (attn_held,)
        else:
            mlp_grads[layer] = plain_scatter(mlp_grad, dp)
            attn_grads[layer] = plain_scatter(attn_grad, dp)
        norm_grads[layer][2:] = [n_grad[2], n_grad[3]]
        if layer + 1 < LAYERS:
            norm_grads[layer + 1][:2] = [n_grad[0], n_grad[1]]
        begin = (grad_mid, d_own, from_left, from_right, source, norm_params[layer])
    after = ()
    if small:
        attn_rows = add_four(attn_mine_rows, attn_found, False)
        below = jnp.concatenate([attn_rows, mlp_rows], axis=2)
        after = (below,)
        below_mine, below_found = scatter_four(below, 1)
    input_grad, reduced = entry_backward(*begin, token_ids[None, :], after)
    norm_grads[0][:2] = [reduced[0], reduced[1]]
    stacked = jnp.concatenate(
        [jnp.stack([row for rows in norm_grads for row in rows]), reduced[8:40]], axis=0
    )
    if small:
        stacked = sum_four(stacked + flip(stacked, 4), 8)
        below_found, stacked = tie(below_found, stacked)
        stacked = sum_four(stacked, 1)
        total = add_four(below_mine, below_found, True)
        attn_grads[0] = total[:, :D]
        mlp_grads[0] = total[:, D:]
    else:
        stacked = lax.psum(stacked, ALL)
    norm_grad = stacked[: 4 * LAYERS].reshape(LAYERS, 4, D)
    embed_grad = stacked[4 * LAYERS : 4 * LAYERS + VOCAB]

    qkv_grad = jnp.stack([g[:, : 3 * PAIR].reshape(high, 3, PAIR) for g in attn_grads])
    out_grad = jnp.stack([g[:, 3 * PAIR :].T for g in attn_grads])
    up_grad = jnp.stack([g[:, :D] for g in mlp_grads])
    down_grad = jnp.stack([g[:, D:].T for g in mlp_grads])
    qkv_master, qkv_mean, qkv_square = adamw(
        qkv_weight, qkv_first, qkv_second, qkv_grad, 2.0 / math.sqrt(D), decay_matrix
    )
    out_master, out_mean, out_square = adamw(
        out_weight, out_first, out_second, out_grad, 2.0 / math.sqrt(D), decay_matrix
    )
    up_master, up_mean, up_square = adamw(
        up_weight, up_first, up_second, up_grad, 2.0 / math.sqrt(D), decay_matrix
    )
    down_master, down_mean, down_square = adamw(
        down_weight, down_first, down_second, down_grad, 2.0 / math.sqrt(FF), decay_matrix
    )
    norm_master, norm_mean, norm_square = adamw(
        norm_params, norm_first, norm_second, norm_grad, vector_rate, 0.0
    )
    embed_master, embed_mean, embed_square = adamw(
        embed_table, embed_first, embed_second, embed_grad, embed_rate, 0.0
    )
    return (
        activations,
        input_grad,
        qkv_master,
        qkv_mean,
        qkv_square,
        qkv_master.astype(bf16),
        out_master,
        out_mean,
        out_square,
        out_master.astype(bf16),
        up_master,
        up_mean,
        up_square,
        up_master.astype(bf16),
        down_master,
        down_mean,
        down_square,
        down_master.astype(bf16),
        norm_master,
        norm_mean,
        norm_square,
        embed_master,
        embed_mean,
        embed_square,
    )


def solution(mesh):
    rows = P(("dp", "mp"), None)
    qkv = P(None, "dp", None, "mp")
    wide = P(None, "mp", "dp")
    tall = P(None, "dp", "mp")
    same = P()
    return jax.shard_map(
        shards,
        mesh=mesh,
        in_specs=(P(("dp", "mp")), P("dp"), P("dp"), rows, qkv, wide, tall, wide, same, same)
        + (qkv, qkv, wide, wide, tall, tall, wide, wide, same, same, same, same),
        out_specs=(rows, rows)
        + (qkv,) * 4
        + (wide,) * 4
        + (tall,) * 4
        + (wide,) * 4
        + (same,) * 6,
        check_vma=False,
    )
```

time: 2150 us -> 400 us (0.19)
  waiting for transfers between devices: 1560 us -> 78.7 us
  matrix products: 260 us -> 4.51 us
  Pallas kernels: 0 us -> 186 us
  local copies, waits for them, and re-layouts: 138 us -> 14.7 us
  blocking collectives: 79.8 us -> 0 us
  starting transfers between devices: 1.7 us -> 73.1 us
  other arithmetic: 88.3 us -> 21.6 us
    reduce_scatter x16 -> x2, waiting for transfers between devices: 1060 us -> 0.02 us  [scatter_dp(): lax.psum_scatter(flat, 'dp', scatter_dimension=0, tiled=True)]
    all_gather x8 -> x2, waiting for transfers between devices: 378 us -> 11.8 us  [gather_dp(): return lax.all_gather(held, 'dp', axis=0, tiled=False)]
    dot_general x58 -> x0, matrix products: 257 us -> none  [the longest x8 43.6 us: contract_last(): lax.dot_general(left_side, right_side, (((1,), (1,)), ((), ())), preferre...]
    pallas_call x0 -> x9, Pallas kernels: none -> 186 us  [the longest x2 72.2 us: attn_backward(): pl.pallas_call(after_operands(functools.partial(attn_backward_kernel, gro...]
    psum x1 -> x0, waiting for transfers between devices: 121 us -> none  [shards(): lax.psum((jnp.stack(norm_grads), embed_local), ('dp', 'mp'))]
    all_gather x8 -> x0, blocking collectives: 79.8 us -> none  [the longest x2 20.6 us: gather_weights(): lax.all_gather(qkv_weight[layer_index].astype(jnp.bfloat16), 'dp', axis=0...]
    ppermute x0 -> x42, starting transfers between devices: none -> 72.7 us  [the longest x34 44.8 us: permute_all(): return lax.ppermute(values, ALL, [(i, target(i)) for i in range(count)])]
    ppermute x0 -> x42, waiting for transfers between devices: none -> 66.8 us  [the longest x34 28.6 us: permute_all(): return lax.ppermute(values, ALL, [(i, target(i)) for i in range(count)])]
  transfers between devices with their start and end apart: 25 -> 46, of which waited for: 23 -> 14; matrix products, arithmetic and copies ran while one was open for 9% -> 9% of each run, Pallas kernels for 0% -> 33%
where the time goes in v1:
time: 400 us; the launch traced here: 393 us
  Pallas kernels  186 us (46%)
  waiting for transfers between devices  78.7 us (20%)
  starting transfers between devices  73.1 us (18%)
  other arithmetic  21.6 us (5%)
  between operations  15.1 us (4%)
  local copies, waits for them, and re-layouts  14.7 us (4%)
  matrix products  4.51 us (1%)
    pallas_call x2, Pallas kernels, attn_backward(): pl.pallas_call(after_operands(functools.partial(attn_backward_kernel, gro...  72.2 us
    pallas_call x2, Pallas kernels, attn_forward(): pl.pallas_call(functools.partial(attn_forward_kernel, gathered, groups),...  47.8 us
    ppermute x34, starting transfers between devices, permute_all(): return lax.ppermute(values, ALL, [(i, target(i)) for i in range(count)])  44.8 us
    pallas_call x2, Pallas kernels, mlp_backward(): pl.pallas_call(after_operands(functools.partial(mlp_backward_kernel, firs...  34.6 us
    ppermute x34, waiting for transfers between devices, permute_all(): return lax.ppermute(values, ALL, [(i, target(i)) for i in range(count)])  28.6 us
    ppermute x4, waiting for transfers between devices, shift_right(): return lax.ppermute(values, 'mp', [(i, i + 1) for i in range(count - 1)])  27.2 us
    pallas_call x2, Pallas kernels, mlp_forward(): pl.pallas_call(functools.partial(mlp_forward_kernel, gathered, last, grou...  27.1 us
    ppermute x4, starting transfers between devices, shift_right(): return lax.ppermute(values, 'mp', [(i, i + 1) for i in range(count - 1)])  22 us
  transfers between devices with their start and end apart: 46, of which 14 were waited for; matrix products, arithmetic and copies ran while one was open for 9% of the time, Pallas kernels for 33%

profile of v1, /device:TPU:0, one launch (start us, length us, event | category | flops | bytes accessed | tf_op | source)
XLA Modules:
  0.0 393.4 jit_solution(15165491368847321726)
XLA Ops:
  9.1 3.1 collective-permute-start
  12.2 2.6 collective-permute-start.1
  14.7 2.8 collective-permute-start.3
  24.6 5.6 %collective-permute-start.7 = (bf16[64,1024]{1,0:T(8,128)(2,1)S(1)}, bf16[64,1024]{1,0:T(8,128)(2,1)S(1)}, u32[]{:S(2)}, u32[]{:S(2)}) collective-permute-start(bf16[64,1024]{1,0:T(8,128)(2,1)S(1)} %pad_maximum_fusion.9), channel_id=1, source_target_pairs={{0,3},{1,2},{2,1},{3,0},{4,7},{5,6},{6,5},{7,4},{8,11},{9,10},{10,... | collective-permute-start | bytes 393224 | tf_op jit(solution)/shard_map/ppermute | solution.py:128
  42.9 3.2 collective-permute-done.10
  50.0 2.9 collective-permute-start.12
  53.9 25.0 %attn_forward.2 = (f32[768,512]{1,0:T(8,128)}, bf16[768,512]{1,0:T(8,128)(2,1)}, bf16[4,3,256,128]{3,2,1,0:T(8,128)(2,1)}, bf16[4,8,256,128]{3,2,1,0:T(8,128)(2,...) custom-call(s32[9]{0:T(128)} %stack.119.meta.refs_0_, ...), custom_call_target="tpu_custom_call" | custom-call | flops 28999999488 | bytes 14000000 | tf_op jit(solution)/shard_map/attn_forward/pallas_call | solution.py:340
  80.0 2.6 all-gather.7.cloned.1.call-done
  82.6 13.9 %mlp_forward.2 = (f32[768,512]{1,0:T(8,128)}, bf16[4,768,512]{2,1,0:T(8,128)(2,1)}, bf16[4,768,512]{2,1,0:T(8,128)(2,1)}, bf16[768,512]{1,0:T(8,128)(2,1)}) custom-call(s32[32]{0:T(128)} %fusion.30.table, bf16[8,4,64,1024]{3,2,1,0:T(8,128)(2,1)} %bitcast.125, bf16[8,4,64,1024]{3,2,1,0:T(8,128)(2,1)} %bitcast.126, ...), custom_call_target="tpu_custom_call" | custom-call | flops 15000000512 | bytes 18000000 | tf_op jit(solution)/shard_map/mlp_forward/pallas_call | solution.py:445
  96.5 3.4 collective-permute-start.15
  102.2 15.3 %collective-permute-done.15.refs_1_.refs_3_ = bf16[768,512]{1,0:T(8,128)(2,1)S(1)} collective-permute-done((bf16[768,512]{1,0:T(8,128)(2,1)}, bf16[768,512]{1,0:T(8,128)(2,1)S(1)}, u32[]{:S(2)}, u32[]{:S(2)}) %collective-permute-start.15) | collective-permute-done | bytes 786464 | tf_op jit(solution)/shard_map/ppermute | solution.py:201
  117.5 4.1 %collective-permute-done.16.refs_3_.refs_5_ = bf16[768,512]{1,0:T(8,128)(2,1)S(1)} collective-permute-done((bf16[768,512]{1,0:T(8,128)(2,1)}, bf16[768,512]{1,0:T(8,128)(2,1)S(1)}, u32[]{:S(2)}, u32[]{:S(2)}) %collective-permute-start.16) | collective-permute-done | bytes 786464 | tf_op jit(solution)/shard_map/ppermute | solution.py:206
  121.5 9.1 %all-gather.5.cloned.1.call-done = bf16[32,64,1536]{2,1,0:T(8,128)(2,1)} async-done(((bf16[4,64,1536]{2,1,0:T(8,128)(2,1)}), bf16[32,64,1536]{2,1,0:T(8,128)(2,1)}) %all-gather.5.cloned.1.call-update) | async-done | bytes 6291472 | tf_op jit(solution)/shard_map/all_gather | solution.py:170
  130.6 22.8 %attn_forward.3 = (f32[768,512]{1,0:T(8,128)}, bf16[768,512]{1,0:T(8,128)(2,1)}, bf16[4,3,256,128]{3,2,1,0:T(8,128)(2,1)}, bf16[4,8,256,128]{3,2,1,0:T(8,128)(2,...) custom-call(s32[9]{0:T(128)} %stack.119.meta.refs_0_, ...), custom_call_target="tpu_custom_call" | custom-call | flops 28999999488 | bytes 14000000 | tf_op jit(solution)/shard_map/attn_forward/pallas_call | solution.py:340
  153.5 13.2 %mlp_forward.3 = (f32[768,512]{1,0:T(8,128)}, bf16[4,768,512]{2,1,0:T(8,128)(2,1)}, bf16[4,768,512]{2,1,0:T(8,128)(2,1)}) custom-call(s32[32]{0:T(128)} %fusion.30.table, bf16[8,4,64,1536]{3,2,1,0:T(8,128)(2,1)} %bitcast.120, bf16[8,4,64,1536]{3,2,1,0:T(8,128)(2,1)} %bitcast.121, bf16[768,512]{1,0:T(8,128)(2,1)} %get-tuple-element.125.refs_2_.refs_8_, ...), custom_call_target="tpu_custom_call" | custom-call | flops 15000000512 | bytes 18000000 | tf_op jit(solution)/shard_map/mlp_forward/pallas_call | solution.py:445
  167.2 15.9 %mlp_backward.2 = (bf16[32,64,1024]{2,1,0:T(8,128)(2,1)}, f32[768,512]{1,0:T(8,128)}, f32[8,512]{1,0:T(8,128)}) custom-call(s32[9]{0:T(128)} %stack.119.meta.refs_0_, s32[32]{0:T(128)} %iota.34.refs_1_, f32[3]{0:T(128)} %refs_2_.1, bf16[768,512]{1,0:T(8,128)(2,1)} %refs_3_.1, bf16[8,4,64,1536]{3,2,1,0:T(8,128)(2,1)} %bitcast.122, ...), custom_call_target="tpu_custom_call" | custom-call | flops 20000000000 | bytes 20000000 | tf_op jit(solution)/shard_map/mlp_backward/pallas_call | solution.py:548
  183.1 35.9 %attn_backward.2 = (bf16[32,64,512]{2,1,0:T(8,128)(2,1)}, bf16[768,512]{1,0:T(8,128)(2,1)}, f32[768,512]{1,0:T(8,128)}, bf16[768,512]{1,0:T(8,128)(2,1)}, f32[8,512]{1,0:T(8,128)}) custom-call(s32[9]{0:T(128)} %stack.119.meta.refs_0_, s32[32]{0:T(128)} %and_or_fusion.refs_1_, bf16[8,4,64,1536]{3,2,1,0:T(8,128)(2,1)} %bitcast.124, ...), custom_call_target="tpu_custom_call" | custom-call | flops 44999999488 | bytes 24000000 | tf_op jit(solution)/shard_map/attn_backward/pallas_call | solution.py:690
  220.9 8.7 %collective-permute-start.21 = (bf16[768,512]{1,0:T(8,128)(2,1)}, bf16[768,512]{1,0:T(8,128)(2,1)S(1)}, u32[]{:S(2)}, u32[]{:S(2)}) collective-permute-start(bf16[768,512]{1,0:T(8,128)(2,1)} %get-tuple-element.139), channel_id=1, source_target_pairs={{0,1},{1,2},{2,3},{4,5},{5,6},{6,7},{8,9},{9,10},{10,11},{12,13},{... | collective-permute-start | bytes 2359304 | tf_op jit(solution)/shard_map/ppermute | solution.py:201
  235.0 12.0 %collective-permute-done.21.refs_5_ = bf16[768,512]{1,0:T(8,128)(2,1)S(1)} collective-permute-done((bf16[768,512]{1,0:T(8,128)(2,1)}, bf16[768,512]{1,0:T(8,128)(2,1)S(1)}, u32[]{:S(2)}, u32[]{:S(2)}) %collective-permute-start.21) | collective-permute-done | bytes 786464 | tf_op jit(solution)/shard_map/ppermute | solution.py:201
  247.0 4.1 %collective-permute-done.22.refs_6_ = bf16[768,512]{1,0:T(8,128)(2,1)S(1)} collective-permute-done((bf16[768,512]{1,0:T(8,128)(2,1)}, bf16[768,512]{1,0:T(8,128)(2,1)S(1)}, u32[]{:S(2)}, u32[]{:S(2)}) %collective-permute-start.22) | collective-permute-done | bytes 786464 | tf_op jit(solution)/shard_map/ppermute | solution.py:206
  252.0 18.7 %mlp_backward.3 = (bf16[32,64,1024]{2,1,0:T(8,128)(2,1)}, f32[768,512]{1,0:T(8,128)}, f32[8,512]{1,0:T(8,128)}) custom-call(s32[9]{0:T(128)} %stack.119.meta.refs_0_, s32[32]{0:T(128)} %iota.35.refs_1_, bf16[16,64,512]{2,1,0:T(8,128)(2,1)} %copy-done.5, f32[768,512]{1,0:T(8,128)} %get-tuple-element.130.refs_6_.refs_3_, ...), custom_call_target="tpu_custom_call" | custom-call | flops 20000000000 | bytes 20000000 | tf_op jit(solution)/shard_map/mlp_backward/pallas_call | solution.py:548
  276.4 2.9 collective-permute-start.25
  279.3 36.3 %attn_backward.3 = (bf16[32,64,512]{2,1,0:T(8,128)(2,1)}, bf16[768,512]{1,0:T(8,128)(2,1)}, f32[768,512]{1,0:T(8,128)}, bf16[768,512]{1,0:T(8,128)(2,1)}, f32[8,512]{1,0:T(8,128)}) custom-call(s32[9]{0:T(128)} %stack.119.meta.refs_0_, s32[32]{0:T(128)} %and_or_fusion.refs_1_, bf16[4,64,1536]{2,1,0:T(8,128)(2,1)} %pad_maximum_fusion.refs_2_, ...), custom_call_target="tpu_custom_call" | custom-call | flops 44999999488 | bytes 24000000 | tf_op jit(solution)/shard_map/attn_backward/pallas_call | solution.py:690
  317.4 7.1 %collective-permute-start.30 = (bf16[768,512]{1,0:T(8,128)(2,1)}, bf16[768,512]{1,0:T(8,128)(2,1)}, u32[]{:S(2)}, u32[]{:S(2)}) collective-permute-start(bf16[768,512]{1,0:T(8,128)(2,1)} %get-tuple-element.163), channel_id=1, source_target_pairs={{0,1},{1,2},{2,3},{4,5},{5,6},{6,7},{8,9},{9,10},{10,11},{12,13},{... | collective-permute-start | bytes 2359304 | tf_op jit(solution)/shard_map/ppermute | solution.py:201
  330.8 5.9 %collective-permute-done.29 = bf16[4,64,512]{2,1,0:T(8,128)(2,1)S(1)} collective-permute-done((bf16[4,64,512]{2,1,0:T(8,128)(2,1)S(1)}, bf16[4,64,512]{2,1,0:T(8,128)(2,1)S(1)}, u32[]{:S(2)}, u32[]{:S(2)}) %collective-permute-start.29) | collective-permute-done | bytes 262176 | tf_op jit(solution)/shard_map/ppermute | solution.py:128
  336.6 4.8 %collective-permute-done.28 = bf16[4,64,512]{2,1,0:T(8,128)(2,1)S(1)} collective-permute-done((bf16[4,64,512]{2,1,0:T(8,128)(2,1)S(1)}, bf16[4,64,512]{2,1,0:T(8,128)(2,1)S(1)}, u32[]{:S(2)}, u32[]{:S(2)}) %collective-permute-start.28) | collective-permute-done | bytes 262176 | tf_op jit(solution)/shard_map/ppermute | solution.py:128
  343.5 2.8 collective-permute-done.31.refs_4_
  347.8 4.1 %entry_backward.1 = (f32[768,512]{1,0:T(8,128)}, f32[40,512]{1,0:T(8,128)S(1)}) custom-call(bf16[4,64,1536]{2,1,0:T(8,128)(2,1)S(1)} %pad_maximum_fusion.1.refs_0_, f32[768,512]{1,0:T(8,128)S(1)} %copy-done.1, f32[768,512]{1,0:T(8,128)S(1)} %copy-done.2, bf16[768,512]{1,0:T(8,128)(2,1)} %collective-permute-done.30.refs_3_, ...), custom_call_target="tpu_custom_call" | custom-call | flops 100000000 | bytes 9000000 | tf_op jit(solution)/shard_map/entry_backward/pallas_call | solution.py:766
  358.4 3.2 collective-permute-start.34
  361.6 3.8 collective-permute-done.32
  365.4 8.8 %collective-permute-done.33 = bf16[1,64,1536]{2,1,0:T(8,128)(2,1)S(1)} collective-permute-done((bf16[1,64,1536]{2,1,0:T(8,128)(2,1)S(1)}, bf16[1,64,1536]{2,1,0:T(8,128)(2,1)S(1)}, u32[]{:S(2)}, u32[]{:S(2)}) %collective-permute-start.33) | collective-permute-done | bytes 196640 | tf_op jit(solution)/shard_map/ppermute | solution.py:128
  374.4 3.5 collective-permute-start.40
  (232 shorter events, 70.3 us)
Async XLA Ops:
  7.2 75.4 %all-gather.7.cloned.1.call-start = ((), (), s32[]{:S(2)}) async-start(), calls=%async_computation.5 | async-start | bytes 4718592 | tf_op jit(solution)/shard_map/all_gather | solution.py:170
  9.1 15.5 %collective-permute-start = (bf16[64,512]{1,0:T(8,128)(2,1)S(1)}, bf16[64,512]{1,0:T(8,128)(2,1)S(1)}, u32[]{:S(2)}, u32[]{:S(2)}) collective-permute-start(bf16[64,512]{1,0:T(8,128)(2,1)S(1)} %pad_maximum_fusion.10), channel_id=1, source_target_pairs={{0,1},{1,0},{2,3},{3,2},{4,5},{5,4},{6,7},{7,6},{8,9},{9,8},{10,11... | collective-permute-start | bytes 196616 | tf_op jit(solution)/shard_map/ppermute | solution.py:128
  12.2 12.4 %collective-permute-start.1 = (bf16[64,512]{1,0:T(8,128)(2,1)S(1)}, bf16[64,512]{1,0:T(8,128)(2,1)S(1)}, u32[]{:S(2)}, u32[]{:S(2)}) collective-permute-start(bf16[64,512]{1,0:T(8,128)(2,1)S(1)} %pad_maximum_fusion.10), channel_id=1, source_target_pairs={{0,2},{1,3},{2,0},{3,1},{4,6},{5,7},{6,4},{7,5},{8,10},{9,11},{10,... | collective-permute-start | bytes 196616 | tf_op jit(solution)/shard_map/ppermute | solution.py:128
  24.6 14.1 %collective-permute-start.7 = (bf16[64,1024]{1,0:T(8,128)(2,1)S(1)}, bf16[64,1024]{1,0:T(8,128)(2,1)S(1)}, u32[]{:S(2)}, u32[]{:S(2)}) collective-permute-start(bf16[64,1024]{1,0:T(8,128)(2,1)S(1)} %pad_maximum_fusion.9), channel_id=1, source_target_pairs={{0,3},{1,2},{2,1},{3,0},{4,7},{5,6},{6,5},{7,4},{8,11},{9,10},{10,... | collective-permute-start | bytes 393224 | tf_op jit(solution)/shard_map/ppermute | solution.py:128
  30.3 11.7 %collective-permute-start.6 = (bf16[64,1024]{1,0:T(8,128)(2,1)S(1)}, bf16[64,1024]{1,0:T(8,128)(2,1)S(1)}, u32[]{:S(2)}, u32[]{:S(2)}) collective-permute-start(bf16[64,1024]{1,0:T(8,128)(2,1)S(1)} %pad_maximum_fusion.9), channel_id=1, source_target_pairs={{0,2},{1,3},{2,0},{3,1},{4,6},{5,7},{6,4},{7,5},{8,10},{9,11},{10,... | collective-permute-start | bytes 393224 | tf_op jit(solution)/shard_map/ppermute | solution.py:128
  30.3 11.7 %collective-permute-start.5 = (bf16[64,1024]{1,0:T(8,128)(2,1)S(1)}, bf16[64,1024]{1,0:T(8,128)(2,1)S(1)}, u32[]{:S(2)}, u32[]{:S(2)}) collective-permute-start(bf16[64,1024]{1,0:T(8,128)(2,1)S(1)} %pad_maximum_fusion.9), channel_id=1, source_target_pairs={{0,1},{1,0},{2,3},{3,2},{4,5},{5,4},{6,7},{7,6},{8,9},{9,8},{10,11... | collective-permute-start | bytes 393224 | tf_op jit(solution)/shard_map/ppermute | solution.py:128
  30.9 12.0 %collective-permute-start.8 = (bf16[4,64,512]{2,1,0:T(8,128)(2,1)S(1)}, bf16[4,64,512]{2,1,0:T(8,128)(2,1)S(1)}, u32[]{:S(2)}, u32[]{:S(2)}) collective-permute-start(bf16[4,64,512]{2,1,0:T(8,128)(2,1)S(1)} %pad_maximum_fusion.5), channel_id=1, source_target_pairs={{0,8},{1,9},{2,10},{3,11},{4,12},{5,13},{6,14},{7,15},{8,0},{9,1},... | collective-permute-start | bytes 786440 | tf_op jit(solution)/shard_map/ppermute | solution.py:128
  32.4 10.5 %collective-permute-start.9 = (bf16[4,64,512]{2,1,0:T(8,128)(2,1)S(1)}, bf16[4,64,512]{2,1,0:T(8,128)(2,1)S(1)}, u32[]{:S(2)}, u32[]{:S(2)}) collective-permute-start(bf16[4,64,512]{2,1,0:T(8,128)(2,1)S(1)} %pad_maximum_fusion.5), channel_id=1, source_target_pairs={{0,16},{1,17},{2,18},{3,19},{4,20},{5,21},{6,22},{7,23},{8,24},{9,... | collective-permute-start | bytes 786440 | tf_op jit(solution)/shard_map/ppermute | solution.py:128
  46.2 84.4 %all-gather.5.cloned.1.call-start = ((), (), s32[]{:S(2)}) async-start(), calls=%async_computation.4 | async-start | bytes 7077888 | tf_op jit(solution)/shard_map/all_gather | solution.py:170
  48.5 30.4 %collective-permute-start.11 = (bf16[64,1536]{1,0:T(8,128)(2,1)S(1)}, bf16[64,1536]{1,0:T(8,128)(2,1)S(1)}, u32[]{:S(2)}, u32[]{:S(2)}) collective-permute-start(bf16[64,1536]{1,0:T(8,128)(2,1)S(1)} %pad_maximum_fusion.8), channel_id=1, source_target_pairs={{0,1},{1,0},{2,3},{3,2},{4,5},{5,4},{6,7},{7,6},{8,9},{9,8},{10,11... | collective-permute-start | bytes 589832 | tf_op jit(solution)/shard_map/ppermute | solution.py:128
  50.0 29.0 %collective-permute-start.12 = (bf16[64,1536]{1,0:T(8,128)(2,1)S(1)}, bf16[64,1536]{1,0:T(8,128)(2,1)S(1)}, u32[]{:S(2)}, u32[]{:S(2)}) collective-permute-start(bf16[64,1536]{1,0:T(8,128)(2,1)S(1)} %pad_maximum_fusion.8), channel_id=1, source_target_pairs={{0,2},{1,3},{2,0},{3,1},{4,6},{5,7},{6,4},{7,5},{8,10},{9,11},{10,... | collective-permute-start | bytes 589832 | tf_op jit(solution)/shard_map/ppermute | solution.py:128
  52.9 26.0 %collective-permute-start.13 = (bf16[64,1536]{1,0:T(8,128)(2,1)S(1)}, bf16[64,1536]{1,0:T(8,128)(2,1)S(1)}, u32[]{:S(2)}, u32[]{:S(2)}) collective-permute-start(bf16[64,1536]{1,0:T(8,128)(2,1)S(1)} %pad_maximum_fusion.8), channel_id=1, source_target_pairs={{0,3},{1,2},{2,1},{3,0},{4,7},{5,6},{6,5},{7,4},{8,11},{9,10},{10,... | collective-permute-start | bytes 589832 | tf_op jit(solution)/shard_map/ppermute | solution.py:128
  79.9 191.9 %reduce-scatter.3.cloned.1.call-start = ((), (), s32[]{:S(2)}) async-start(), calls=%async_computation.2 | async-start | bytes 4718592 | tf_op jit(solution)/shard_map/reduce_scatter | solution.py:176
  96.5 20.9 %collective-permute-start.15 = (bf16[768,512]{1,0:T(8,128)(2,1)}, bf16[768,512]{1,0:T(8,128)(2,1)S(1)}, u32[]{:S(2)}, u32[]{:S(2)}) collective-permute-start(bf16[768,512]{1,0:T(8,128)(2,1)} %get-tuple-element.123.refs_2_.refs_4_), channel_id=1, source_target_pairs={{0,1},{1,2},{2,3},{4,5},{5,6},{6,7},{8,9},{9,10},{10,11},{12,13},{... | collective-permute-start | bytes 2359304 | tf_op jit(solution)/shard_map/ppermute | solution.py:201
  100.0 21.5 %collective-permute-start.16 = (bf16[768,512]{1,0:T(8,128)(2,1)}, bf16[768,512]{1,0:T(8,128)(2,1)S(1)}, u32[]{:S(2)}, u32[]{:S(2)}) collective-permute-start(bf16[768,512]{1,0:T(8,128)(2,1)} %get-tuple-element.123.refs_2_.refs_4_), channel_id=1, source_target_pairs={{1,0},{2,1},{3,2},{5,4},{6,5},{7,6},{9,8},{10,9},{11,10},{13,12},{... | collective-permute-start | bytes 2359304 | tf_op jit(solution)/shard_map/ppermute | solution.py:206
  183.1 159.2 %reduce-scatter.5.cloned.1.call-start = ((), (), s32[]{:S(2)}) async-start(), calls=%async_computation.3 | async-start | bytes 4718592 | tf_op jit(solution)/shard_map/reduce_scatter | solution.py:176
  220.5 10.5 %collective-permute-start.17 = (bf16[16,64,512]{2,1,0:T(8,128)(2,1)S(1)}, bf16[16,64,512]{2,1,0:T(8,128)(2,1)S(1)}, u32[]{:S(2)}, u32[]{:S(2)}) collective-permute-start(bf16[16,64,512]{2,1,0:T(8,128)(2,1)S(1)} %slice.202), channel_id=1, source_target_pairs={{0,4},{1,5},{2,6},{3,7},{4,0},{5,1},{6,2},{7,3},{8,12},{9,13},{10,... | collective-permute-start | bytes 3145736 | tf_op jit(solution)/shard_map/ppermute | solution.py:128
  220.9 26.2 %collective-permute-start.21 = (bf16[768,512]{1,0:T(8,128)(2,1)}, bf16[768,512]{1,0:T(8,128)(2,1)S(1)}, u32[]{:S(2)}, u32[]{:S(2)}) collective-permute-start(bf16[768,512]{1,0:T(8,128)(2,1)} %get-tuple-element.139), channel_id=1, source_target_pairs={{0,1},{1,2},{2,3},{4,5},{5,6},{6,7},{8,9},{9,10},{10,11},{12,13},{... | collective-permute-start | bytes 2359304 | tf_op jit(solution)/shard_map/ppermute | solution.py:201
  229.6 21.5 %collective-permute-start.22 = (bf16[768,512]{1,0:T(8,128)(2,1)}, bf16[768,512]{1,0:T(8,128)(2,1)S(1)}, u32[]{:S(2)}, u32[]{:S(2)}) collective-permute-start(bf16[768,512]{1,0:T(8,128)(2,1)} %get-tuple-element.140), channel_id=1, source_target_pairs={{1,0},{2,1},{3,2},{5,4},{6,5},{7,6},{9,8},{10,9},{11,10},{13,12},{... | collective-permute-start | bytes 2359304 | tf_op jit(solution)/shard_map/ppermute | solution.py:206
  231.5 39.2 %collective-permute-start.18 = (bf16[4,64,512]{2,1,0:T(8,128)(2,1)S(1)}, bf16[4,64,512]{2,1,0:T(8,128)(2,1)S(1)}, u32[]{:S(2)}, u32[]{:S(2)}) collective-permute-start(bf16[4,64,512]{2,1,0:T(8,128)(2,1)S(1)} %get-tuple-element.278), channel_id=1, source_target_pairs={{0,8},{1,9},{2,10},{3,11},{4,12},{5,13},{6,14},{7,15},{8,0},{9,1},... | collective-permute-start | bytes 786440 | tf_op jit(solution)/shard_map/ppermute | solution.py:128
  233.0 37.7 %collective-permute-start.19 = (bf16[4,64,512]{2,1,0:T(8,128)(2,1)S(1)}, bf16[4,64,512]{2,1,0:T(8,128)(2,1)S(1)}, u32[]{:S(2)}, u32[]{:S(2)}) collective-permute-start(bf16[4,64,512]{2,1,0:T(8,128)(2,1)S(1)} %get-tuple-element.277), channel_id=1, source_target_pairs={{0,16},{1,17},{2,18},{3,19},{4,20},{5,21},{6,22},{7,23},{8,24},{9,... | collective-permute-start | bytes 786440 | tf_op jit(solution)/shard_map/ppermute | solution.py:128
  233.6 37.1 %collective-permute-start.20 = (bf16[4,64,512]{2,1,0:T(8,128)(2,1)S(1)}, bf16[4,64,512]{2,1,0:T(8,128)(2,1)S(1)}, u32[]{:S(2)}, u32[]{:S(2)}) collective-permute-start(bf16[4,64,512]{2,1,0:T(8,128)(2,1)S(1)} %get-tuple-element.276), channel_id=1, source_target_pairs={{0,24},{1,25},{2,26},{3,27},{4,28},{5,29},{6,30},{7,31},{8,16},{9,... | collective-permute-start | bytes 786440 | tf_op jit(solution)/shard_map/ppermute | solution.py:128
  274.9 40.7 %collective-permute-start.23 = (bf16[1,64,1536]{2,1,0:T(8,128)(2,1)S(1)}, bf16[1,64,1536]{2,1,0:T(8,128)(2,1)S(1)}, u32[]{:S(2)}, u32[]{:S(2)}) collective-permute-start(bf16[1,64,1536]{2,1,0:T(8,128)(2,1)S(1)} %get-tuple-element.283), channel_id=1, source_target_pairs={{0,1},{1,0},{2,3},{3,2},{4,5},{5,4},{6,7},{7,6},{8,9},{9,8},{10,11... | collective-permute-start | bytes 589832 | tf_op jit(solution)/shard_map/ppermute | solution.py:128
  276.4 39.3 %collective-permute-start.24 = (bf16[1,64,1536]{2,1,0:T(8,128)(2,1)S(1)}, bf16[1,64,1536]{2,1,0:T(8,128)(2,1)S(1)}, u32[]{:S(2)}, u32[]{:S(2)}) collective-permute-start(bf16[1,64,1536]{2,1,0:T(8,128)(2,1)S(1)} %get-tuple-element.284), channel_id=1, source_target_pairs={{0,2},{1,3},{2,0},{3,1},{4,6},{5,7},{6,4},{7,5},{8,10},{9,11},{10,... | collective-permute-start | bytes 589832 | tf_op jit(solution)/shard_map/ppermute | solution.py:128
  276.4 39.3 %collective-permute-start.25 = (bf16[1,64,1536]{2,1,0:T(8,128)(2,1)S(1)}, bf16[1,64,1536]{2,1,0:T(8,128)(2,1)S(1)}, u32[]{:S(2)}, u32[]{:S(2)}) collective-permute-start(bf16[1,64,1536]{2,1,0:T(8,128)(2,1)S(1)} %get-tuple-element.282), channel_id=1, source_target_pairs={{0,3},{1,2},{2,1},{3,0},{4,7},{5,6},{6,5},{7,4},{8,11},{9,10},{10,... | collective-permute-start | bytes 589832 | tf_op jit(solution)/shard_map/ppermute | solution.py:128
  317.4 26.1 %collective-permute-start.30 = (bf16[768,512]{1,0:T(8,128)(2,1)}, bf16[768,512]{1,0:T(8,128)(2,1)}, u32[]{:S(2)}, u32[]{:S(2)}) collective-permute-start(bf16[768,512]{1,0:T(8,128)(2,1)} %get-tuple-element.163), channel_id=1, source_target_pairs={{0,1},{1,2},{2,3},{4,5},{5,6},{6,7},{8,9},{9,10},{10,11},{12,13},{... | collective-permute-start | bytes 2359304 | tf_op jit(solution)/shard_map/ppermute | solution.py:201
  324.5 21.8 %collective-permute-start.31 = (bf16[768,512]{1,0:T(8,128)(2,1)}, bf16[768,512]{1,0:T(8,128)(2,1)}, u32[]{:S(2)}, u32[]{:S(2)}) collective-permute-start(bf16[768,512]{1,0:T(8,128)(2,1)} %get-tuple-element.164), channel_id=1, source_target_pairs={{1,0},{2,1},{3,2},{5,4},{6,5},{7,6},{9,8},{10,9},{11,10},{13,12},{... | collective-permute-start | bytes 2359304 | tf_op jit(solution)/shard_map/ppermute | solution.py:206
  326.5 10.2 %collective-permute-start.29 = (bf16[4,64,512]{2,1,0:T(8,128)(2,1)S(1)}, bf16[4,64,512]{2,1,0:T(8,128)(2,1)S(1)}, u32[]{:S(2)}, u32[]{:S(2)}) collective-permute-start(bf16[4,64,512]{2,1,0:T(8,128)(2,1)S(1)} %get-tuple-element.274), channel_id=1, source_target_pairs={{0,24},{1,25},{2,26},{3,27},{4,28},{5,29},{6,30},{7,31},{8,16},{9,... | collective-permute-start | bytes 786440 | tf_op jit(solution)/shard_map/ppermute | solution.py:128
  328.0 13.5 %collective-permute-start.28 = (bf16[4,64,512]{2,1,0:T(8,128)(2,1)S(1)}, bf16[4,64,512]{2,1,0:T(8,128)(2,1)S(1)}, u32[]{:S(2)}, u32[]{:S(2)}) collective-permute-start(bf16[4,64,512]{2,1,0:T(8,128)(2,1)S(1)} %get-tuple-element.275), channel_id=1, source_target_pairs={{0,16},{1,17},{2,18},{3,19},{4,20},{5,21},{6,22},{7,23},{8,24},{9,... | collective-permute-start | bytes 786440 | tf_op jit(solution)/shard_map/ppermute | solution.py:128
  329.5 12.0 %collective-permute-start.27 = (bf16[4,64,512]{2,1,0:T(8,128)(2,1)S(1)}, bf16[4,64,512]{2,1,0:T(8,128)(2,1)S(1)}, u32[]{:S(2)}, u32[]{:S(2)}) collective-permute-start(bf16[4,64,512]{2,1,0:T(8,128)(2,1)S(1)} %get-tuple-element.273), channel_id=1, source_target_pairs={{0,8},{1,9},{2,10},{3,11},{4,12},{5,13},{6,14},{7,15},{8,0},{9,1},... | collective-permute-start | bytes 786440 | tf_op jit(solution)/shard_map/ppermute | solution.py:128
  357.1 17.1 %collective-permute-start.33 = (bf16[1,64,1536]{2,1,0:T(8,128)(2,1)S(1)}, bf16[1,64,1536]{2,1,0:T(8,128)(2,1)S(1)}, u32[]{:S(2)}, u32[]{:S(2)}) collective-permute-start(bf16[1,64,1536]{2,1,0:T(8,128)(2,1)S(1)} %get-tuple-element.281), channel_id=1, source_target_pairs={{0,2},{1,3},{2,0},{3,1},{4,6},{5,7},{6,4},{7,5},{8,10},{9,11},{10,... | collective-permute-start | bytes 589832 | tf_op jit(solution)/shard_map/ppermute | solution.py:128
  358.4 15.8 %collective-permute-start.34 = (bf16[1,64,1536]{2,1,0:T(8,128)(2,1)S(1)}, bf16[1,64,1536]{2,1,0:T(8,128)(2,1)S(1)}, u32[]{:S(2)}, u32[]{:S(2)}) collective-permute-start(bf16[1,64,1536]{2,1,0:T(8,128)(2,1)S(1)} %get-tuple-element.279), channel_id=1, source_target_pairs={{0,3},{1,2},{2,1},{3,0},{4,7},{5,6},{6,5},{7,4},{8,11},{9,10},{10,... | collective-permute-start | bytes 589832 | tf_op jit(solution)/shard_map/ppermute | solution.py:128
  (55 other events, 474.6 us)
Sparse Core Ops, SparseCore 0:
  46.4 36.2 all-gather.6
  85.1 45.5 all-gather.4
  183.2 52.1 reduce-scatter.2
  270.8 49.4 reduce-scatter.4

commit v2 on v1

--- a/solution.py
+++ b/solution.py
@@ -60,6 +60,14 @@
     return call
 
 
+def kept_out(shape, dtype):
+    return pltpu.HBM(shape, dtype)
+
+
+def from_hbm(*arrays):
+    return tuple(pltpu.with_memory_space_constraint(x, pltpu.HBM) for x in arrays)
+
+
 def params(mib):
     return pltpu.CompilerParams(
         dimension_semantics=("arbitrary",), vmem_limit_bytes=mib * 1024 * 1024
@@ -128,12 +136,9 @@
     return lax.ppermute(values, ALL, [(i, target(i)) for i in range(count)])
 
 
-def block_places(my_dp):
+def block_owners(my_dp):
     index = jnp.arange(32, dtype=jnp.int32)
-    apart = (index >> 2) ^ my_dp
-    place = ((apart & 1) << 4) | ((apart >> 1) << 2) | (index & 3)
-    owner = my_dp ^ ((((index >> 2) & 3) << 1) | (index >> 4))
-    return place, owner
+    return my_dp ^ ((((index >> 2) & 3) << 1) | (index >> 4))
 
 
 def tie(values, after):
@@ -148,10 +153,8 @@
     return jnp.stack([values] + [flip(values, bits) for bits in (1, 2, 3)])
 
 
-def scatter_core(blocks):
-    half = blocks.shape[0] // 2
-    arrived = flip(blocks[half:], 4)
-    return (blocks[:half].astype(f32) + arrived.astype(f32)).astype(bf16)
+def scatter_core(own, other):
+    return (own.astype(f32) + flip(other, 4).astype(f32)).astype(bf16)
 
 
 def scatter_four(blocks, unit):
@@ -204,11 +207,6 @@
 def shift_left(values):
     count = lax.axis_size("mp")
     return lax.ppermute(values, "mp", [(i + 1, i) for i in range(count - 1)])
-
-
-def sum_four(values, unit):
-    one, two, three = [flip(values, i * unit) for i in (1, 2, 3)]
-    return (values + one) + (two + three)
 
 
 def fetch_blocks(table, near, far, targets, sems):
@@ -268,25 +266,28 @@
         return carry
 
     lax.fori_loop(0, meta[2], project, 0)
-    lane = lax.broadcasted_iota(jnp.int32, (CH, PAIR), 1)
+    lane = lax.broadcasted_iota(jnp.int32, (CH, PAIR), 1) // HEAD_DIM
+    lane_all = lax.broadcasted_iota(jnp.int32, (LEN, PAIR), 1) // HEAD_DIM
 
     for j in range(3):
         slot = meta[3 + j]
         query = q_o[0, j]
         keys = k_o[0, pl.ds(slot * SLOT, SLOT)].reshape(LEN, PAIR)
         values = v_o[0, pl.ds(slot * SLOT, SLOT)].reshape(LEN, PAIR)
+        zero = jnp.zeros_like(query)
+        both = jnp.concatenate([jnp.where(lane == h, query, zero) for h in range(2)], axis=0)
+        scores = mm(both, keys, NT)
+        top = jnp.max(scores, axis=1, keepdims=True)
+        weights = jnp.exp2(scores - top).astype(bf16)
         parts = []
         for h in range(2):
-            q_h = jnp.where((lane // HEAD_DIM) == h, query, jnp.zeros_like(query))
-            scores = mm(q_h, keys, NT)
-            top = jnp.max(scores, axis=1, keepdims=True)
-            weights = jnp.exp2(scores - top)
-            denominator = jnp.sum(weights, axis=1, keepdims=True)
-            mixed = mm(weights.astype(bf16), values)
-            parts.append(mixed * (1.0 / denominator))
-            spread = jnp.broadcast_to(top + jnp.log2(denominator), (CH, PAIR))
-            lse_o[0, j, h : h + 1] = spread.T[0:1]
-        out = jnp.where((lane // HEAD_DIM) == 0, parts[0], parts[1]).astype(bf16)
+            value_h = jnp.where(lane_all == h, values, jnp.ones_like(values))
+            mixed = mm(weights[h * CH : (h + 1) * CH], value_h)
+            sums = pltpu.roll(mixed, HEAD_DIM, 1)
+            parts.append(mixed / sums)
+            spread = top[h * CH : (h + 1) * CH] + jnp.log2(sums)
+            lse_o[0, j, h : h + 1] = spread.T[h * HEAD_DIM : h * HEAD_DIM + 1]
+        out = jnp.where(lane == 0, parts[0], parts[1]).astype(bf16)
         o_o[0, j] = out
         total[j] += mm(out, weight(3 * PAIR, D), NT)
 
@@ -299,20 +300,21 @@
             normed[rows] = layer_norm(values, norm[2:3], norm[3:4]).astype(bf16)
 
 
-def attn_forward(weights, meta, table, left, own, right, resid, norm, groups):
+def attn_forward(weights, meta, table, left, own, right, resid, norm, groups, keep):
     rows = own.shape[0]
     gathered = isinstance(weights, tuple)
     const = lambda s, *_: (0, 0)
     pair = lambda s, *_: (s, 0, 0, 0)
     full = pl.BlockSpec((rows, D), const)
+    near_out = kept_out if keep else jax.ShapeDtypeStruct
     out_shape = [
-        jax.ShapeDtypeStruct((rows, D), f32),
-        jax.ShapeDtypeStruct((rows, D), bf16),
-        jax.ShapeDtypeStruct((groups, 3, CH, PAIR), bf16),
-        jax.ShapeDtypeStruct((groups, 2 * SLOT, CH, PAIR), bf16),
-        jax.ShapeDtypeStruct((groups, 2 * SLOT, CH, PAIR), bf16),
-        jax.ShapeDtypeStruct((groups, 3, CH, PAIR), bf16),
-        jax.ShapeDtypeStruct((groups, 3, 8, CH), f32),
+        near_out((rows, D), f32),
+        near_out((rows, D), bf16),
+        kept_out((groups, 3, CH, PAIR), bf16),
+        kept_out((groups, 2 * SLOT, CH, PAIR), bf16),
+        kept_out((groups, 2 * SLOT, CH, PAIR), bf16),
+        kept_out((groups, 3, CH, PAIR), bf16),
+        kept_out((groups, 3, 8, CH), f32),
     ]
     out_specs = [
         full,
@@ -330,7 +332,7 @@
     if gathered:
         w_args = list(weights)
         w_specs = [hbm(), hbm()]
-        out_shape.append(jax.ShapeDtypeStruct((8, 4, 64, D), bf16))
+        out_shape.append(kept_out((8, 4, 64, D), bf16))
         out_specs.append(pl.BlockSpec((8, 4, 64, D), pair_zero))
         scratch.append(pltpu.SemaphoreType.DMA((32, 1)))
     else:
@@ -348,12 +350,12 @@
             scratch_shapes=scratch,
         ),
         out_shape=out_shape,
-        compiler_params=params(56),
+        compiler_params=params(28),
         cost_estimate=pl.CostEstimate(
             flops=29_000_000_000, bytes_accessed=14_000_000, transcendentals=0
         ),
         name="attn_forward",
-    )(meta, table, *w_args, left, own, right, resid, norm)
+    )(meta, table, *from_hbm(*w_args), left, own, right, resid, norm)
     if gathered:
         return outs[:7], outs[7]
     return outs, weights
@@ -363,18 +365,15 @@
     return (0, 0, 0, 0)
 
 
-def mlp_forward_kernel(gathered, last, groups, table, *refs):
+def mlp_forward_kernel(gathered, groups, table, *refs):
     if gathered:
         near, far, normed, middle, norm = refs[:5]
         refs = refs[5:]
     else:
         up_in, down_in, normed, middle, norm = refs[:5]
         refs = refs[5:]
-    after, act_o, slope_o = refs[:3]
-    refs = refs[3:]
-    if not last:
-        next_o = refs[0]
-        refs = refs[1:]
+    after, act_o, slope_o, next_o = refs[:4]
+    refs = refs[4:]
     if gathered:
         up_o, down_o, total, sems = refs
     else:
@@ -411,25 +410,22 @@
             rows = pl.ds(j * CH, CH)
             values = middle[rows] + total[j]
             after[rows] = values
-            if not last:
-                next_o[rows] = layer_norm(values, norm[0:1], norm[1:2]).astype(bf16)
-
-
-def mlp_forward(weights, table, normed, middle, norm, groups, last):
+            next_o[rows] = layer_norm(values, norm[0:1], norm[1:2]).astype(bf16)
+
+
+def mlp_forward(weights, table, normed, middle, norm, groups):
     rows = normed.shape[0]
     gathered = not isinstance(weights[0], tuple)
     const = lambda s, *_: (0, 0)
     full = pl.BlockSpec((rows, D), const)
     part = pl.BlockSpec((1, rows, D), lambda s, *_: (s, 0, 0))
     out_shape = [
-        jax.ShapeDtypeStruct((rows, D), f32),
-        jax.ShapeDtypeStruct((groups, rows, D), bf16),
-        jax.ShapeDtypeStruct((groups, rows, D), bf16),
+        kept_out((rows, D), f32),
+        kept_out((groups, rows, D), bf16),
+        kept_out((groups, rows, D), bf16),
+        jax.ShapeDtypeStruct((rows, D), bf16),
     ]
-    out_specs = [full, part, part]
-    if not last:
-        out_shape.append(jax.ShapeDtypeStruct((rows, D), bf16))
-        out_specs.append(full)
+    out_specs = [full, part, part, full]
     scratch = [pltpu.VMEM((3, CH, D), f32)]
     if gathered:
         w_args = list(weights)
@@ -443,7 +439,7 @@
         w_args = [up_w, down_w]
         w_specs = [weight_spec(up_w, up_at), weight_spec(down_w, down_at)]
     outs = pl.pallas_call(
-        functools.partial(mlp_forward_kernel, gathered, last, groups),
+        functools.partial(mlp_forward_kernel, gathered, groups),
         grid_spec=pltpu.PrefetchScalarGridSpec(
             num_scalar_prefetch=1,
             grid=(groups,),
@@ -452,12 +448,12 @@
             scratch_shapes=scratch,
         ),
         out_shape=out_shape,
-        compiler_params=params(56),
+        compiler_params=params(28),
         cost_estimate=pl.CostEstimate(
             flops=15_000_000_000, bytes_accessed=18_000_000, transcendentals=0
         ),
         name="mlp_forward",
-    )(table, *w_args, normed, middle, norm)
+    )(table, *from_hbm(*w_args, normed, middle), norm)
     if gathered:
         return outs[:-2], ((outs[-2], 0), (outs[-1], 0))
     return outs, weights
@@ -476,13 +472,9 @@
         out[place, :, begin : begin + width] = values[d * high : (d + 1) * high]
 
 
-def mlp_backward_kernel(first, groups, split, meta, place, *refs):
-    if first:
-        scale, cot = refs[:2]
-        refs = refs[2:]
-    else:
-        grad_in, d_own, d_left, d_right, source, norm_up = refs[:6]
-        refs = refs[6:]
+def mlp_backward_kernel(groups, split, meta, place, *refs):
+    grad_in, d_own, d_near, d_left, d_right, source, norm_up = refs[:7]
+    refs = refs[7:]
     up_in, down_in, act, slope, normed, middle, norm = refs[:7]
     refs = refs[7:]
     w_grad, grad_out, n_grad = refs[:3]
@@ -495,14 +487,12 @@
         n_grad[...] = jnp.zeros_like(n_grad)
         for j in range(3):
             rows = pl.ds(j * CH, CH)
-            if first:
-                values = cot[rows].astype(f32) * scale[meta[6 + j]]
-            else:
-                arrived = d_own[rows] + d_left[rows].astype(f32) + d_right[rows].astype(f32)
-                back, gain_grad, shift_grad = norm_backward(arrived, source[rows], norm_up[0:1])
-                values = grad_in[rows] + back
-                n_grad[0:1] += gain_grad
-                n_grad[1:2] += shift_grad
+            arrived = d_own[rows] + d_near[rows] + d_left[rows].astype(f32)
+            arrived += d_right[rows].astype(f32)
+            back, gain_grad, shift_grad = norm_backward(arrived, source[rows], norm_up[0:1])
+            values = grad_in[rows] + back
+            n_grad[0:1] += gain_grad
+            n_grad[1:2] += shift_grad
             grad[j] = values
             rounded = values.astype(bf16)
             low[rows] = rounded
@@ -537,17 +527,16 @@
     weights, meta, place, begin, act, slope, normed, middle, norm, groups, split, after=()
 ):
     rows = normed.shape[0]
-    first = len(begin) == 2
     const = lambda s, *_: (0, 0)
     full = pl.BlockSpec((rows, D), const)
     part = pl.BlockSpec((1, rows, D), lambda s, *_: (s, 0, 0))
     vec = pl.BlockSpec((4, D), const)
     (up_w, up_at), (down_w, down_at) = weights
-    begin_specs = [smem(), full] if first else [full] * 5 + [vec]
+    begin_specs = [full] * 6 + [vec]
     places = split * groups
     return pl.pallas_call(
         after_operands(
-            functools.partial(mlp_backward_kernel, first, groups, split), 2, len(after)
+            functools.partial(mlp_backward_kernel, groups, split), 2, len(after)
         ),
         grid_spec=pltpu.PrefetchScalarGridSpec(
             num_scalar_prefetch=2,
@@ -570,104 +559,202 @@
             ],
         ),
         out_shape=[
-            jax.ShapeDtypeStruct((places, D // split, 2 * D), bf16),
-            jax.ShapeDtypeStruct((rows, D), f32),
+            kept_out((places, D // split, 2 * D), bf16),
+            kept_out((rows, D), f32),
             jax.ShapeDtypeStruct((8, D), f32),
         ],
-        compiler_params=params(56),
+        compiler_params=params(28),
         cost_estimate=pl.CostEstimate(
             flops=20_000_000_000, bytes_accessed=20_000_000, transcendentals=0
         ),
         name="mlp_backward",
-    )(meta, place, *after, *begin, up_w, down_w, act, slope, normed, middle, norm)
-
-
-def attn_backward_kernel(groups, split, meta, place, *refs):
-    w_in, left, own, right, grad_in, small, q_i, k_i, v_i, o_i, lse_i = refs[:11]
-    w_grad, d_left, d_own, d_right, small_o = refs[11:16]
-    ext, ext_t, low, low_t, k_t, dk, dv, d_ext, dq_all = refs[16:]
+    )(meta, place, *from_hbm(*after), *begin, *from_hbm(up_w, down_w, act, slope), normed, middle, norm)
+
+
+def mlp_last_kernel(groups, split, meta, place, *refs):
+    scale, cot, up_in, down_in, normed, middle, norm = refs[:7]
+    after, w_grad, grad_out, n_grad = refs[7:11]
+    low, low_t, norm_t, total, total_grad = refs[11:]
     step = pl.program_id(0)
+
+    def start_grad(j):
+        return cot[pl.ds(j * CH, CH)].astype(f32) * scale[meta[6 + j]]
 
     @pl.when(step == 0)
     def _():
-        for index, part in enumerate((left, own, right)):
-            for j in range(3):
-                values = part[pl.ds(j * CH, CH)]
-                ext[3 * index + j] = values
-                ext_t[3 * index + j] = values.T
+        n_grad[...] = jnp.zeros_like(n_grad)
         for j in range(3):
-            rounded = grad_in[pl.ds(j * CH, CH)].astype(bf16)
-            low[j] = rounded
+            rows = pl.ds(j * CH, CH)
+            rounded = start_grad(j).astype(bf16)
+            low[rows] = rounded
             low_t[:, j * CH : (j + 1) * CH] = rounded.T
+            norm_t[:, j * CH : (j + 1) * CH] = normed[rows].T
+        total[...] = jnp.zeros_like(total)
+        total_grad[...] = jnp.zeros_like(total_grad)
+
+    up_w = up_in[:, 0].reshape(D, D)
+    down_w = down_in[:, 0].reshape(D, D)
+    acts, pieces = [], []
+    for j in range(3):
+        rows = pl.ds(j * CH, CH)
+        act, slope = gelu_pair(mm(normed[rows], up_w))
+        act = act.astype(bf16)
+        acts.append(act)
+        total[j] += mm(act, down_w, NT)
+        piece = (mm(low[rows], down_w) * slope).astype(bf16)
+        pieces.append(piece)
+        total_grad[j] += mm(piece, up_w, NT)
+    down_grad = mm(low_t[...], jnp.concatenate(acts, axis=0)).astype(bf16)
+    put_blocks(w_grad, place, step, groups, split, D, down_grad)
+    up_grad = mm(norm_t[...], jnp.concatenate(pieces, axis=0)).astype(bf16)
+    put_blocks(w_grad, place, step, groups, split, 0, up_grad)
+
+    @pl.when(step == groups - 1)
+    def _():
+        for j in range(3):
+            rows = pl.ds(j * CH, CH)
+            values = middle[rows]
+            after[rows] = values + total[j]
+            back, gain_grad, shift_grad = norm_backward(total_grad[j], values, norm[2:3])
+            grad_out[rows] = start_grad(j) + back
+            n_grad[2:3] += gain_grad
+            n_grad[3:4] += shift_grad
+
+
+def mlp_last(weights, meta, place, scale, cot, normed, middle, norm, groups, split):
+    rows = normed.shape[0]
+    const = lambda s, *_: (0, 0)
+    full = pl.BlockSpec((rows, D), const)
+    (up_w, up_at), (down_w, down_at) = weights
+    places = split * groups
+    return pl.pallas_call(
+        functools.partial(mlp_last_kernel, groups, split),
+        grid_spec=pltpu.PrefetchScalarGridSpec(
+            num_scalar_prefetch=2,
+            grid=(groups,),
+            in_specs=[smem(), full]
+            + [weight_spec(up_w, up_at), weight_spec(down_w, down_at)]
+            + [full, full, pl.BlockSpec((4, D), const)],
+            out_specs=[
+                full,
+                pl.BlockSpec((places, D // split, 2 * D), lambda s, *_: (0, 0, 0)),
+                full,
+                pl.BlockSpec((8, D), const),
+            ],
+            scratch_shapes=[
+                pltpu.VMEM((rows, D), bf16),
+                pltpu.VMEM((D, rows), bf16),
+                pltpu.VMEM((D, rows), bf16),
+                pltpu.VMEM((3, CH, D), f32),
+                pltpu.VMEM((3, CH, D), f32),
+            ],
+        ),
+        out_shape=[
+            kept_out((rows, D), f32),
+            kept_out((places, D // split, 2 * D), bf16),
+            kept_out((rows, D), f32),
+            jax.ShapeDtypeStruct((8, D), f32),
+        ],
+        compiler_params=params(28),
+        cost_estimate=pl.CostEstimate(
+            flops=30_000_000_000, bytes_accessed=18_000_000, transcendentals=0
+        ),
+        name="mlp_last",
+    )(meta, place, scale, cot, *from_hbm(up_w, down_w), normed, middle, norm)
+
+
+def head_rows(values, lane):
+    zero = jnp.zeros_like(values)
+    return [jnp.where(lane == h, values, zero) for h in range(2)]
+
+
+def group_backward(keys, values, queries, grads, lse, delta):
+    scores = mm(keys, queries, NT)
+    grad_p = mm(values, grads, NT)
+    probability = jnp.exp2(scores - lse)
+    grad_s = (probability * (grad_p - delta)).astype(bf16)
+    dv = mm(probability.astype(bf16), grads)
+    dk = mm(grad_s, queries) * LN2
+    both = jnp.concatenate([dk.astype(bf16), dv.astype(bf16)], axis=1)
+    return both, mm(keys.T, grad_s)
+
+
+def pick_heads(dq_t, index):
+    begin = 2 * CH * index
+    return jnp.concatenate(
+        [dq_t[:HEAD_DIM, begin : begin + CH], dq_t[HEAD_DIM:, begin + CH : begin + 2 * CH]], axis=0
+    )
+
+
+def group_inputs(meta, q_i, lse_i, g_t, delta_t):
+    lane = lax.broadcasted_iota(jnp.int32, (CH, PAIR), 1) // HEAD_DIM
+    queries, grads, lse, delta = [], [], [], []
+    for t in range(3):
+        j = meta[9 + t]
+        queries.append(head_rows(q_i[0, j], lane))
+        grads.append(head_rows(g_t[t], lane))
+        lse.append([lse_i[0, j, h : h + 1] for h in range(2)])
+        delta.append([delta_t[t][h : h + 1] for h in range(2)])
+    found = []
+    for parts in ((0,), (1, 2)):
+        found.append(
+            tuple(
+                jnp.concatenate([row for t in parts for row in rows[t]], axis=axis)
+                for rows, axis in ((queries, 0), (grads, 0), (lse, 1), (delta, 1))
+            )
+        )
+    return found
+
+
+def key_range(ref, begin, count):
+    return ref[0, pl.ds(begin, count)].reshape(count * CH, PAIR)
+
+
+def attn_backward_far_kernel(groups, meta, *refs):
+    w_in, grad_in, small, q_i, k_i, v_i, o_i, lse_i = refs[:8]
+    d_left, d_own, d_right, dq_o, dkv_o, g_o, delta_o, small_o = refs[8:16]
+    low, d_ext = refs[16:]
+    step = pl.program_id(0)
+
+    @pl.when(step == 0)
+    def _():
+        for t in range(3):
+            rows = pl.ds(pl.multiple_of(meta[9 + t] * CH, CH), CH)
+            low[t] = grad_in[rows].astype(bf16)
         d_ext[...] = jnp.zeros_like(d_ext)
         small_o[...] = small[...]
 
     def weight(begin, end):
         return w_in[:, 0, :, begin:end].reshape(D, end - begin)
 
-    slots = meta[2]
-
-    def prepare(slot, carry):
-        for i in range(SLOT):
-            k_t[slot, :, i * CH : (i + 1) * CH] = k_i[0, slot * SLOT + i].T
-        dk[slot] = jnp.zeros((LEN, PAIR), f32)
-        dv[slot] = jnp.zeros((LEN, PAIR), f32)
-        return carry
-
-    lax.fori_loop(0, slots, prepare, 0)
-    lane = lax.broadcasted_iota(jnp.int32, (CH, PAIR), 1)
-
-    def chunk(j, carry):
-        slot = meta[3 + j]
-        query = q_i[0, j]
-        out = o_i[0, j]
-        keys = k_i[0, pl.ds(slot * SLOT, SLOT)].reshape(LEN, PAIR)
-        values = v_i[0, pl.ds(slot * SLOT, SLOT)].reshape(LEN, PAIR)
-        grad_out = mm(low[j], weight(3 * PAIR, D))
-        grad_low = grad_out.astype(bf16)
-        product = (grad_low.astype(f32) * out.astype(f32)).T
-        delta = jnp.sum(product.reshape(2, HEAD_DIM, CH), axis=1)
-        p_all = []
-        ds_all = []
-        q_all = []
-        g_all = []
-        dq_t = []
+    grad_low = mm(low[...].reshape(3 * CH, D), weight(3 * PAIR, D)).astype(bf16)
+    g_t = [grad_low[t * CH : (t + 1) * CH] for t in range(3)]
+    delta_t = []
+    for t in range(3):
+        g_o[0, t] = g_t[t]
+        product = (g_t[t].astype(f32) * o_i[0, meta[9 + t]].astype(f32)).T
+        rows = [
+            jnp.sum(product[h * HEAD_DIM : (h + 1) * HEAD_DIM], axis=0, keepdims=True)
+            for h in range(2)
+        ]
         for h in range(2):
-            q_h = jnp.where((lane // HEAD_DIM) == h, query, jnp.zeros_like(query))
-            g_h = jnp.where((lane // HEAD_DIM) == h, grad_low, jnp.zeros_like(grad_low))
-            probability = jnp.exp2(mm(keys, q_h, NT) - lse_i[0, j, h : h + 1])
-            grad_p = mm(values, g_h, NT)
-            grad_s = (probability * (grad_p - delta[h : h + 1])).astype(bf16)
-            dq_t.append(mm(k_t[slot, h * HEAD_DIM : (h + 1) * HEAD_DIM, :], grad_s))
-            dv[slot] += mm(probability.astype(bf16), g_h)
-            dk[slot] += mm(grad_s, q_h)
-        dq = jnp.concatenate(dq_t, axis=0).T * (1.0 / math.sqrt(HEAD_DIM))
-        dq_low = dq.astype(bf16)
-        dq_all[pl.ds(j * CH, CH)] = dq_low
-        d_ext[3 + j] += mm(dq_low, weight(0, PAIR), NT)
-        return carry
-
-    lax.fori_loop(0, 3, chunk, 0)
-    out_grad = mm(low_t[...], o_i[0].reshape(3 * CH, PAIR)).astype(bf16)
-    put_blocks(w_grad, place, step, groups, split, 3 * PAIR, out_grad)
-    own_t = jnp.concatenate([ext_t[3], ext_t[4], ext_t[5]], axis=1)
-    q_grad = mm(own_t, dq_all[...]).astype(bf16)
-    put_blocks(w_grad, place, step, groups, split, 0, q_grad)
-
-    def collect(slot, running):
-        begin = meta[slot]
-        kv_w = weight(PAIR, 3 * PAIR)
-        for i in range(SLOT):
-            rows = pl.ds(i * CH, CH)
-            both = jnp.concatenate(
-                [(dk[slot, rows] * LN2).astype(bf16), dv[slot, rows].astype(bf16)], axis=1
-            )
-            d_ext[begin + i] += mm(both, kv_w, NT)
-            running = running + mm(ext_t[begin + i], both)
-        return running
-
-    kv_grad = lax.fori_loop(0, slots, collect, jnp.zeros((D, 2 * PAIR), f32))
-    put_blocks(w_grad, place, step, groups, split, PAIR, kv_grad.astype(bf16))
+            delta_o[0, t, h : h + 1] = rows[h]
+        delta_t.append(jnp.concatenate(rows, axis=0))
+    one, two = group_inputs(meta, q_i, lse_i, g_t, delta_t)
+    kv_w = weight(PAIR, 3 * PAIR)
+    both, dq_t = group_backward(
+        key_range(k_i, meta[12], 3), key_range(v_i, meta[12], 3), *one
+    )
+    dkv_o[0, 0:3] = both.reshape(3, CH, 2 * PAIR)
+    d_ext[pl.ds(meta[16], 3)] += mm(both, kv_w, NT).reshape(3, CH, D)
+    dq_o[0, 0] = pick_heads(dq_t, 0)
+    both, dq_t = group_backward(
+        key_range(k_i, meta[13], 2), key_range(v_i, meta[13], 2), *two
+    )
+    dkv_o[0, 3:5] = both.reshape(2, CH, 2 * PAIR)
+    d_ext[pl.ds(meta[17], 2)] += mm(both, kv_w, NT).reshape(2, CH, D)
+    dq_o[0, 1] = pick_heads(dq_t, 0)
+    dq_o[0, 2] = pick_heads(dq_t, 1)
 
     @pl.when(step == groups - 1)
     def _():
@@ -678,75 +765,167 @@
             d_right[rows] = d_ext[6 + j].astype(bf16)
 
 
-def attn_backward(
-    weight, meta, place, left, own, right, grad_in, kept, groups, split, small, after=()
-):
-    rows = own.shape[0]
-    q_i, k_i, v_i, o_i, lse_i = kept
+def attn_backward_near_kernel(groups, split, halves, meta, base, *refs):
+    w_in, left, own, right, grad_in, q_i, k_i, v_i, o_i, lse_i = refs[:10]
+    dq_i, dkv_i, g_i, delta_i, small = refs[10:15]
+    w_grads = refs[15 : 15 + halves]
+    d_own, small_o, ext_t, low_t, total, dq_all, w_all = refs[15 + halves :]
+    step = pl.program_id(0)
+
+    @pl.when(step == 0)
+    def _():
+        for index, part in enumerate((left, own, right)):
+            for j in range(3):
+                ext_t[3 * index + j] = part[pl.ds(j * CH, CH)].T
+        for j in range(3):
+            low_t[:, j * CH : (j + 1) * CH] = grad_in[pl.ds(j * CH, CH)].astype(bf16).T
+        total[...] = jnp.zeros_like(total)
+        small_o[...] = small[...]
+
+    def weight(begin, end):
+        return w_in[:, 0, :, begin:end].reshape(D, end - begin)
+
+    def columns(begin, count):
+        return jnp.concatenate([ext_t[begin + i] for i in range(count)], axis=1)
+
+    g_t = [g_i[0, t] for t in range(3)]
+    delta_t = [delta_i[0, t] for t in range(3)]
+    one, two = group_inputs(meta, q_i, lse_i, g_t, delta_t)
+    kv_w = weight(PAIR, 3 * PAIR)
+    first, dq_one = group_backward(
+        key_range(k_i, meta[14], 1), key_range(v_i, meta[14], 1), *one
+    )
+    second, dq_two = group_backward(
+        key_range(k_i, meta[15], 2), key_range(v_i, meta[15], 2), *two
+    )
+    total[meta[18] - 3] += mm(first, kv_w, NT)
+    total[pl.ds(meta[19] - 3, 2)] += mm(second, kv_w, NT).reshape(2, CH, D)
+    for t, part in enumerate((pick_heads(dq_one, 0), pick_heads(dq_two, 0), pick_heads(dq_two, 1))):
+        whole = ((dq_i[0, t] + part).T * (1.0 / math.sqrt(HEAD_DIM))).astype(bf16)
+        j = meta[9 + t]
+        dq_all[pl.ds(pl.multiple_of(j * CH, CH), CH)] = whole
+        total[j] += mm(whole, weight(0, PAIR), NT)
+    out_grad = mm(low_t[...], o_i[0].reshape(3 * CH, PAIR)).astype(bf16)
+    w_all[:, 3 * PAIR :] = out_grad
+    q_grad = mm(columns(3, 3), dq_all[...]).astype(bf16)
+    w_all[:, :PAIR] = q_grad
+    kv_grad = (
+        mm(columns(meta[16], 3), dkv_i[0, 0:3].reshape(3 * CH, 2 * PAIR))
+        + mm(columns(meta[17], 2), dkv_i[0, 3:5].reshape(2 * CH, 2 * PAIR))
+        + mm(columns(meta[18], 1), first)
+        + mm(columns(meta[19], 2), second)
+    )
+    w_all[:, PAIR : 3 * PAIR] = kv_grad.astype(bf16)
+    high = D // split
+    for apart in range(split):
+        rows = pl.ds(pl.multiple_of((base[0] ^ apart) * high, high), high)
+        w_grads[apart % halves][(apart // halves) * groups + step] = w_all[rows]
+
+    @pl.when(step == groups - 1)
+    def _():
+        d_own[...] = total[...].reshape(3 * CH, D)
+
+
+def attn_backward_far(weight, meta, grad_in, kept, groups, small, after=()):
+    rows = grad_in.shape[0]
     const = lambda s, *_: (0, 0)
     pair = lambda s, *_: (s, 0, 0, 0)
     full = pl.BlockSpec((rows, D), const)
+    three = pl.BlockSpec((1, 3, CH, PAIR), pair)
+    eight = pl.BlockSpec((1, 2 * SLOT, CH, PAIR), pair)
+    lines = pl.BlockSpec((1, 3, 8, CH), pair)
+    tiny = pl.BlockSpec((8, D), const)
+    return pl.pallas_call(
+        after_operands(functools.partial(attn_backward_far_kernel, groups), 1, len(after)),
+        grid_spec=pltpu.PrefetchScalarGridSpec(
+            num_scalar_prefetch=1,
+            grid=(groups,),
+            in_specs=[hbm()] * len(after)
+            + [weight_spec(*weight), full, tiny, three, eight, eight, three, lines],
+            out_specs=[
+                full,
+                full,
+                full,
+                pl.BlockSpec((1, 3, PAIR, CH), pair),
+                pl.BlockSpec((1, 5, CH, 2 * PAIR), pair),
+                three,
+                lines,
+                tiny,
+            ],
+            scratch_shapes=[
+                pltpu.VMEM((3, CH, D), bf16),
+                pltpu.VMEM((9, CH, D), f32),
+            ],
+        ),
+        out_shape=[
+            jax.ShapeDtypeStruct((rows, D), bf16),
+            jax.ShapeDtypeStruct((rows, D), f32),
+            jax.ShapeDtypeStruct((rows, D), bf16),
+            jax.ShapeDtypeStruct((groups, 3, PAIR, CH), f32),
+            jax.ShapeDtypeStruct((groups, 5, CH, 2 * PAIR), bf16),
+            jax.ShapeDtypeStruct((groups, 3, CH, PAIR), bf16),
+            jax.ShapeDtypeStruct((groups, 3, 8, CH), f32),
+            jax.ShapeDtypeStruct((8, D), f32),
+        ],
+        compiler_params=params(28),
+        cost_estimate=pl.CostEstimate(
+            flops=24_000_000_000, bytes_accessed=16_000_000, transcendentals=0
+        ),
+        name="attn_backward_far",
+    )(meta, *from_hbm(*after, weight[0]), grad_in, small, *from_hbm(*kept))
+
+
+def attn_backward_near(weight, meta, base, ext, grad_in, kept, far, groups, split, small, halves):
+    rows = grad_in.shape[0]
+    const = lambda s, *_: (0, 0)
+    pair = lambda s, *_: (s, 0, 0, 0)
+    full = pl.BlockSpec((rows, D), const)
+    three = pl.BlockSpec((1, 3, CH, PAIR), pair)
+    eight = pl.BlockSpec((1, 2 * SLOT, CH, PAIR), pair)
+    lines = pl.BlockSpec((1, 3, 8, CH), pair)
+    tiny = pl.BlockSpec((8, D), const)
     places = split * groups
     return pl.pallas_call(
-        after_operands(
-            functools.partial(attn_backward_kernel, groups, split), 2, len(after)
-        ),
+        functools.partial(attn_backward_near_kernel, groups, split, halves),
         grid_spec=pltpu.PrefetchScalarGridSpec(
             num_scalar_prefetch=2,
             grid=(groups,),
-            in_specs=[hbm()] * len(after)
+            in_specs=[weight_spec(*weight), full, full, full, full, three, eight, eight, three, lines]
             + [
-                weight_spec(*weight),
-                full,
-                full,
-                full,
-                full,
-                pl.BlockSpec((8, D), const),
-                pl.BlockSpec((1, 3, CH, PAIR), pair),
-                pl.BlockSpec((1, 2 * SLOT, CH, PAIR), pair),
-                pl.BlockSpec((1, 2 * SLOT, CH, PAIR), pair),
-                pl.BlockSpec((1, 3, CH, PAIR), pair),
-                pl.BlockSpec((1, 3, 8, CH), pair),
+                pl.BlockSpec((1, 3, PAIR, CH), pair),
+                pl.BlockSpec((1, 5, CH, 2 * PAIR), pair),
+                three,
+                lines,
+                tiny,
             ],
-            out_specs=[
-                pl.BlockSpec((places, D // split, D), lambda s, *_: (0, 0, 0)),
-                full,
-                full,
-                full,
-                pl.BlockSpec((8, D), const),
+            out_specs=[pl.BlockSpec((places // halves, D // split, D), lambda s, *_: (0, 0, 0))]
+            * halves
+            + [full, tiny],
+            scratch_shapes=[
+                pltpu.VMEM((9, D, CH), bf16),
+                pltpu.VMEM((D, rows), bf16),
+                pltpu.VMEM((3, CH, D), f32),
+                pltpu.VMEM((rows, PAIR), bf16),
+                pltpu.VMEM((D, D), bf16),
             ],
-            scratch_shapes=[
-                pltpu.VMEM((9, CH, D), bf16),
-                pltpu.VMEM((9, D, CH), bf16),
-                pltpu.VMEM((3, CH, D), bf16),
-                pltpu.VMEM((D, rows), bf16),
-                pltpu.VMEM((2, PAIR, LEN), bf16),
-                pltpu.VMEM((2, LEN, PAIR), f32),
-                pltpu.VMEM((2, LEN, PAIR), f32),
-                pltpu.VMEM((9, CH, D), f32),
-                pltpu.VMEM((rows, PAIR), bf16),
-            ],
-        ),
-        out_shape=[
-            jax.ShapeDtypeStruct((places, D // split, D), bf16),
-            jax.ShapeDtypeStruct((rows, D), bf16),
-            jax.ShapeDtypeStruct((rows, D), f32),
-            jax.ShapeDtypeStruct((rows, D), bf16),
-            jax.ShapeDtypeStruct((8, D), f32),
-        ],
-        compiler_params=params(58),
+        ),
+        out_shape=[jax.ShapeDtypeStruct((places // halves, D // split, D), bf16)] * halves
+        + [jax.ShapeDtypeStruct((rows, D), f32), jax.ShapeDtypeStruct((8, D), f32)],
+        compiler_params=params(28),
         cost_estimate=pl.CostEstimate(
-            flops=45_000_000_000, bytes_accessed=24_000_000, transcendentals=0
-        ),
-        name="attn_backward",
-    )(meta, place, *after, weight[0], left, own, right, grad_in, small, q_i, k_i, v_i, o_i, lse_i)
-
-
-def entry_backward_kernel(grad_in, d_own, d_left, d_right, source, norm, ids, grad_out, small):
+            flops=20_000_000_000, bytes_accessed=22_000_000, transcendentals=0
+        ),
+        name="attn_backward_near",
+    )(meta, base, *from_hbm(weight[0]), *ext, grad_in, *from_hbm(*kept), *far, small)
+
+
+def entry_backward_kernel(
+    grad_in, d_own, d_near, d_left, d_right, source, norm, ids, grad_out, small
+):
     small[...] = jnp.zeros_like(small)
     for j in range(3):
         rows = pl.ds(j * CH, CH)
-        arrived = d_own[rows] + d_left[rows].astype(f32) + d_right[rows].astype(f32)
+        arrived = d_own[rows] + d_near[rows] + d_left[rows].astype(f32) + d_right[rows].astype(f32)
         back, gain_grad, shift_grad = norm_backward(arrived, source[rows], norm[0:1])
         values = grad_in[rows] + back
         grad_out[rows] = values
@@ -761,14 +940,14 @@
         small[8:40] += mm(chosen, high) + mm(chosen, middle) + mm(chosen, low)
 
 
-def entry_backward(grad_in, d_own, d_left, d_right, source, norm, ids, after=()):
+def entry_backward(grad_in, d_own, d_near, d_left, d_right, source, norm, ids, after=()):
     rows = grad_in.shape[0]
     return pl.pallas_call(
         after_operands(entry_backward_kernel, 0, len(after)),
-        in_specs=[hbm()] * len(after) + [vmem()] * 7,
+        in_specs=[hbm()] * len(after) + [vmem()] * 8,
         out_specs=[vmem()] * 2,
         out_shape=[
-            jax.ShapeDtypeStruct((rows, D), f32),
+            kept_out((rows, D), f32),
             jax.ShapeDtypeStruct((40, D), f32),
         ],
         compiler_params=pltpu.CompilerParams(vmem_limit_bytes=40 * 1024 * 1024),
@@ -776,7 +955,24 @@
             flops=100_000_000, bytes_accessed=9_000_000, transcendentals=0
         ),
         name="entry_backward",
-    )(*after, grad_in, d_own, d_left, d_right, source, norm, ids)
+    )(*after, grad_in, d_own, d_near, d_left, d_right, source, norm, ids)
+
+
+def backward_plan(my_mp, row_start, first_seq, chunk_seq):
+    lead = jnp.where(my_mp < 2, 0, 2)
+    late_one = my_mp % 2 == 0
+    late_two = my_mp < 2
+    found = [lead, 1, 2 - lead]
+    lead_seq = jnp.where(my_mp < 2, chunk_seq[0], chunk_seq[2])
+    shifts = [
+        (lead_seq, jnp.where(late_one, 1, 0)),
+        (chunk_seq[1], jnp.where(late_two, 2, 0)),
+        (lead_seq, jnp.where(late_one, 0, 3)),
+        (chunk_seq[1], jnp.where(late_two, 0, 2)),
+    ]
+    found += [(seq - first_seq) * SLOT + shift for seq, shift in shifts]
+    found += [3 + (seq * LEN - row_start) // CH + shift for seq, shift in shifts]
+    return [jnp.asarray(entry) for entry in found]
 
 
 def shards(
@@ -825,12 +1021,12 @@
         ]
         + [seq - first_seq for seq in chunk_seq]
         + chunk_seq
+        + backward_plan(my_mp, row_start, first_seq, chunk_seq)
     ).astype(jnp.int32)
     in_order = jnp.arange(split * groups, dtype=jnp.int32)
-    if small:
-        place, owner = block_places(my_dp)
-    else:
-        place = owner = in_order
+    owner = block_owners(my_dp) if small else in_order
+    base = jnp.where(small, my_dp, 0).astype(jnp.int32)[None]
+    halves = 2 if small else 1
 
     attn_mine = []
     mlp_mine = []
@@ -844,11 +1040,17 @@
             jnp.concatenate([up_weight[layer], down_weight[layer].T], axis=1).astype(bf16)
         )
     both_mine = jnp.concatenate([attn_mine[1], mlp_mine[1]], axis=1)
-    ids_left, ids_right = shift_right(token_ids), shift_left(token_ids)
     if small:
-        attn_sent = [flip(attn_mine[0], bits) for bits in (1, 2, 3)]
-        attn_sent, (ids_left, ids_right) = tie(attn_sent, (ids_left, ids_right))
-        attn_z = jnp.stack([attn_mine[0]] + list(attn_sent))
+        lines = row_count // D + (row_count % D > 0)
+        ids_low = jnp.pad(token_ids.astype(bf16), (0, lines * D - row_count)).reshape(lines, D)
+        first_mine = jnp.concatenate([attn_mine[0], ids_low], axis=0)
+        first_z = gather_z(first_mine)
+        attn_z = first_z[:, :high]
+        ids_z = first_z[:, high:].reshape(4, lines * D)[:, :row_count].astype(jnp.int32)
+        ids_left = ids_z[my_mp ^ jnp.maximum(my_mp - 1, 0)]
+        ids_right = ids_z[my_mp ^ jnp.minimum(my_mp + 1, mp - 1)]
+    else:
+        ids_left, ids_right = shift_right(token_ids), shift_left(token_ids)
     ids_ext = jnp.concatenate([ids_left, token_ids, ids_right])
     seq_ext = (row_start - row_count + jnp.arange(3 * row_count, dtype=jnp.int32)) // LEN
     letters = (ids_ext[:, None] == jnp.arange(VOCAB, dtype=jnp.int32)[None, :]).astype(f32)
@@ -885,7 +1087,7 @@
     for layer in range(LAYERS):
         last = layer == LAYERS - 1
         outs, w_attn = attn_forward(
-            attn_w[layer], meta, owner, *ext, resid, norm_params[layer], groups
+            attn_w[layer], meta, owner, *ext, resid, norm_params[layer], groups, layer + 1 < LAYERS
         )
         middle, normed = outs[:2]
         if small and layer == 0:
@@ -893,38 +1095,42 @@
             both_found = gather_dp(jnp.stack([both_mine] + list(both_sent)))
             attn_w.append(both_found)
             mlp_w = [((mlp_found, 0), (mlp_found, 1)), ((both_found, 1), (both_found, 2))]
-        next_norm = norm_params[min(layer + 1, LAYERS - 1)]
-        mlp_outs, w_mlp = mlp_forward(
-            mlp_w[layer], owner, normed, middle, next_norm, groups, last
-        )
+        w_mlp = mlp_w[layer]
+        if layer + 1 < LAYERS:
+            mlp_outs, w_mlp = mlp_forward(
+                w_mlp, owner, normed, middle, norm_params[layer + 1], groups
+            )
         kept.append((ext, resid, middle, normed, outs[2:], mlp_outs[1:3], (w_attn, 0), w_mlp))
-        resid = mlp_outs[0]
-        if not last:
-            following = mlp_outs[3]
+        if layer + 1 < LAYERS:
+            resid, following = mlp_outs[0], mlp_outs[3]
             ext = (shift_right(following), following, shift_left(following))
-    activations = resid
 
     norm_grads = [[None] * 4 for _ in range(LAYERS)]
     attn_grads = [None] * LAYERS
     mlp_grads = [None] * LAYERS
-    begin = (importance, cotangent)
     after = ()
     for layer in reversed(range(LAYERS)):
         ext, source, middle, normed, attn_kept, (act, slope), w_attn, w_mlp = kept[layer]
-        mlp_grad, grad_mid, n_grad = mlp_backward(
-            w_mlp,
-            meta,
-            in_order,
-            begin,
-            act,
-            slope,
-            normed,
-            middle,
-            norm_params[layer],
-            groups,
-            split,
-            after,
-        )
+        norm = norm_params[layer]
+        if layer + 1 == LAYERS:
+            activations, mlp_grad, grad_mid, n_grad = mlp_last(
+                w_mlp, meta, in_order, importance, cotangent, normed, middle, norm, groups, split
+            )
+        else:
+            mlp_grad, grad_mid, n_grad = mlp_backward(
+                w_mlp,
+                meta,
+                in_order,
+                begin,
+                act,
+                slope,
+                normed,
+                middle,
+                norm,
+                groups,
+                split,
+                after,
+            )
         after = ()
         if small:
             if layer + 1 < LAYERS:
@@ -935,50 +1141,64 @@
                 above = jnp.concatenate([attn_rows, above], axis=2)
                 above_mine, above_found = scatter_four(above, 1)
                 after = (above,)
-        attn_grad, d_left, d_own, d_right, n_grad = attn_backward(
-            w_attn, meta, place, *ext, grad_mid, attn_kept, groups, split, n_grad, after
+        d_left, d_own, d_right, *far, n_grad = attn_backward_far(
+            w_attn, meta, grad_mid, attn_kept, groups, n_grad, after
         )
         if small and layer + 1 < LAYERS:
-            above_found, (attn_grad, d_left, d_right) = tie(
-                above_found, (attn_grad, d_left, d_right)
-            )
+            above_found, (d_left, d_right) = tie(above_found, (d_left, d_right))
         from_right = shift_left(d_left)
         from_left = shift_right(d_right)
-        if small:
-            attn_held = scatter_core(attn_grad)
+        *attn_grad, d_near, n_grad = attn_backward_near(
+            w_attn, meta, base, ext, grad_mid, attn_kept, far, groups, split, n_grad, halves
+        )
+        (from_left, from_right), (attn_grad, d_near) = tie(
+            (from_left, from_right), (attn_grad, d_near)
+        )
+        after = ()
+        if not small:
+            mlp_grads[layer] = plain_scatter(mlp_grad, dp)
+            attn_grads[layer] = plain_scatter(attn_grad[0], dp)
+        elif layer + 1 == LAYERS:
+            attn_held = scatter_core(*attn_grad)
             attn_mine_rows, attn_found = scatter_four(attn_held, 8)
-            if layer + 1 < LAYERS:
-                above_total = add_four(above_mine, above_found, True)
-                attn_grads[1] = above_total[:, :D]
-                mlp_grads[1] = above_total[:, D:]
-            else:
-                above = mlp_rows
+            above = mlp_rows
             after = (attn_held,)
         else:
-            mlp_grads[layer] = plain_scatter(mlp_grad, dp)
-            attn_grads[layer] = plain_scatter(attn_grad, dp)
+            above_total = add_four(above_mine, above_found, True)
+            attn_grads[1] = above_total[:, :D]
+            mlp_grads[1] = above_total[:, D:]
         norm_grads[layer][2:] = [n_grad[2], n_grad[3]]
         if layer + 1 < LAYERS:
             norm_grads[layer + 1][:2] = [n_grad[0], n_grad[1]]
-        begin = (grad_mid, d_own, from_left, from_right, source, norm_params[layer])
-    after = ()
-    if small:
-        attn_rows = add_four(attn_mine_rows, attn_found, False)
-        below = jnp.concatenate([attn_rows, mlp_rows], axis=2)
-        after = (below,)
-        below_mine, below_found = scatter_four(below, 1)
-    input_grad, reduced = entry_backward(*begin, token_ids[None, :], after)
+        begin = (grad_mid, d_own, d_near, from_left, from_right, source, norm_params[layer])
+    input_grad, reduced = entry_backward(*begin, token_ids[None, :])
     norm_grads[0][:2] = [reduced[0], reduced[1]]
     stacked = jnp.concatenate(
         [jnp.stack([row for rows in norm_grads for row in rows]), reduced[8:40]], axis=0
     )
     if small:
-        stacked = sum_four(stacked + flip(stacked, 4), 8)
-        below_found, stacked = tie(below_found, stacked)
-        stacked = sum_four(stacked, 1)
-        total = add_four(below_mine, below_found, True)
-        attn_grads[0] = total[:, :D]
-        mlp_grads[0] = total[:, D:]
+        rows = D // dp
+        rest = stacked.astype(bf16)
+        rest = (rest.astype(f32) + flip(rest, 4).astype(f32)).astype(bf16)
+        held = scatter_core(*attn_grad).reshape(16 * rows, D)
+        sent = [
+            flip(jnp.concatenate([held[4 * rows * i : 4 * rows * (i + 1)], rest], axis=0), 8 * i)
+            for i in (1, 2, 3)
+        ]
+        mlp_own, mlp_sent = scatter_four(mlp_rows, 1)
+        mlp_sent, sent = tie(mlp_sent, sent)
+        mine = add_four(jnp.concatenate([held[: 4 * rows], rest], axis=0)[None], [p[None] for p in sent], True)
+        held, rest = mine[: 4 * rows].astype(bf16), mine[4 * rows :].astype(bf16)
+        sent = [
+            flip(jnp.concatenate([held[rows * i : rows * (i + 1)], rest], axis=0), i)
+            for i in (1, 2, 3)
+        ]
+        total = add_four(
+            jnp.concatenate([held[:rows], rest], axis=0)[None], [p[None] for p in sent], True
+        )
+        attn_grads[0] = total[:rows]
+        stacked = total[rows:]
+        mlp_grads[0] = add_four(mlp_own, mlp_sent, True)
     else:
         stacked = lax.psum(stacked, ALL)
     norm_grad = stacked[: 4 * LAYERS].reshape(LAYERS, 4, D)

time: 400 us -> 350 us (0.88)
  waiting for transfers between devices: 78.7 us -> 55.6 us
  Pallas kernels: 186 us -> 164 us
  starting transfers between devices: 73.1 us -> 63 us
  other arithmetic: 21.6 us -> 26.8 us
    ppermute x4 -> x3, waiting for transfers between devices: 27.2 us -> 1.18 us  [shift_right(): return lax.ppermute(values, 'mp', [(i, i + 1) for i in range(count - 1)])]
    pallas_call x6 -> x7, Pallas kernels: 134 us -> 122 us  [the longest x2 40.2 us: attn_backward_near(): pl.pallas_call(functools.partial(attn_backward_near_kernel, groups, split...]
    ppermute x4 -> x3, starting transfers between devices: 22 us -> 13.6 us  [shift_right(): return lax.ppermute(values, 'mp', [(i, i + 1) for i in range(count - 1)])]
    pallas_call x2, Pallas kernels: 47.8 us -> 39.8 us  [attn_forward(): pl.pallas_call(functools.partial(attn_forward_kernel, gathered, groups),...]
    ppermute x34 -> x31, waiting for transfers between devices: 28.6 us -> 21.2 us  [permute_all(): return lax.ppermute(values, ALL, [(i, target(i)) for i in range(count)])]
    all_gather x2, waiting for transfers between devices: 11.8 us -> 17.6 us  [gather_dp(): return lax.all_gather(held, 'dp', axis=0, tiled=False)]
    ppermute x4 -> x3, waiting for transfers between devices: 10.9 us -> 15.5 us  [shift_left(): return lax.ppermute(values, 'mp', [(i + 1, i) for i in range(count - 1)])]
    unnamed x85 -> x106, local copies, waits for them, and re-layouts: 2.95 us -> 7.35 us
  transfers between devices with their start and end apart: 46 -> 41, of which waited for: 14 -> 13; matrix products, arithmetic and copies ran while one was open for 9% -> 8% of each run, Pallas kernels for 33% -> 36%
where the time goes in v2:
time: 350 us; the launch traced here: 343 us
  Pallas kernels  164 us (47%)
  starting transfers between devices  63 us (18%)
  waiting for transfers between devices  55.6 us (16%)
  other arithmetic  26.8 us (8%)
  between operations  15.3 us (4%)
  local copies, waits for them, and re-layouts  13.8 us (4%)
  matrix products  4.51 us (1%)
    ppermute x31, starting transfers between devices, permute_all(): return lax.ppermute(values, ALL, [(i, target(i)) for i in range(count)])  44.5 us
    pallas_call x2, Pallas kernels, attn_backward_near(): pl.pallas_call(functools.partial(attn_backward_near_kernel, groups, split...  40.2 us
    pallas_call x2, Pallas kernels, attn_forward(): pl.pallas_call(functools.partial(attn_forward_kernel, gathered, groups),...  39.8 us
    pallas_call x2, Pallas kernels, attn_backward_far(): pl.pallas_call(after_operands(functools.partial(attn_backward_far_kernel,...  29.9 us
    pallas_call x1, Pallas kernels, mlp_last(): pl.pallas_call(functools.partial(mlp_last_kernel, groups, split), grid_sp...  22 us
    ppermute x31, waiting for transfers between devices, permute_all(): return lax.ppermute(values, ALL, [(i, target(i)) for i in range(count)])  21.2 us
    all_gather x2, waiting for transfers between devices, gather_dp(): return lax.all_gather(held, 'dp', axis=0, tiled=False)  17.6 us
    pallas_call x1, Pallas kernels, mlp_backward(): pl.pallas_call(after_operands(functools.partial(mlp_backward_kernel, grou...  16.1 us
  transfers between devices with their start and end apart: 41, of which 13 were waited for; matrix products, arithmetic and copies ran while one was open for 8% of the time, Pallas kernels for 36%

profile of v2, /device:TPU:0, one launch (start us, length us, event | category | flops | bytes accessed | tf_op | source)
XLA Modules:
  0.0 343.4 jit_solution(737826801722998659)
XLA Ops:
  11.1 4.1 %collective-permute-start.1 = (bf16[66,512]{1,0:T(8,128)(2,1)S(1)}, bf16[66,512]{1,0:T(8,128)(2,1)S(1)}, u32[]{:S(2)}, u32[]{:S(2)}) collective-permute-start(bf16[66,512]{1,0:T(8,128)(2,1)S(1)} %get-tuple-element.339), channel_id=1, source_target_pairs={{0,2},{1,3},{2,0},{3,1},{4,6},{5,7},{6,4},{7,5},{8,10},{9,11},{10,... | collective-permute-start | bytes 202760 | tf_op jit(solution)/shard_map/ppermute | solution.py:136
  20.4 2.1 fusion.13
  23.0 3.5 %collective-permute-start.5 = (bf16[64,1024]{1,0:T(8,128)(2,1)S(1)}, bf16[64,1024]{1,0:T(8,128)(2,1)S(1)}, u32[]{:S(2)}, u32[]{:S(2)}) collective-permute-start(bf16[64,1024]{1,0:T(8,128)(2,1)S(1)} %pad_maximum_fusion.16), channel_id=1, source_target_pairs={{0,3},{1,2},{2,1},{3,0},{4,7},{5,6},{6,5},{7,4},{8,11},{9,10},{10,... | collective-permute-start | bytes 393224 | tf_op jit(solution)/shard_map/ppermute | solution.py:136
  27.4 2.4 collective-permute-start.8
  30.5 2.4 fusion.44
  38.1 2.2 collective-permute-done.7
  41.8 2.2 pad_maximum_fusion.1.refs_0_
  46.5 3.5 %collective-permute-start.11 = (bf16[64,1536]{1,0:T(8,128)(2,1)S(1)}, bf16[64,1536]{1,0:T(8,128)(2,1)S(1)}, u32[]{:S(2)}, u32[]{:S(2)}) collective-permute-start(bf16[64,1536]{1,0:T(8,128)(2,1)S(1)} %pad_maximum_fusion.11), channel_id=1, source_target_pairs={{0,3},{1,2},{2,1},{3,0},{4,7},{5,6},{6,5},{7,4},{8,11},{9,10},{10,... | collective-permute-start | bytes 589832 | tf_op jit(solution)/shard_map/ppermute | solution.py:136
  52.2 20.9 %attn_forward.2 = (f32[768,512]{1,0:T(8,128)}, bf16[768,512]{1,0:T(8,128)(2,1)}, bf16[4,3,256,128]{3,2,1,0:T(8,128)(2,1)}, bf16[4,8,256,128]{3,2,1,0:T(8,128)(2,...) custom-call(s32[20]{0:T(128)S(1)} %stack.151.meta.refs_0_, ...), custom_call_target="tpu_custom_call" | custom-call | flops 28999999488 | bytes 14000000 | tf_op jit(solution)/shard_map/attn_forward/pallas_call | solution.py:342
  74.2 6.8 %all-gather.7.cloned.1.call-done = bf16[32,64,1024]{2,1,0:T(8,128)(2,1)} async-done(((bf16[4,64,1024]{2,1,0:T(8,128)(2,1)}), bf16[32,64,1024]{2,1,0:T(8,128)(2,1)}) %all-gather.7.cloned.1.call-update) | async-done | bytes 4194320 | tf_op jit(solution)/shard_map/all_gather | solution.py:173
  81.0 13.5 %mlp_forward.1 = (f32[768,512]{1,0:T(8,128)}, bf16[4,768,512]{2,1,0:T(8,128)(2,1)}, bf16[4,768,512]{2,1,0:T(8,128)(2,1)}, bf16[768,512]{1,0:T(8,128)(2,1)S(1)}) custom-call(s32[32]{0:T(128)S(1)} %fusion.25.table, bf16[8,4,64,1024]{3,2,1,0:T(8,128)(2,1)} %bitcast.175, bf16[8,4,64,1024]{3,2,1,0:T(8,128)(2,1)} %bitcast.176, ...), custom_call_target="tpu_custom_call" | custom-call | flops 15000000512 | bytes 18000000 | tf_op jit(solution)/shard_map/mlp_forward/pallas_call | solution.py:441
  95.9 4.8 %collective-permute-start.13 = (bf16[768,512]{1,0:T(8,128)(2,1)S(1)}, bf16[768,512]{1,0:T(8,128)(2,1)S(1)}, u32[]{:S(2)}, u32[]{:S(2)}) collective-permute-start(bf16[768,512]{1,0:T(8,128)(2,1)S(1)} %get-tuple-element.136.refs_2_), channel_id=1, source_target_pairs={{0,1},{1,2},{2,3},{4,5},{5,6},{6,7},{8,9},{9,10},{10,11},{12,13},{... | collective-permute-start | bytes 2359304 | tf_op jit(solution)/shard_map/ppermute | solution.py:204
  100.6 15.5 %collective-permute-done.14.refs_3_ = bf16[768,512]{1,0:T(8,128)(2,1)S(1)} collective-permute-done((bf16[768,512]{1,0:T(8,128)(2,1)S(1)}, bf16[768,512]{1,0:T(8,128)(2,1)S(1)}, u32[]{:S(2)}, u32[]{:S(2)}) %collective-permute-start.14) | collective-permute-done | bytes 786464 | tf_op jit(solution)/shard_map/ppermute | solution.py:209
  118.3 10.8 %all-gather.5.cloned.1.call-done = bf16[32,64,1536]{2,1,0:T(8,128)(2,1)} async-done(((bf16[4,64,1536]{2,1,0:T(8,128)(2,1)}), bf16[32,64,1536]{2,1,0:T(8,128)(2,1)}) %all-gather.5.cloned.1.call-update) | async-done | bytes 6291472 | tf_op jit(solution)/shard_map/all_gather | solution.py:173
  131.6 18.9 %attn_forward.3 = (f32[768,512]{1,0:T(8,128)S(1)}, bf16[768,512]{1,0:T(8,128)(2,1)S(1)}, bf16[4,3,256,128]{3,2,1,0:T(8,128)(2,1)}, bf16[4,8,256,128]{3,2,1,0:T(8...) custom-call(s32[20]{0:T(128)S(1)} %stack.151.meta.refs_0_, ...), custom_call_target="tpu_custom_call" | custom-call | flops 28999999488 | bytes 14000000 | tf_op jit(solution)/shard_map/attn_forward/pallas_call | solution.py:342
  150.5 22.0 %mlp_last.1 = (f32[768,512]{1,0:T(8,128)}, bf16[32,64,1024]{2,1,0:T(8,128)(2,1)}, f32[768,512]{1,0:T(8,128)}, f32[8,512]{1,0:T(8,128)S(1)}) custom-call(s32[20]{0:T(128)S(1)} %stack.151.meta.refs_0_, s32[32]{0:T(128)S(1)} %iota.26.place, f32[3]{0:T(128)S(1)} %copy-done.14, bf16[768,512]{1,0:T(8,128)(2,1)S(1)} %copy-done.8, ...), custom_call_target="tpu_custom_call" | custom-call | flops 30000001024 | bytes 18000000 | tf_op jit(solution)/shard_map/mlp_last/pallas_call | solution.py:630
  174.1 14.7 %attn_backward_far.2 = (bf16[768,512]{1,0:T(8,128)(2,1)S(1)}, f32[768,512]{1,0:T(8,128)S(1)}, bf16[768,512]{1,0:T(8,128)(2,1)S(1)}, f32[4,3,128,256]{3,2,1,0:T(8...) custom-call(s32[20]{0:T(128)S(1)} %stack.151.meta.refs_0_, ...), custom_call_target="tpu_custom_call" | custom-call | flops 24000000000 | bytes 16000000 | tf_op jit(solution)/shard_map/attn_backward_far/pallas_call | solution.py:838
  188.8 5.2 %collective-permute-start.15 = (bf16[768,512]{1,0:T(8,128)(2,1)S(1)}, bf16[768,512]{1,0:T(8,128)(2,1)S(1)}, u32[]{:S(2)}, u32[]{:S(2)}) collective-permute-start(bf16[768,512]{1,0:T(8,128)(2,1)S(1)} %get-tuple-element.148), channel_id=1, source_target_pairs={{0,1},{1,2},{2,3},{4,5},{5,6},{6,7},{8,9},{9,10},{10,11},{12,13},{... | collective-permute-start | bytes 2359304 | tf_op jit(solution)/shard_map/ppermute | solution.py:204
  195.7 19.6 %attn_backward_near.2 = (bf16[16,64,512]{2,1,0:T(8,128)(2,1)S(1)}, bf16[16,64,512]{2,1,0:T(8,128)(2,1)S(1)}, f32[768,512]{1,0:T(8,128)S(1)}, f32[8,512]{1,0:T(8,128)S(1)}) custom-call(s32[20]{0:T(128)S(1)} %stack.151.meta.refs_0_, s32[1]{0:T(128)} %bitcast.46.base, bf16[8,4,64,1536]{3,2,1,0:T(8,128)(2,1)} %bitcast.174, bf16[768,512]{1,0:T(8,128)(2,1)S(1)} %copy-done.13, ...), custom_call_target="tpu_custom_call" | custom-call | flops 20000000000 | bytes 22000000 | tf_op jit(solution)/shard_map/attn_backward_near/pallas_call | solution.py:888
  215.6 2.6 collective-permute-done.17
  222.1 16.1 %mlp_backward.1 = (bf16[32,64,1024]{2,1,0:T(8,128)(2,1)}, f32[768,512]{1,0:T(8,128)}, f32[8,512]{1,0:T(8,128)S(1)}) custom-call(s32[20]{0:T(128)S(1)} %stack.151.meta.refs_0_, s32[32]{0:T(128)S(1)} %iota.30.refs_1_, bf16[16,64,512]{2,1,0:T(8,128)(2,1)} %copy-done.22, f32[768,512]{1,0:T(8,128)S(1)} %copy-done.19, f32[768,512]{1,0:T(8,128)S(1)} %get-tuple-element.160.refs_4_, ...), custom_call_target="tpu_custom_call" | custom-call | flops 20000000000 | bytes 20000000 | tf_op jit(solution)/shard_map/mlp_backward/pallas_call | solution.py:537
  240.8 3.4 collective-permute-start.23
  247.3 15.2 %attn_backward_far.3 = (bf16[768,512]{1,0:T(8,128)(2,1)S(1)}, f32[768,512]{1,0:T(8,128)S(1)}, bf16[768,512]{1,0:T(8,128)(2,1)S(1)}, f32[4,3,128,256]{3,2,1,0:T(8...) custom-call(s32[20]{0:T(128)S(1)} %stack.151.meta.refs_0_, ...), custom_call_target="tpu_custom_call" | custom-call | flops 24000000000 | bytes 16000000 | tf_op jit(solution)/shard_map/attn_backward_far/pallas_call | solution.py:838
  262.6 3.7 %collective-permute-start.24 = (bf16[768,512]{1,0:T(8,128)(2,1)S(1)}, bf16[768,512]{1,0:T(8,128)(2,1)S(1)}, u32[]{:S(2)}, u32[]{:S(2)}) collective-permute-start(bf16[768,512]{1,0:T(8,128)(2,1)S(1)} %get-tuple-element.183), channel_id=1, source_target_pairs={{0,1},{1,2},{2,3},{4,5},{5,6},{6,7},{8,9},{9,10},{10,11},{12,13},{... | collective-permute-start | bytes 2359304 | tf_op jit(solution)/shard_map/ppermute | solution.py:204
  267.6 20.6 %attn_backward_near.3 = (bf16[16,64,512]{2,1,0:T(8,128)(2,1)S(1)}, bf16[16,64,512]{2,1,0:T(8,128)(2,1)}, f32[768,512]{1,0:T(8,128)S(1)}, f32[8,512]{1,0:T(8,128)S(1)}) custom-call(s32[20]{0:T(128)S(1)} %stack.151.meta.refs_0_, s32[1]{0:T(128)} %bitcast.46.base, bf16[8,4,64,512]{3,2,1,0:T(8,128)(2,1)} %get-tuple-element.173.refs_2_.refs_0_, ...), custom_call_target="tpu_custom_call" | custom-call | flops 20000000000 | bytes 22000000 | tf_op jit(solution)/shard_map/attn_backward_near/pallas_call | solution.py:888
  289.4 2.8 entry_backward.1
  301.9 4.2 %collective-permute-start.30 = (bf16[1,64,1024]{2,1,0:T(8,128)(2,1)}, bf16[1,64,1024]{2,1,0:T(8,128)(2,1)S(1)}, u32[]{:S(2)}, u32[]{:S(2)}) collective-permute-start(bf16[1,64,1024]{2,1,0:T(8,128)(2,1)} %get-tuple-element.321), channel_id=1, source_target_pairs={{0,3},{1,2},{2,1},{3,0},{4,7},{5,6},{6,5},{7,4},{8,11},{9,10},{10,... | collective-permute-start | bytes 393224 | tf_op jit(solution)/shard_map/ppermute | solution.py:136
  306.4 4.1 %collective-permute-done.30 = bf16[1,64,1024]{2,1,0:T(8,128)(2,1)S(1)} collective-permute-done((bf16[1,64,1024]{2,1,0:T(8,128)(2,1)}, bf16[1,64,1024]{2,1,0:T(8,128)(2,1)S(1)}, u32[]{:S(2)}, u32[]{:S(2)}) %collective-permute-start.30) | collective-permute-done | bytes 131104 | tf_op jit(solution)/shard_map/ppermute | solution.py:136
  310.5 5.3 %collective-permute-start.28 = (bf16[1,64,1024]{2,1,0:T(8,128)(2,1)S(1)}, bf16[1,64,1024]{2,1,0:T(8,128)(2,1)S(1)}, u32[]{:S(2)}, u32[]{:S(2)}) collective-permute-start(bf16[1,64,1024]{2,1,0:T(8,128)(2,1)S(1)} %get-tuple-element.323), channel_id=1, source_target_pairs={{0,1},{1,0},{2,3},{3,2},{4,5},{5,4},{6,7},{7,6},{8,9},{9,8},{10,11... | collective-permute-start | bytes 393224 | tf_op jit(solution)/shard_map/ppermute | solution.py:136
  317.7 2.7 collective-permute-done.28
  324.0 2.1 collective-permute-start.36
  328.4 5.0 %collective-permute-done.35 = bf16[104,512]{1,0:T(8,128)(2,1)S(1)} collective-permute-done((bf16[104,512]{1,0:T(8,128)(2,1)S(1)}, bf16[104,512]{1,0:T(8,128)(2,1)S(1)}, u32[]{:S(2)}, u32[]{:S(2)}) %collective-permute-start.35) | collective-permute-done | bytes 106528 | tf_op jit(solution)/shard_map/ppermute | solution.py:136
  (255 shorter events, 65.1 us)
Async XLA Ops:
  7.2 73.8 %all-gather.7.cloned.1.call-start = ((), (), s32[]{:S(2)}) async-start(), calls=%async_computation.5 | async-start | bytes 4718592 | tf_op jit(solution)/shard_map/all_gather | solution.py:173
  11.1 11.4 %collective-permute-start.1 = (bf16[66,512]{1,0:T(8,128)(2,1)S(1)}, bf16[66,512]{1,0:T(8,128)(2,1)S(1)}, u32[]{:S(2)}, u32[]{:S(2)}) collective-permute-start(bf16[66,512]{1,0:T(8,128)(2,1)S(1)} %get-tuple-element.339), channel_id=1, source_target_pairs={{0,2},{1,3},{2,0},{3,1},{4,6},{5,7},{6,4},{7,5},{8,10},{9,11},{10,... | collective-permute-start | bytes 202760 | tf_op jit(solution)/shard_map/ppermute | solution.py:136
  23.0 12.3 %collective-permute-start.5 = (bf16[64,1024]{1,0:T(8,128)(2,1)S(1)}, bf16[64,1024]{1,0:T(8,128)(2,1)S(1)}, u32[]{:S(2)}, u32[]{:S(2)}) collective-permute-start(bf16[64,1024]{1,0:T(8,128)(2,1)S(1)} %pad_maximum_fusion.16), channel_id=1, source_target_pairs={{0,3},{1,2},{2,1},{3,0},{4,7},{5,6},{6,5},{7,4},{8,11},{9,10},{10,... | collective-permute-start | bytes 393224 | tf_op jit(solution)/shard_map/ppermute | solution.py:136
  26.5 10.6 %collective-permute-start.4 = (bf16[64,1024]{1,0:T(8,128)(2,1)S(1)}, bf16[64,1024]{1,0:T(8,128)(2,1)S(1)}, u32[]{:S(2)}, u32[]{:S(2)}) collective-permute-start(bf16[64,1024]{1,0:T(8,128)(2,1)S(1)} %pad_maximum_fusion.16), channel_id=1, source_target_pairs={{0,2},{1,3},{2,0},{3,1},{4,6},{5,7},{6,4},{7,5},{8,10},{9,11},{10,... | collective-permute-start | bytes 393224 | tf_op jit(solution)/shard_map/ppermute | solution.py:136
  26.5 10.6 %collective-permute-start.3 = (bf16[64,1024]{1,0:T(8,128)(2,1)S(1)}, bf16[64,1024]{1,0:T(8,128)(2,1)S(1)}, u32[]{:S(2)}, u32[]{:S(2)}) collective-permute-start(bf16[64,1024]{1,0:T(8,128)(2,1)S(1)} %pad_maximum_fusion.16), channel_id=1, source_target_pairs={{0,1},{1,0},{2,3},{3,2},{4,5},{5,4},{6,7},{7,6},{8,9},{9,8},{10,11... | collective-permute-start | bytes 393224 | tf_op jit(solution)/shard_map/ppermute | solution.py:136
  27.4 10.7 %collective-permute-start.8 = (bf16[4,64,512]{2,1,0:T(8,128)(2,1)S(1)}, bf16[4,64,512]{2,1,0:T(8,128)(2,1)}, u32[]{:S(2)}, u32[]{:S(2)}) collective-permute-start(bf16[4,64,512]{2,1,0:T(8,128)(2,1)S(1)} %slice.331), channel_id=1, source_target_pairs={{0,24},{1,25},{2,26},{3,27},{4,28},{5,29},{6,30},{7,31},{8,16},{9,... | collective-permute-start | bytes 786440 | tf_op jit(solution)/shard_map/ppermute | solution.py:136
  29.9 10.5 %collective-permute-start.7 = (bf16[4,64,512]{2,1,0:T(8,128)(2,1)S(1)}, bf16[4,64,512]{2,1,0:T(8,128)(2,1)}, u32[]{:S(2)}, u32[]{:S(2)}) collective-permute-start(bf16[4,64,512]{2,1,0:T(8,128)(2,1)S(1)} %slice.331), channel_id=1, source_target_pairs={{0,16},{1,17},{2,18},{3,19},{4,20},{5,21},{6,22},{7,23},{8,24},{9,... | collective-permute-start | bytes 786440 | tf_op jit(solution)/shard_map/ppermute | solution.py:136
  44.0 85.0 %all-gather.5.cloned.1.call-start = ((), (), s32[]{:S(2)}) async-start(), calls=%async_computation.4 | async-start | bytes 7077888 | tf_op jit(solution)/shard_map/all_gather | solution.py:173
  46.5 26.6 %collective-permute-start.11 = (bf16[64,1536]{1,0:T(8,128)(2,1)S(1)}, bf16[64,1536]{1,0:T(8,128)(2,1)S(1)}, u32[]{:S(2)}, u32[]{:S(2)}) collective-permute-start(bf16[64,1536]{1,0:T(8,128)(2,1)S(1)} %pad_maximum_fusion.11), channel_id=1, source_target_pairs={{0,3},{1,2},{2,1},{3,0},{4,7},{5,6},{6,5},{7,4},{8,11},{9,10},{10,... | collective-permute-start | bytes 589832 | tf_op jit(solution)/shard_map/ppermute | solution.py:136
  50.0 23.1 %collective-permute-start.10 = (bf16[64,1536]{1,0:T(8,128)(2,1)S(1)}, bf16[64,1536]{1,0:T(8,128)(2,1)S(1)}, u32[]{:S(2)}, u32[]{:S(2)}) collective-permute-start(bf16[64,1536]{1,0:T(8,128)(2,1)S(1)} %pad_maximum_fusion.11), channel_id=1, source_target_pairs={{0,2},{1,3},{2,0},{3,1},{4,6},{5,7},{6,4},{7,5},{8,10},{9,11},{10,... | collective-permute-start | bytes 589832 | tf_op jit(solution)/shard_map/ppermute | solution.py:136
  50.0 23.1 %collective-permute-start.9 = (bf16[64,1536]{1,0:T(8,128)(2,1)S(1)}, bf16[64,1536]{1,0:T(8,128)(2,1)S(1)}, u32[]{:S(2)}, u32[]{:S(2)}) collective-permute-start(bf16[64,1536]{1,0:T(8,128)(2,1)S(1)} %pad_maximum_fusion.11), channel_id=1, source_target_pairs={{0,1},{1,0},{2,3},{3,2},{4,5},{5,4},{6,7},{7,6},{8,9},{9,8},{10,11... | collective-permute-start | bytes 589832 | tf_op jit(solution)/shard_map/ppermute | solution.py:136
  74.2 165.5 %reduce-scatter.3.cloned.1.call-start = ((), (), s32[]{:S(2)}) async-start(), calls=%async_computation.2 | async-start | bytes 4718592 | tf_op jit(solution)/shard_map/reduce_scatter | solution.py:179
  94.6 21.6 %collective-permute-start.14 = (bf16[768,512]{1,0:T(8,128)(2,1)S(1)}, bf16[768,512]{1,0:T(8,128)(2,1)S(1)}, u32[]{:S(2)}, u32[]{:S(2)}) collective-permute-start(bf16[768,512]{1,0:T(8,128)(2,1)S(1)} %get-tuple-element.136.refs_2_), channel_id=1, source_target_pairs={{1,0},{2,1},{3,2},{5,4},{6,5},{7,6},{9,8},{10,9},{11,10},{13,12},{... | collective-permute-start | bytes 2359304 | tf_op jit(solution)/shard_map/ppermute | solution.py:209
  95.9 21.5 %collective-permute-start.13 = (bf16[768,512]{1,0:T(8,128)(2,1)S(1)}, bf16[768,512]{1,0:T(8,128)(2,1)S(1)}, u32[]{:S(2)}, u32[]{:S(2)}) collective-permute-start(bf16[768,512]{1,0:T(8,128)(2,1)S(1)} %get-tuple-element.136.refs_2_), channel_id=1, source_target_pairs={{0,1},{1,2},{2,3},{4,5},{5,6},{6,7},{8,9},{9,10},{10,11},{12,13},{... | collective-permute-start | bytes 2359304 | tf_op jit(solution)/shard_map/ppermute | solution.py:204
  172.6 127.5 %reduce-scatter.5.cloned.1.call-start = ((), (), s32[]{:S(2)}) async-start(), calls=%async_computation.3 | async-start | bytes 4718592 | tf_op jit(solution)/shard_map/reduce_scatter | solution.py:179
  188.8 26.6 %collective-permute-start.15 = (bf16[768,512]{1,0:T(8,128)(2,1)S(1)}, bf16[768,512]{1,0:T(8,128)(2,1)S(1)}, u32[]{:S(2)}, u32[]{:S(2)}) collective-permute-start(bf16[768,512]{1,0:T(8,128)(2,1)S(1)} %get-tuple-element.148), channel_id=1, source_target_pairs={{0,1},{1,2},{2,3},{4,5},{5,6},{6,7},{8,9},{9,10},{10,11},{12,13},{... | collective-permute-start | bytes 2359304 | tf_op jit(solution)/shard_map/ppermute | solution.py:204
  194.0 21.4 %collective-permute-start.16 = (bf16[768,512]{1,0:T(8,128)(2,1)S(1)}, bf16[768,512]{1,0:T(8,128)(2,1)S(1)}, u32[]{:S(2)}, u32[]{:S(2)}) collective-permute-start(bf16[768,512]{1,0:T(8,128)(2,1)S(1)} %get-tuple-element.149), channel_id=1, source_target_pairs={{1,0},{2,1},{3,2},{5,4},{6,5},{7,6},{9,8},{10,9},{11,10},{13,12},{... | collective-permute-start | bytes 2359304 | tf_op jit(solution)/shard_map/ppermute | solution.py:209
  218.5 19.7 %collective-permute-start.20 = (bf16[4,64,512]{2,1,0:T(8,128)(2,1)S(1)}, bf16[4,64,512]{2,1,0:T(8,128)(2,1)}, u32[]{:S(2)}, u32[]{:S(2)}) collective-permute-start(bf16[4,64,512]{2,1,0:T(8,128)(2,1)S(1)} %get-tuple-element.315), channel_id=1, source_target_pairs={{0,24},{1,25},{2,26},{3,27},{4,28},{5,29},{6,30},{7,31},{8,16},{9,... | collective-permute-start | bytes 786440 | tf_op jit(solution)/shard_map/ppermute | solution.py:136
  220.5 17.7 %collective-permute-start.19 = (bf16[4,64,512]{2,1,0:T(8,128)(2,1)S(1)}, bf16[4,64,512]{2,1,0:T(8,128)(2,1)}, u32[]{:S(2)}, u32[]{:S(2)}) collective-permute-start(bf16[4,64,512]{2,1,0:T(8,128)(2,1)S(1)} %get-tuple-element.316), channel_id=1, source_target_pairs={{0,16},{1,17},{2,18},{3,19},{4,20},{5,21},{6,22},{7,23},{8,24},{9,... | collective-permute-start | bytes 786440 | tf_op jit(solution)/shard_map/ppermute | solution.py:136
  221.7 16.5 %collective-permute-start.18 = (bf16[4,64,512]{2,1,0:T(8,128)(2,1)S(1)}, bf16[4,64,512]{2,1,0:T(8,128)(2,1)}, u32[]{:S(2)}, u32[]{:S(2)}) collective-permute-start(bf16[4,64,512]{2,1,0:T(8,128)(2,1)S(1)} %get-tuple-element.317), channel_id=1, source_target_pairs={{0,8},{1,9},{2,10},{3,11},{4,12},{5,13},{6,14},{7,15},{8,0},{9,1},... | collective-permute-start | bytes 786440 | tf_op jit(solution)/shard_map/ppermute | solution.py:136
  240.8 21.8 %collective-permute-start.23 = (bf16[1,64,1536]{2,1,0:T(8,128)(2,1)S(1)}, bf16[1,64,1536]{2,1,0:T(8,128)(2,1)S(1)}, u32[]{:S(2)}, u32[]{:S(2)}) collective-permute-start(bf16[1,64,1536]{2,1,0:T(8,128)(2,1)S(1)} %get-tuple-element.318), channel_id=1, source_target_pairs={{0,3},{1,2},{2,1},{3,0},{4,7},{5,6},{6,5},{7,4},{8,11},{9,10},{10,... | collective-permute-start | bytes 589832 | tf_op jit(solution)/shard_map/ppermute | solution.py:136
  244.1 18.4 %collective-permute-start.21 = (bf16[1,64,1536]{2,1,0:T(8,128)(2,1)S(1)}, bf16[1,64,1536]{2,1,0:T(8,128)(2,1)S(1)}, u32[]{:S(2)}, u32[]{:S(2)}) collective-permute-start(bf16[1,64,1536]{2,1,0:T(8,128)(2,1)S(1)} %get-tuple-element.319), channel_id=1, source_target_pairs={{0,1},{1,0},{2,3},{3,2},{4,5},{5,4},{6,7},{7,6},{8,9},{9,8},{10,11... | collective-permute-start | bytes 589832 | tf_op jit(solution)/shard_map/ppermute | solution.py:136
  244.9 17.7 %collective-permute-start.22 = (bf16[1,64,1536]{2,1,0:T(8,128)(2,1)S(1)}, bf16[1,64,1536]{2,1,0:T(8,128)(2,1)S(1)}, u32[]{:S(2)}, u32[]{:S(2)}) collective-permute-start(bf16[1,64,1536]{2,1,0:T(8,128)(2,1)S(1)} %get-tuple-element.320), channel_id=1, source_target_pairs={{0,2},{1,3},{2,0},{3,1},{4,6},{5,7},{6,4},{7,5},{8,10},{9,11},{10,... | collective-permute-start | bytes 589832 | tf_op jit(solution)/shard_map/ppermute | solution.py:136
  262.6 26.7 %collective-permute-start.24 = (bf16[768,512]{1,0:T(8,128)(2,1)S(1)}, bf16[768,512]{1,0:T(8,128)(2,1)S(1)}, u32[]{:S(2)}, u32[]{:S(2)}) collective-permute-start(bf16[768,512]{1,0:T(8,128)(2,1)S(1)} %get-tuple-element.183), channel_id=1, source_target_pairs={{0,1},{1,2},{2,3},{4,5},{5,6},{6,7},{8,9},{9,10},{10,11},{12,13},{... | collective-permute-start | bytes 2359304 | tf_op jit(solution)/shard_map/ppermute | solution.py:204
  266.3 23.0 %collective-permute-start.25 = (bf16[768,512]{1,0:T(8,128)(2,1)S(1)}, bf16[768,512]{1,0:T(8,128)(2,1)S(1)}, u32[]{:S(2)}, u32[]{:S(2)}) collective-permute-start(bf16[768,512]{1,0:T(8,128)(2,1)S(1)} %get-tuple-element.184), channel_id=1, source_target_pairs={{1,0},{2,1},{3,2},{5,4},{6,5},{7,6},{9,8},{10,9},{11,10},{13,12},{... | collective-permute-start | bytes 2359304 | tf_op jit(solution)/shard_map/ppermute | solution.py:209
  296.6 23.7 %collective-permute-start.33 = (bf16[296,512]{1,0:T(8,128)(2,1)}, bf16[296,512]{1,0:T(8,128)(2,1)S(1)}, u32[]{:S(2)}, u32[]{:S(2)}) collective-permute-start(bf16[296,512]{1,0:T(8,128)(2,1)} %get-tuple-element.343), channel_id=1, source_target_pairs={{0,24},{1,25},{2,26},{3,27},{4,28},{5,29},{6,30},{7,31},{8,16},{9,... | collective-permute-start | bytes 909320 | tf_op jit(solution)/shard_map/ppermute | solution.py:136
  298.0 22.4 %collective-permute-start.31 = (bf16[296,512]{1,0:T(8,128)(2,1)}, bf16[296,512]{1,0:T(8,128)(2,1)S(1)}, u32[]{:S(2)}, u32[]{:S(2)}) collective-permute-start(bf16[296,512]{1,0:T(8,128)(2,1)} %get-tuple-element.344), channel_id=1, source_target_pairs={{0,8},{1,9},{2,10},{3,11},{4,12},{5,13},{6,14},{7,15},{8,0},{9,1},... | collective-permute-start | bytes 909320 | tf_op jit(solution)/shard_map/ppermute | solution.py:136
  299.2 21.1 %collective-permute-start.32 = (bf16[296,512]{1,0:T(8,128)(2,1)}, bf16[296,512]{1,0:T(8,128)(2,1)S(1)}, u32[]{:S(2)}, u32[]{:S(2)}) collective-permute-start(bf16[296,512]{1,0:T(8,128)(2,1)} %get-tuple-element.345), channel_id=1, source_target_pairs={{0,16},{1,17},{2,18},{3,19},{4,20},{5,21},{6,22},{7,23},{8,24},{9,... | collective-permute-start | bytes 909320 | tf_op jit(solution)/shard_map/ppermute | solution.py:136
  306.3 11.3 %collective-permute-start.29 = (bf16[1,64,1024]{2,1,0:T(8,128)(2,1)}, bf16[1,64,1024]{2,1,0:T(8,128)(2,1)S(1)}, u32[]{:S(2)}, u32[]{:S(2)}) collective-permute-start(bf16[1,64,1024]{2,1,0:T(8,128)(2,1)} %get-tuple-element.322), channel_id=1, source_target_pairs={{0,2},{1,3},{2,0},{3,1},{4,6},{5,7},{6,4},{7,5},{8,10},{9,11},{10,... | collective-permute-start | bytes 393224 | tf_op jit(solution)/shard_map/ppermute | solution.py:136
  310.5 9.9 %collective-permute-start.28 = (bf16[1,64,1024]{2,1,0:T(8,128)(2,1)S(1)}, bf16[1,64,1024]{2,1,0:T(8,128)(2,1)S(1)}, u32[]{:S(2)}, u32[]{:S(2)}) collective-permute-start(bf16[1,64,1024]{2,1,0:T(8,128)(2,1)S(1)} %get-tuple-element.323), channel_id=1, source_target_pairs={{0,1},{1,0},{2,3},{3,2},{4,5},{5,4},{6,7},{7,6},{8,9},{9,8},{10,11... | collective-permute-start | bytes 393224 | tf_op jit(solution)/shard_map/ppermute | solution.py:136
  322.2 11.2 %collective-permute-start.35 = (bf16[104,512]{1,0:T(8,128)(2,1)S(1)}, bf16[104,512]{1,0:T(8,128)(2,1)S(1)}, u32[]{:S(2)}, u32[]{:S(2)}) collective-permute-start(bf16[104,512]{1,0:T(8,128)(2,1)S(1)} %get-tuple-element.341), channel_id=1, source_target_pairs={{0,2},{1,3},{2,0},{3,1},{4,6},{5,7},{6,4},{7,5},{8,10},{9,11},{10,... | collective-permute-start | bytes 319496 | tf_op jit(solution)/shard_map/ppermute | solution.py:136
  324.0 9.4 %collective-permute-start.36 = (bf16[104,512]{1,0:T(8,128)(2,1)S(1)}, bf16[104,512]{1,0:T(8,128)(2,1)S(1)}, u32[]{:S(2)}, u32[]{:S(2)}) collective-permute-start(bf16[104,512]{1,0:T(8,128)(2,1)S(1)} %get-tuple-element.342), channel_id=1, source_target_pairs={{0,3},{1,2},{2,1},{3,0},{4,7},{5,6},{6,5},{7,4},{8,11},{9,10},{10,... | collective-permute-start | bytes 319496 | tf_op jit(solution)/shard_map/ppermute | solution.py:136
  (60 other events, 659.5 us)
Sparse Core Ops, SparseCore 0:
  44.2 36.8 all-gather.6
  83.5 45.5 all-gather.4
  172.7 58.6 reduce-scatter.2
  238.3 51.4 reduce-scatter.4
